TPU v7x, 32 devices: a whole 2x2x4 slice. The times are simulated.
32 devices in a mesh: bank: 4 (over y, x), seg: 8 (over z, core).
Axes of the slice: x: 2, y: 2, z: 4, core: 2. Of those that a mesh axis runs over, the one named last changes fastest.
Arguments:
- strain: bfloat16 [64, 2, 2, 65536], P(('bank', 'seg')), may hold values from -6 to 6
- templates: bfloat16 [4, 2, 65536], P('bank', None, 'seg'), may hold values from -0.0234375 to 0.0234375
- bin_edges: int32 [4, 15], replicated, may hold values from 1 to 255, as said below
- live_flags: int32 [64], P(('bank', 'seg')), may hold values from 0 to 1, as said below
Outputs:
- peak_snr: float32 [4, 64], P(None, ('bank', 'seg'))
- coarse_snr: float32 [4, 64, 256], P(None, ('bank', 'seg'))
- chi_series: float32 [4, 64, 256], P(None, ('bank', 'seg'))
Inputs may be any that keep to these rules, and one draw needn't show every extreme that they name: `bin_edges`: each row rises strictly. `live_flags`: on each device the live slots (1) come first; two devices whose indices along seg differ only in the lowest bit hold exactly 2 live slots together; some device holds 2 live slots.
All inputs are finite; a program needn't handle non-finite values.
Results may differ from a plain program's by a relative error of at most 0.0025.
Values may be sent and summed in bfloat16 or wider, within the bound.
No kernel may reach another device: no remote copies, remote signals or barrier semaphores. Data moves between devices by JAX's collectives and lax.ppermute only.
A program may use at most 64 MiB of HBM per device.

v0:
```python
import math

import jax
import jax.numpy as jnp
from jax import lax
from jax.sharding import PartitionSpec as P

FREQ = 65536
FA = 256
FB = 256
BINS = 16


def passed_along(block, axis, distance):
    devices = range(lax.axis_size(axis))
    route = [((i - distance) % len(devices), i) for i in devices]
    return lax.ppermute(block, axis, route)


def complex_table(rows, cols, length, dtype):
    left = jnp.arange(rows, dtype=jnp.int32)[:, None]
    right = jnp.arange(cols, dtype=jnp.int32)[None, :]
    angle = (left * right % length).astype(jnp.float32) * (2.0 * math.pi / length)
    cosine = jnp.cos(angle).astype(dtype)
    sine = jnp.sin(angle).astype(dtype)
    upper = jnp.stack([cosine, sine], axis=1)
    lower = jnp.stack([-sine, cosine], axis=1)
    return jnp.stack([upper, lower], axis=0)


def twiddles():
    left = jnp.arange(FA, dtype=jnp.int32)[:, None]
    right = jnp.arange(FB, dtype=jnp.int32)[None, :]
    angle = (left * right % FREQ).astype(jnp.float32) * (2.0 * math.pi / FREQ)
    return (jnp.cos(angle), jnp.sin(angle))


def bin_table(edges):
    blocks = jnp.arange(FB, dtype=jnp.int32)
    labels = jnp.sum((edges[:, :, None] <= blocks[None, None, :]).astype(jnp.int32), axis=1)
    return (labels[:, None, :] == jnp.arange(BINS, dtype=jnp.int32)[None, :, None]).astype(
        jnp.bfloat16
    )


def accumulate(spectra, piece, onehot):
    width = piece.shape[-1]
    rows = width // FA
    sre = spectra[:, :, 0].astype(jnp.float32)[None]
    sim = spectra[:, :, 1].astype(jnp.float32)[None]
    hre = piece[:, 0].astype(jnp.float32)
    him = piece[:, 1].astype(jnp.float32)
    hre_b = hre[:, None, None, :]
    him_b = him[:, None, None, :]
    real_part = sre * hre_b + sim * him_b
    imag_part = sim * hre_b - sre * him_b
    product = jnp.stack([real_part, imag_part], axis=3).astype(jnp.bfloat16)
    product = product.reshape(product.shape[:4] + (rows, FA))
    binsum = jnp.einsum("tbf,tsdcfa->tsdcba", onehot, product, preferred_element_type=jnp.float32)
    rowpower = jnp.sum((hre * hre + him * him).reshape(hre.shape[0], rows, FA), axis=-1)
    return (product, binsum, rowpower)


def finish(carry, onehot, wbig, wa_table, wc_table, tw_cos, tw_sin):
    prodbuf, binsum, hsq = carry
    first = jnp.einsum("tsdcfa,cfox->tsdaox", prodbuf, wbig, preferred_element_type=jnp.float32)
    are = first[..., 0, :]
    aim = first[..., 1, :]
    bre = are * tw_cos - aim * tw_sin
    bim = are * tw_sin + aim * tw_cos
    turned = jnp.stack([bre, bim], axis=-2).astype(jnp.bfloat16)
    series = jnp.einsum("tsdacx,caou->tsdoux", turned, wa_table, preferred_element_type=jnp.float32)
    hpower = jnp.einsum(
        "tbf,tf->tb", onehot.astype(jnp.float32), hsq, precision=lax.Precision.HIGHEST
    )
    sigma = jnp.sum(hpower, axis=-1)
    power = jnp.sum(series * series, axis=(2, 3))
    peak = jnp.sqrt(jnp.max(power, axis=(2, 3)) / sigma[:, None])
    part = jnp.einsum("tsdcba,caok->tsdobk", binsum, wc_table, precision=lax.Precision.HIGHEST)
    whole = jnp.sum(part, axis=4)
    share = hpower / sigma[:, None]
    diff = part - share[:, None, None, None, :, None] * whole[:, :, :, :, None, :]
    chi = jnp.sum(diff * diff, axis=(2, 3, 4)) / sigma[:, None, None] / (4.0 * (BINS - 1))
    coarse = jnp.sum(whole * whole, axis=(2, 3)) / sigma[:, None, None]
    return (peak, coarse, chi)


def on_device(strain, templates, bin_edges, live_flags):
    wbig = complex_table(FB, FB, FB, jnp.bfloat16)
    wa_table = complex_table(FA, FA, FA, jnp.bfloat16)
    wc_table = complex_table(FA, FB, FB, jnp.float32)
    tw_cos, tw_sin = twiddles()
    nbank = lax.axis_size("bank")
    bank_index = lax.axis_index("bank")
    tile_count = templates.shape[0]
    total = tile_count * nbank
    held = strain.shape[0]

    def tile_results(tile, owner):
        edges = lax.dynamic_slice_in_dim(bin_edges, owner * tile_count, tile_count, 0)
        onehot = bin_table(edges)
        carry = accumulate(strain, lax.all_gather(tile, "seg", axis=2, tiled=True), onehot)
        return finish(carry, onehot, wbig, wa_table, wc_table, tw_cos, tw_sin)

    def place(results, outputs, owner):
        row = owner * tile_count
        return tuple(
            (
                lax.dynamic_update_slice_in_dim(full, new, row, 0)
                for full, new in zip(outputs, results)
            )
        )

    outputs = (
        jnp.zeros((total, held), jnp.float32),
        jnp.zeros((total, held, FB), jnp.float32),
        jnp.zeros((total, held, FB), jnp.float32),
    )
    tile = templates

    def step(turn, state):
        current, gathered = state
        owner = (bank_index - turn) % nbank
        gathered = place(tile_results(current, owner), gathered, owner)
        current = passed_along(current, "bank", 1)
        return (current, gathered)

    tile, outputs = lax.fori_loop(0, nbank - 1, step, (tile, outputs))
    owner = (bank_index - (nbank - 1)) % nbank
    peak, coarse, chi = place(tile_results(tile, owner), outputs, owner)
    weight = live_flags.astype(jnp.float32)
    return (peak * weight[None, :], coarse * weight[None, :, None], chi * weight[None, :, None])


def solution(mesh):
    in_specs = (
        P(("bank", "seg"), None, None, None),
        P("bank", None, "seg"),
        P(),
        P(("bank", "seg")),
    )
    out_specs = (
        P(None, ("bank", "seg")),
        P(None, ("bank", "seg"), None),
        P(None, ("bank", "seg"), None),
    )
    return jax.shard_map(
        on_device, mesh=mesh, in_specs=in_specs, out_specs=out_specs, check_vma=False
    )
```

profile of v0, /device:TPU:1, one launch (start us, length us, event | category | flops | bytes accessed | tf_op | source)
XLA Modules:
  0.0 150.4 jit_solution(15986313041743085885)
XLA Ops:
  0.6 1.4 copy.161
  3.4 1.1 fusion.66
  8.6 1.2 fusion.77
  10.0 2.1 %copy.80 = bf16[2,2,2,65536]{3,1,0,2:T(2,128)(2,1)} copy(bf16[2,2,2,65536]{3,2,1,0:T(2,128)(2,1)S(1)} %copy-done.3) | data formatting | bytes 2097152
  12.8 102.3 %while.23 = (s32[]{:T(128)}, bf16[1,2,8192]{2,1,0:T(2,128)(2,1)}, f32[4,2]{1,0:T(4,128)}, f32[4,2,256]{2,1,0:T(2,128)S(1)}, f32[4,2,256]{2,1,0:T(2,128)S(1)}, /*...) while((s32[]{:T(128)}, bf16[1,2,8192]{2,1,0:T(2,128)(2,1)}, ...), condition=%wide.region_9.10_spmd.clone.clone, body=%wide.region_0.9_spmd.clone.clone.sunk | while | flops 1302435072 | bytes 33568704 | solution.py:128
  12.8 1.4 copy.146
  14.1 2.0 %collective-permute-start = (bf16[1,2,8192]{2,1,0:T(2,128)(2,1)}, bf16[1,2,8192]{2,1,0:T(2,128)(2,1)}, u32[]{:S(2)}, u32[]{:S(2)}) collective-permute-start(bf16[1,2,8192]{2,1,0:T(2,128)(2,1)} %copy.146), channel_id=1, source_target_pairs={{24,0},{0,8},{8,16},{16,24},{25,1},{1,9},{9,17},{17,25},{26,2},{2,... | collective-permute-start | bytes 98312 | tf_op jit(solution)/shard_map/while/body/eval_jaxpr/ppermute | solution.py:17
  16.2 15.6 %all_gather.16 = bf16[1,2,65536]{2,1,0:T(2,128)(2,1)S(1)} all-gather(bf16[1,2,8192]{2,1,0:T(2,128)(2,1)} %copy.146), channel_id=1, replica_groups=mesh['bank'=4,'seg'=8] {'seg'}, dimensions={2}, use_global_device_ids=true | all-gather | bytes 294912 | tf_op jit(solution)/shard_map/while/body/eval_jaxpr/all_gather | solution.py:102
  33.1 1.0 fusion.110
  34.1 1.4 fusion.109
  36.7 1.7 %convolution_bitcast_fusion.10 = f32[1,2,2,256,2,256]{5,3,4,2,1,0:T(8,128)S(1)} fusion(bf16[2,2,1,256,256]{3,4,2,1,0:T(8,128)(2,1)S(1)} %copy.135, bf16[2,2,1,256,256]{3,4,2,1,0:T(8,128)(2,1)S(1)} %copy.136, bf16[2,256,2,256]{3,1,0,2:T(8,128)(2,1)} %get-tuple-element.614), kind=kOutput, calls=%fused_computation.4.clone.1 | convolution fusion | flops 538968064 | bytes 3670016 | tf_op jit(solution)/shard_map/while/body/eval_jaxpr/tsdcfa,cfox->tsdaox/dot_general | solution.py:66
  41.7 1.4 fusion.116
  46.6 1.3 dynamic_update_slice.52
  47.9 1.4 copy.146
  49.3 1.2 collective-permute-start
  50.5 14.8 %all_gather.16 = bf16[1,2,65536]{2,1,0:T(2,128)(2,1)S(1)} all-gather(bf16[1,2,8192]{2,1,0:T(2,128)(2,1)} %copy.146), channel_id=1, replica_groups=mesh['bank'=4,'seg'=8] {'seg'}, dimensions={2}, use_global_device_ids=true | all-gather | bytes 294912 | tf_op jit(solution)/shard_map/while/body/eval_jaxpr/all_gather | solution.py:102
  66.6 1.0 fusion.110
  67.7 1.4 fusion.109
  70.3 1.7 %convolution_bitcast_fusion.10 = f32[1,2,2,256,2,256]{5,3,4,2,1,0:T(8,128)S(1)} fusion(bf16[2,2,1,256,256]{3,4,2,1,0:T(8,128)(2,1)S(1)} %copy.135, bf16[2,2,1,256,256]{3,4,2,1,0:T(8,128)(2,1)S(1)} %copy.136, bf16[2,256,2,256]{3,1,0,2:T(8,128)(2,1)} %get-tuple-element.614), kind=kOutput, calls=%fused_computation.4.clone.1 | convolution fusion | flops 538968064 | bytes 3670016 | tf_op jit(solution)/shard_map/while/body/eval_jaxpr/tsdcfa,cfox->tsdaox/dot_general | solution.py:66
  75.3 1.4 fusion.116
  80.2 1.3 dynamic_update_slice.52
  81.5 1.4 copy.146
  82.9 1.2 collective-permute-start
  84.1 14.8 %all_gather.16 = bf16[1,2,65536]{2,1,0:T(2,128)(2,1)S(1)} all-gather(bf16[1,2,8192]{2,1,0:T(2,128)(2,1)} %copy.146), channel_id=1, replica_groups=mesh['bank'=4,'seg'=8] {'seg'}, dimensions={2}, use_global_device_ids=true | all-gather | bytes 294912 | tf_op jit(solution)/shard_map/while/body/eval_jaxpr/all_gather | solution.py:102
  100.2 1.0 fusion.110
  101.3 1.4 fusion.109
  103.9 1.7 %convolution_bitcast_fusion.10 = f32[1,2,2,256,2,256]{5,3,4,2,1,0:T(8,128)S(1)} fusion(bf16[2,2,1,256,256]{3,4,2,1,0:T(8,128)(2,1)S(1)} %copy.135, bf16[2,2,1,256,256]{3,4,2,1,0:T(8,128)(2,1)S(1)} %copy.136, bf16[2,256,2,256]{3,1,0,2:T(8,128)(2,1)} %get-tuple-element.614), kind=kOutput, calls=%fused_computation.4.clone.1 | convolution fusion | flops 538968064 | bytes 3670016 | tf_op jit(solution)/shard_map/while/body/eval_jaxpr/tsdcfa,cfox->tsdaox/dot_general | solution.py:66
  108.9 1.4 fusion.116
  113.7 1.3 dynamic_update_slice.52
  115.0 14.6 %all_gather.12 = bf16[1,2,65536]{2,1,0:T(2,128)(2,1)S(1)} all-gather(bf16[1,2,8192]{2,1,0:T(2,128)(2,1)} %get-tuple-element.340), channel_id=1, replica_groups=mesh['bank'=4,'seg'=8] {'seg'}, dimensions={2}, use_global_device_ids=true | all-gather | bytes 294912 | tf_op jit(solution)/shard_map/all_gather | solution.py:102
  130.1 8.3 %convert_reduce_fusion.1 = (bf16[2,2,65536]{2,1,0:T(2,128)(2,1)S(1)}, bf16[2,2,65536]{2,1,0:T(2,128)(2,1)S(1)}) fusion(bf16[2,2,2,65536]{3,2,1,0:T(2,128)(2,1)S(1)} %copy-done.4, f32[65536]{0:T(1024)S(1)} %bitcast.267, f32[65536]{0:T(1024)S(1)} %bitcast.266), kind=kLoop, calls=%fused_computation.83 | loop fusion | flops 2621440 | bytes 2621440 | tf_op jit(solution)/shard_map/convert.19
  146.4 1.0 fusion.61
  (150 shorter events, 45.1 us)
Async XLA Ops:
  5.5 2.0 %copy-start.6 = (bf16[1,256,2,256]{3,1,0,2:T(8,128)(2,1)}, bf16[1,256,2,256]{3,1,0,2:T(8,128)(2,1)S(1)}, u32[]{:S(2)}) copy-start(bf16[1,256,2,256]{3,1,0,2:T(8,128)(2,1)S(1)} %get-tuple-element.477) | copy-start | bytes 786436
  5.5 2.0 %copy-start.8 = (bf16[1,256,2,256]{3,1,0,2:T(8,128)(2,1)}, bf16[1,256,2,256]{3,1,0,2:T(8,128)(2,1)S(1)}, u32[]{:S(2)}) copy-start(bf16[1,256,2,256]{3,1,0,2:T(8,128)(2,1)S(1)} %get-tuple-element.478) | copy-start | bytes 786436
  8.6 1.5 copy-start.3
  14.1 33.8 %collective-permute-start = (bf16[1,2,8192]{2,1,0:T(2,128)(2,1)}, bf16[1,2,8192]{2,1,0:T(2,128)(2,1)}, u32[]{:S(2)}, u32[]{:S(2)}) collective-permute-start(bf16[1,2,8192]{2,1,0:T(2,128)(2,1)} %copy.146), channel_id=1, source_target_pairs={{24,0},{0,8},{8,16},{16,24},{25,1},{1,9},{9,17},{17,25},{26,2},{2,... | collective-permute-start | bytes 98312 | tf_op jit(solution)/shard_map/while/body/eval_jaxpr/ppermute | solution.py:17
  16.2 17.9 %copy-start = (bf16[2,2,2,65536]{3,1,0,2:T(2,128)(2,1)S(1)}, bf16[2,2,2,65536]{3,1,0,2:T(2,128)(2,1)}, u32[]{:S(2)}) copy-start(bf16[2,2,2,65536]{3,1,0,2:T(2,128)(2,1)} %get-tuple-element.613) | copy-start | bytes 3145732 | tf_op jit(solution)/shard_map/while
  39.7 4.8 %copy-start.1 = (bf16[2,256,2,256]{3,1,0,2:T(8,128)(2,1)S(1)}, bf16[2,256,2,256]{3,1,0,2:T(8,128)(2,1)}, u32[]{:S(2)}) copy-start(bf16[2,256,2,256]{3,1,0,2:T(8,128)(2,1)} %get-tuple-element.614) | copy-start | bytes 1572868 | tf_op jit(solution)/shard_map/while
  40.6 0.6 copy-start.13
  41.5 3.1 %copy-start.2 = (bf16[2,2,256,1,256]{4,2,1,0,3:T(8,128)(2,1)S(1)}, bf16[2,2,256,1,256]{4,2,1,0,3:T(8,128)(2,1)}, u32[]{:S(2)}) copy-start(bf16[2,2,256,1,256]{4,2,1,0,3:T(8,128)(2,1)} %fusion.111) | copy-start | bytes 1572868 | tf_op jit(solution)/shard_map/while
  49.3 32.2 %collective-permute-start = (bf16[1,2,8192]{2,1,0:T(2,128)(2,1)}, bf16[1,2,8192]{2,1,0:T(2,128)(2,1)}, u32[]{:S(2)}, u32[]{:S(2)}) collective-permute-start(bf16[1,2,8192]{2,1,0:T(2,128)(2,1)} %copy.146), channel_id=1, source_target_pairs={{24,0},{0,8},{8,16},{16,24},{25,1},{1,9},{9,17},{17,25},{26,2},{2,... | collective-permute-start | bytes 98312 | tf_op jit(solution)/shard_map/while/body/eval_jaxpr/ppermute | solution.py:17
  50.5 17.2 %copy-start = (bf16[2,2,2,65536]{3,1,0,2:T(2,128)(2,1)S(1)}, bf16[2,2,2,65536]{3,1,0,2:T(2,128)(2,1)}, u32[]{:S(2)}) copy-start(bf16[2,2,2,65536]{3,1,0,2:T(2,128)(2,1)} %get-tuple-element.613) | copy-start | bytes 3145732 | tf_op jit(solution)/shard_map/while
  73.3 4.8 %copy-start.1 = (bf16[2,256,2,256]{3,1,0,2:T(8,128)(2,1)S(1)}, bf16[2,256,2,256]{3,1,0,2:T(8,128)(2,1)}, u32[]{:S(2)}) copy-start(bf16[2,256,2,256]{3,1,0,2:T(8,128)(2,1)} %get-tuple-element.614) | copy-start | bytes 1572868 | tf_op jit(solution)/shard_map/while
  74.2 0.6 copy-start.13
  75.1 3.1 %copy-start.2 = (bf16[2,2,256,1,256]{4,2,1,0,3:T(8,128)(2,1)S(1)}, bf16[2,2,256,1,256]{4,2,1,0,3:T(8,128)(2,1)}, u32[]{:S(2)}) copy-start(bf16[2,2,256,1,256]{4,2,1,0,3:T(8,128)(2,1)} %fusion.111) | copy-start | bytes 1572868 | tf_op jit(solution)/shard_map/while
  82.9 32.2 %collective-permute-start = (bf16[1,2,8192]{2,1,0:T(2,128)(2,1)}, bf16[1,2,8192]{2,1,0:T(2,128)(2,1)}, u32[]{:S(2)}, u32[]{:S(2)}) collective-permute-start(bf16[1,2,8192]{2,1,0:T(2,128)(2,1)} %copy.146), channel_id=1, source_target_pairs={{24,0},{0,8},{8,16},{16,24},{25,1},{1,9},{9,17},{17,25},{26,2},{2,... | collective-permute-start | bytes 98312 | tf_op jit(solution)/shard_map/while/body/eval_jaxpr/ppermute | solution.py:17
  84.1 17.2 %copy-start = (bf16[2,2,2,65536]{3,1,0,2:T(2,128)(2,1)S(1)}, bf16[2,2,2,65536]{3,1,0,2:T(2,128)(2,1)}, u32[]{:S(2)}) copy-start(bf16[2,2,2,65536]{3,1,0,2:T(2,128)(2,1)} %get-tuple-element.613) | copy-start | bytes 3145732 | tf_op jit(solution)/shard_map/while
  106.9 4.8 %copy-start.1 = (bf16[2,256,2,256]{3,1,0,2:T(8,128)(2,1)S(1)}, bf16[2,256,2,256]{3,1,0,2:T(8,128)(2,1)}, u32[]{:S(2)}) copy-start(bf16[2,256,2,256]{3,1,0,2:T(8,128)(2,1)} %get-tuple-element.614) | copy-start | bytes 1572868 | tf_op jit(solution)/shard_map/while
  107.7 0.6 copy-start.13
  108.7 3.1 %copy-start.2 = (bf16[2,2,256,1,256]{4,2,1,0,3:T(8,128)(2,1)S(1)}, bf16[2,2,256,1,256]{4,2,1,0,3:T(8,128)(2,1)}, u32[]{:S(2)}) copy-start(bf16[2,2,256,1,256]{4,2,1,0,3:T(8,128)(2,1)} %fusion.111) | copy-start | bytes 1572868 | tf_op jit(solution)/shard_map/while
  115.0 15.0 %copy-start.4 = (bf16[2,2,2,65536]{3,2,1,0:T(2,128)(2,1)S(1)}, bf16[2,2,2,65536]{3,2,1,0:T(2,128)(2,1)}, u32[]{:S(2)}) copy-start(bf16[2,2,2,65536]{3,2,1,0:T(2,128)(2,1)} %param.6) | copy-start | bytes 3145732
  138.3 1.2 copy-start.12
  138.9 1.2 copy-start.5
  139.5 5.4 %copy-start.11 = (s32[2]{0:T(128)S(1)}, s32[2]{0:T(128)}, u32[]{:S(2)}) copy-start(s32[2]{0:T(128)} %param.9) | copy-start | bytes 28
  139.6 6.1 %copy-start.7 = (bf16[1,256,2,256]{3,1,0,2:T(8,128)(2,1)S(1)}, bf16[1,256,2,256]{3,1,0,2:T(8,128)(2,1)}, u32[]{:S(2)}) copy-start(bf16[1,256,2,256]{3,1,0,2:T(8,128)(2,1)} %copy-done.6) | copy-start | bytes 786436
  139.6 6.1 %copy-start.9 = (bf16[1,256,2,256]{3,1,0,2:T(8,128)(2,1)S(1)}, bf16[1,256,2,256]{3,1,0,2:T(8,128)(2,1)}, u32[]{:S(2)}) copy-start(bf16[1,256,2,256]{3,1,0,2:T(8,128)(2,1)} %copy-done.8) | copy-start | bytes 786436
  147.9 1.7 %copy-start.10 = (f32[4,2]{1,0:T(4,128)S(1)}, f32[4,2]{1,0:T(4,128)}, u32[]{:S(2)}) copy-start(f32[4,2]{1,0:T(4,128)} %get-tuple-element.339) | copy-start | bytes 100
where the time goes:
time: 151 us; the launch traced here: 150 us
  blocking collectives  59.8 us (40%)
  other arithmetic  44 us (29%)
  local copies, waits for them, and re-layouts  22.5 us (15%)
  matrix products  18.4 us (12%)
  starting transfers between devices  4.46 us (3%)
    all_gather x4, blocking collectives, tile_results(): lax.all_gather(tile, 'seg', axis=2, tiled=True)  59.8 us
    another operation x4, other arithmetic  12.5 us
    dot_general x4, matrix products, finish(): jnp.einsum('tsdcfa,cfox->tsdaox', prodbuf, wbig, preferred_element_type=j...  5.95 us
    while x27, local copies, waits for them, and re-layouts  5.87 us
    dot_general x4, matrix products, finish(): jnp.einsum('tbf,tf->tb', onehot.astype(jnp.float32), hsq, precision=lax.P...  4.88 us
    another operation x16, local copies, waits for them, and re-layouts, accumulate(): product = jnp.stack([real_part, imag_part], axis=3).astype(jnp.bfloat16)  4.65 us
    ppermute x3, starting transfers between devices, passed_along(): return lax.ppermute(block, axis, route)  4.46 us
    another operation x8, other arithmetic, finish(): turned = jnp.stack([bre, bim], axis=-2).astype(jnp.bfloat16)  4.25 us
  transfers between devices with their start and end apart: 3, of which 0 were waited for; matrix products, arithmetic and copies ran while one was open for 31% of the time, Pallas kernels for 0%

commit v1 on v0

v1 whole, which is shorter than its diff:
```python
import functools
import math

import jax
import jax.numpy as jnp
import numpy as np
from jax import lax
from jax.experimental import pallas as pl
from jax.experimental.pallas import tpu as pltpu
from jax.sharding import PartitionSpec as P

FA = 256
FB = 256
HALF = 128
BINS = 16
BF16 = jnp.bfloat16
F32 = jnp.float32


def waves(rows, cols, length):
    turns = np.outer(rows, cols) % length
    angle = turns * (2.0 * math.pi / length)
    return np.cos(angle), np.sin(angle)


def tables():
    bf = np.dtype(BF16)
    every = np.arange(FA)
    cosine, sine = waves(every, every, FA)
    first = np.block([[cosine, -sine], [sine, cosine]]).astype(bf)
    half = np.arange(HALF)
    even_c, even_s = waves(half, 2 * half, FA)
    odd_c, odd_s = waves(half, 2 * half + 1, FA)
    second = np.stack(
        [
            np.block([[even_c, even_s], [-even_s, even_c]]),
            np.block([[odd_c, odd_s], [-odd_s, odd_c]]),
        ]
    ).astype(bf)
    coarse = np.block([[cosine, sine], [-sine, cosine]]).astype(np.float32)
    upper = coarse.astype(bf)
    lower = (coarse - upper.astype(np.float32)).astype(bf)
    turn = np.stack(waves(every, every, FA * FB)).astype(np.float32)
    return first, second, np.stack([upper, lower]), turn


def dot(left, right):
    return jnp.dot(left, right, preferred_element_type=F32)


def split(value):
    upper = value.astype(BF16)
    return upper, (value - upper.astype(F32)).astype(BF16)


def flip_orders(nbank, nseg):
    seg = [(0, 1 << k) for k in range(1, nseg.bit_length() - 1)]
    bank = [(1 << k, 0) for k in range(nbank.bit_length() - 1)]
    return (seg[::-1] + bank, seg + bank[::-1]), len(seg)


def reach(order, place):
    bank = seg = 0
    for k, (b, s) in enumerate(order):
        if place >> k & 1:
            bank, seg = bank ^ b, seg ^ s
    return bank, seg


def filter_body(
    nbank, nseg, held, tiles, live_ref, edges_ref, strain_ref, mine0, mine1, theirs0, theirs1,
    first_ref, second_ref, coarse_ref, turn_ref, peak_ref, snr_ref, chi_ref,
    left, spectrum, product, turned, sums, hpow,
):
    orders, seg_steps = flip_orders(nbank, nseg)
    my_bank = lax.axis_index("bank")
    my_seg = lax.axis_index("seg")
    core = my_seg & 1
    rows = FB // nseg
    total = nbank * tiles
    low = 1 << seg_steps
    places = 1 << len(orders[0])
    swapped = {reach(orders[1], p): p for p in range(places)}

    left[0 : 2 * FB] = first_ref[...]
    peak_ref[...] = jnp.zeros(peak_ref.shape, F32)
    snr_ref[...] = jnp.zeros(snr_ref.shape, F32)
    chi_ref[...] = jnp.zeros(chi_ref.shape, F32)
    blocks = lax.broadcasted_iota(jnp.int32, (BINS, FB), 1)
    bins = lax.broadcasted_iota(jnp.int32, (BINS, FB), 0)

    def piece(refs, place, k):
        ref, at = (refs[0], place) if place < places // 2 else (refs[1], place - places // 2)
        return ref[at * tiles + k]

    for q in range(nbank):
        bank0 = reach(orders[0], q * low)[0]
        bank1 = reach(orders[1], q * low)[0]
        bank = my_bank ^ jnp.where(core == 0, bank0, bank1)
        partner_q = swapped[(bank0, 0)] // low
        for k in range(tiles):
            t = bank * tiles + k
            for z in range(low):
                seg0, seg1 = reach(orders[0], z)[1], reach(orders[1], z)[1]
                own = my_seg ^ jnp.where(core == 0, seg0, seg1)
                other = my_seg ^ 1 ^ jnp.where(core == 0, seg1, seg0)
                for refs, place, seg in (
                    ((mine0, mine1), q * low + z, own),
                    ((theirs0, theirs1), partner_q * low + z, other),
                ):
                    data = piece(refs, place, k).astype(F32)
                    start = pl.multiple_of(seg * rows, rows)
                    spectrum[:, pl.ds(start, rows), :] = data

            label = jnp.zeros((BINS, FB), jnp.int32)
            for j in range(BINS - 1):
                label = label + (edges_ref[t, j] <= blocks).astype(jnp.int32)
            onehot = (label == bins).astype(F32).astype(BF16)
            nothing = jnp.zeros((BINS, FB), BF16)
            left[2 * FB : 2 * FB + BINS, 0:FB] = onehot
            left[2 * FB : 2 * FB + BINS, FB:] = nothing
            left[2 * FB + BINS :, 0:FB] = nothing
            left[2 * FB + BINS :, FB:] = onehot

            energy = spectrum[0] * spectrum[0] + spectrum[1] * spectrum[1]
            energy = energy[:, :HALF] + energy[:, HALF:]
            upper, lower = split(energy)
            power = dot(onehot, upper) + dot(onehot, lower)
            hpower = jnp.sum(power, axis=1, keepdims=True)
            sigma = jnp.sum(hpower, axis=0, keepdims=True)
            share = hpower / sigma

            for s in range(held):

                @pl.when(live_ref[s] != 0)
                def _():
                    hre, him = spectrum[0], spectrum[1]
                    for d in range(2):
                        sre = strain_ref[s, d, 0].astype(F32)
                        sim = strain_ref[s, d, 1].astype(F32)
                        cols = slice(d * FA, (d + 1) * FA)
                        product[0:FB, cols] = (sre * hre + sim * him).astype(BF16)
                        product[FB:, cols] = (sim * hre - sre * him).astype(BF16)
                    for d in range(2):
                        cols = slice(d * FA, (d + 1) * FA)
                        one = dot(left[...], product[:, cols])
                        are, aim = one[0:FB], one[FB : 2 * FB]
                        bre = are * turn_ref[0] - aim * turn_ref[1]
                        bim = are * turn_ref[1] + aim * turn_ref[0]
                        lines = slice(d * FB, (d + 1) * FB)
                        turned[0, lines, 0:HALF] = (bre[:, :HALF] + bre[:, HALF:]).astype(BF16)
                        turned[0, lines, HALF:] = (bim[:, :HALF] + bim[:, HALF:]).astype(BF16)
                        turned[1, lines, 0:HALF] = (bre[:, :HALF] - bre[:, HALF:]).astype(BF16)
                        turned[1, lines, HALF:] = (bim[:, :HALF] - bim[:, HALF:]).astype(BF16)
                        here = slice(d * BINS, (d + 1) * BINS)
                        sums[here, 0:FA] = one[2 * FB : 2 * FB + BINS]
                        sums[here, FA:] = one[2 * FB + BINS :]
                    best = jnp.zeros((FB, HALF), F32)
                    for parity in range(2):
                        series = dot(turned[parity], second_ref[parity])
                        series = series * series
                        series = series[:FB] + series[FB:]
                        best = jnp.maximum(best, series[:, :HALF] + series[:, HALF:])
                    upper, lower = split(sums[...])
                    part = (
                        dot(upper, coarse_ref[0])
                        + dot(lower, coarse_ref[0])
                        + dot(upper, coarse_ref[1])
                    )
                    snr = jnp.zeros((1, FB), F32)
                    chi = jnp.zeros((1, FB), F32)
                    for d in range(2):
                        own = part[d * BINS : (d + 1) * BINS]
                        whole = jnp.sum(own, axis=0, keepdims=True)
                        diff = own - share * whole
                        diff = jnp.sum(diff * diff, axis=0, keepdims=True)
                        whole = whole * whole
                        snr = snr + whole[:, :FB] + whole[:, FB:]
                        chi = chi + diff[:, :FB] + diff[:, FB:]
                    snr_ref[t, s : s + 1] = snr / sigma
                    chi_ref[t, s : s + 1] = chi / sigma / (4.0 * (BINS - 1))
                    peak = jnp.max(jnp.max(best, axis=0, keepdims=True), axis=1, keepdims=True)
                    peak = jnp.sqrt(peak / sigma)
                    at = (lax.broadcasted_iota(jnp.int32, peak_ref.shape, 0) == t) & (
                        lax.broadcasted_iota(jnp.int32, peak_ref.shape, 1) == s
                    )
                    peak_ref[...] = jnp.where(at, peak, peak_ref[...])


def on_device(nbank, nseg, strain, templates, bin_edges, live_flags):
    held = strain.shape[0]
    tiles = templates.shape[0]
    total = tiles * nbank
    rows = FB // nseg
    first, second, coarse, turn = (jnp.asarray(x) for x in tables())
    orders, _ = flip_orders(nbank, nseg)

    def swap(block, step):
        route = []
        for b in range(nbank):
            for s in range(nseg):
                flip_bank, flip_seg = (0, 1) if step is None else orders[s & 1][step]
                route.append((b * nseg + s, (b ^ flip_bank) * nseg + (s ^ flip_seg)))
        return lax.ppermute(block, ("bank", "seg"), route)

    block = templates.reshape(tiles, 2, rows, FA)
    steps = len(orders[0])
    for step in range(steps - 1):
        block = jnp.concatenate([block, swap(block, step)], axis=0)
    late = swap(block, steps - 1)
    other = swap(block, None)
    other_late = swap(late, None)
    whole = strain.reshape(held, 2, 2, FB, FA)

    body = functools.partial(filter_body, nbank, nseg, held, tiles)
    smem = pl.BlockSpec(memory_space=pltpu.SMEM)
    vmem = pl.BlockSpec(memory_space=pltpu.VMEM)
    return pl.pallas_call(
        body,
        in_specs=[smem, smem] + [vmem] * 9,
        out_specs=[vmem] * 3,
        out_shape=[
            jax.ShapeDtypeStruct((total, held), F32),
            jax.ShapeDtypeStruct((total, held, FB), F32),
            jax.ShapeDtypeStruct((total, held, FB), F32),
        ],
        scratch_shapes=[
            pltpu.VMEM((2 * FB + 2 * BINS, 2 * FB), BF16),
            pltpu.VMEM((2, FB, FA), F32),
            pltpu.VMEM((2 * FB, 2 * FA), BF16),
            pltpu.VMEM((2, 2 * FB, FA), BF16),
            pltpu.VMEM((2 * BINS, 2 * FA), F32),
            pltpu.VMEM((BINS, HALF), F32),
        ],
        compiler_params=pltpu.CompilerParams(vmem_limit_bytes=40 << 20),
    )(live_flags, bin_edges, whole, block, late, other, other_late, first, second, coarse, turn)


def solution(mesh):
    in_specs = (
        P(("bank", "seg"), None, None, None),
        P("bank", None, "seg"),
        P(),
        P(("bank", "seg")),
    )
    out_specs = (
        P(None, ("bank", "seg")),
        P(None, ("bank", "seg"), None),
        P(None, ("bank", "seg"), None),
    )
    body = functools.partial(on_device, mesh.shape["bank"], mesh.shape["seg"])
    return jax.shard_map(body, mesh=mesh, in_specs=in_specs, out_specs=out_specs, check_vma=False)
```

time: 151 us -> 40.5 us (0.27)
  the two profiles are of different devices: /device:TPU:1 before, /device:TPU:21 now
where the time goes in v1:
time: 40.5 us; the launch traced here: 40.2 us
  starting transfers between devices  12.6 us (31%)
  Pallas kernels  12.2 us (30%)
  waiting for transfers between devices  9.75 us (24%)
  local copies, waits for them, and re-layouts  4.85 us (12%)
  between operations  0.75 us (2%)
    ppermute x6, starting transfers between devices, swap(): return lax.ppermute(block, ('bank', 'seg'), route)  12.6 us
    pallas_call x1, Pallas kernels, on_device(): pl.pallas_call(body, in_specs=[smem, smem] + [vmem] * 9, out_specs=[vmem]...  12.2 us
    ppermute x6, waiting for transfers between devices, swap(): return lax.ppermute(block, ('bank', 'seg'), route)  9.75 us
    reshape x1, local copies, waits for them, and re-layouts, on_device(): whole = strain.reshape(held, 2, 2, FB, FA)  2.45 us
    unnamed x14, local copies, waits for them, and re-layouts  0.98 us
  transfers between devices with their start and end apart: 6, of which 4 were waited for; matrix products, arithmetic and copies ran while one was open for 6% of the time, Pallas kernels for 0%

profile of v1, /device:TPU:21, one launch (start us, length us, event | category | flops | bytes accessed | tf_op | source)
XLA Modules:
  0.0 40.2 jit_solution(8206777818186113537)
XLA Ops:
  0.6 0.8 %copy_bitcast_fusion = (bf16[1,2,32,256]{3,2,1,0:T(8,128)(2,1)S(1)}, bf16[8,2,32,256]{3,2,1,0:T(8,128)(2,1)S(1)}) fusion(bf16[1,2,32,256]{3,1,2,0:T(2,128)(2,1)} %bitcast.7), kind=kLoop, calls=%fused_computation.2 | loop fusion | bytes 98304 | tf_op jit(solution)/shard_map/reshape | solution.py:206
  1.4 1.3 %collective-permute-start = (bf16[1,2,32,256]{3,2,1,0:T(8,128)(2,1)S(1)}, bf16[1,2,32,256]{3,2,1,0:T(8,128)(2,1)S(1)}, u32[]{:S(2)}, u32[]{:S(2)}) collective-permute-start(bf16[1,2,32,256]{3,2,1,0:T(8,128)(2,1)S(1)} %get-tuple-element.6), channel_id=1, source_target_pairs={{0,4},{1,3},{2,6},{3,1},{4,0},{5,7},{6,2},{7,5},{8,12},{9,11},{10,... | collective-permute-start | bytes 98312 | tf_op jit(solution)/shard_map/ppermute | solution.py:204
  2.7 1.5 %collective-permute-done = bf16[1,2,32,256]{3,2,1,0:T(8,128)(2,1)S(1)} collective-permute-done((bf16[1,2,32,256]{3,2,1,0:T(8,128)(2,1)S(1)}, bf16[1,2,32,256]{3,2,1,0:T(8,128)(2,1)S(1)}, u32[]{:S(2)}, u32[]{:S(2)}) %collective-permute-start) | collective-permute-done | bytes 32800 | tf_op jit(solution)/shard_map/ppermute | solution.py:204
  4.2 0.1 collective-permute-start.1
  4.3 4.0 %collective-permute-done.1 = bf16[2,2,32,256]{3,2,1,0:T(8,128)(2,1)S(1)} collective-permute-done((bf16[2,2,32,256]{3,2,1,0:T(8,128)(2,1)S(1)}, bf16[2,2,32,256]{3,2,1,0:T(8,128)(2,1)S(1)}, u32[]{:S(2)}, u32[]{:S(2)}) %collective-permute-start.1) | collective-permute-done | bytes 65568 | tf_op jit(solution)/shard_map/ppermute | solution.py:204
  8.3 0.3 collective-permute-start.2
  8.6 3.6 %collective-permute-done.2 = bf16[4,2,32,256]{3,2,1,0:T(8,128)(2,1)S(1)} collective-permute-done((bf16[4,2,32,256]{3,2,1,0:T(8,128)(2,1)S(1)}, bf16[4,2,32,256]{3,2,1,0:T(8,128)(2,1)S(1)}, u32[]{:S(2)}, u32[]{:S(2)}) %collective-permute-start.2) | collective-permute-done | bytes 131104 | tf_op jit(solution)/shard_map/ppermute | solution.py:204
  12.2 0.0 copy-start.4
  12.2 0.0 copy-start.5
  12.2 0.0 copy-start
  12.2 0.0 copy-start.1
  12.3 0.0 copy-start.2
  12.3 1.3 %collective-permute-start.3 = (bf16[8,2,32,256]{3,2,1,0:T(8,128)(2,1)S(1)}, bf16[8,2,32,256]{3,2,1,0:T(8,128)(2,1)}, u32[]{:S(2)}, u32[]{:S(2)}) collective-permute-start(bf16[8,2,32,256]{3,2,1,0:T(8,128)(2,1)S(1)} %constant_dynamic-update-slice_fusion.mine0), channel_id=1, source_target_pairs={{0,16},{1,9},{2,18},{3,11},{4,20},{5,13},{6,22},{7,15},{8,24},{9,1... | collective-permute-start | bytes 786440 | tf_op jit(solution)/shard_map/ppermute | solution.py:204
  13.5 4.3 %collective-permute-start.4 = (bf16[8,2,32,256]{3,2,1,0:T(8,128)(2,1)S(1)}, bf16[8,2,32,256]{3,2,1,0:T(8,128)(2,1)}, u32[]{:S(2)}, u32[]{:S(2)}) collective-permute-start(bf16[8,2,32,256]{3,2,1,0:T(8,128)(2,1)S(1)} %constant_dynamic-update-slice_fusion.mine0), channel_id=1, source_target_pairs={{0,1},{1,0},{2,3},{3,2},{4,5},{5,4},{6,7},{7,6},{8,9},{9,8},{10,11... | collective-permute-start | bytes 786440 | tf_op jit(solution)/shard_map/ppermute | solution.py:204
  17.9 0.7 %collective-permute-done.3.mine1 = bf16[8,2,32,256]{3,2,1,0:T(8,128)(2,1)} collective-permute-done((bf16[8,2,32,256]{3,2,1,0:T(8,128)(2,1)S(1)}, bf16[8,2,32,256]{3,2,1,0:T(8,128)(2,1)}, u32[]{:S(2)}, u32[]{:S(2)}) %collective-permute-start.3) | collective-permute-done | bytes 262176 | tf_op jit(solution)/shard_map/ppermute | solution.py:204
  18.5 5.3 %collective-permute-start.5 = (bf16[8,2,32,256]{3,2,1,0:T(8,128)(2,1)}, bf16[8,2,32,256]{3,2,1,0:T(8,128)(2,1)}, u32[]{:S(2)}, u32[]{:S(2)}) collective-permute-start(bf16[8,2,32,256]{3,2,1,0:T(8,128)(2,1)} %collective-permute-done.3.mine1), channel_id=1, source_target_pairs={{0,1},{1,0},{2,3},{3,2},{4,5},{5,4},{6,7},{7,6},{8,9},{9,8},{10,11... | collective-permute-start | bytes 786440 | tf_op jit(solution)/shard_map/ppermute | solution.py:204
  23.8 2.4 %reshape.12.strain_ref = bf16[2,2,2,256,256]{4,3,2,1,0:T(8,128)(2,1)S(1)} reshape(bf16[2,2,2,65536]{3,2,1,0:T(2,128)(2,1)} %param.8) | data formatting | bytes 2097152 | tf_op jit(solution)/shard_map/reshape | solution.py:213
  26.3 0.0 collective-permute-done.4.theirs0
  26.3 0.0 collective-permute-done.5.theirs1
  26.3 0.0 copy-done.4
  26.3 0.0 copy-done.5
  26.3 0.0 copy-done
  26.3 0.0 copy-done.1
  26.3 0.0 copy-done.2
  26.3 0.0 copy-start.3
  26.4 0.9 %copy-done.3 = bf16[2,256,256]{2,1,0:T(8,128)(2,1)S(1)} copy-done((bf16[2,256,256]{2,1,0:T(8,128)(2,1)S(1)}, bf16[2,256,256]{2,1,0:T(8,128)(2,1)}, u32[]{:S(2)}) %copy-start.3) | copy-done | bytes 262168
  27.3 12.2 %shard_map.103 = (f32[4,2]{1,0:T(4,128)S(1)}, f32[4,2,256]{2,1,0:T(2,128)}, f32[4,2,256]{2,1,0:T(2,128)}) custom-call(s32[2]{0:T(128)S(1)} %copy-done.5, s32[4,15]{1,0:T(4,128)S(1)} %copy-done.4, bf16[2,2,2,256,256]{4,3,2,1,0:T(8,128)(2,1)S(1)} %reshape.12.strain_ref, bf16[8,2,32,256]{3,2,1,0:T(8,128)(2,1)S(1)} %constant_dynamic-update-slice_fusion.mine0, ...), custom_call_target="tpu_custom_call" | custom-call | tf_op jit(solution)/shard_map/pallas_call | solution.py:218
  39.6 0.6 %copy.11 = f32[4,2]{0,1:T(2,128)} copy(f32[4,2]{1,0:T(4,128)S(1)} %get-tuple-element.3) | data formatting | bytes 64 | tf_op jit(solution)/shard_map/pallas_call | solution.py:218
  (5 shorter events, 0.0 us)
Async XLA Ops:
  1.4 2.8 %collective-permute-start = (bf16[1,2,32,256]{3,2,1,0:T(8,128)(2,1)S(1)}, bf16[1,2,32,256]{3,2,1,0:T(8,128)(2,1)S(1)}, u32[]{:S(2)}, u32[]{:S(2)}) collective-permute-start(bf16[1,2,32,256]{3,2,1,0:T(8,128)(2,1)S(1)} %get-tuple-element.6), channel_id=1, source_target_pairs={{0,4},{1,3},{2,6},{3,1},{4,0},{5,7},{6,2},{7,5},{8,12},{9,11},{10,... | collective-permute-start | bytes 98312 | tf_op jit(solution)/shard_map/ppermute | solution.py:204
  4.2 4.1 %collective-permute-start.1 = (bf16[2,2,32,256]{3,2,1,0:T(8,128)(2,1)S(1)}, bf16[2,2,32,256]{3,2,1,0:T(8,128)(2,1)S(1)}, u32[]{:S(2)}, u32[]{:S(2)}) collective-permute-start(bf16[2,2,32,256]{3,2,1,0:T(8,128)(2,1)S(1)} %pad_maximum_fusion.1), channel_id=1, source_target_pairs={{0,2},{1,5},{2,0},{3,7},{4,6},{5,1},{6,4},{7,3},{8,10},{9,13},{10,... | collective-permute-start | bytes 196616 | tf_op jit(solution)/shard_map/ppermute | solution.py:204
  8.3 3.9 %collective-permute-start.2 = (bf16[4,2,32,256]{3,2,1,0:T(8,128)(2,1)S(1)}, bf16[4,2,32,256]{3,2,1,0:T(8,128)(2,1)S(1)}, u32[]{:S(2)}, u32[]{:S(2)}) collective-permute-start(bf16[4,2,32,256]{3,2,1,0:T(8,128)(2,1)S(1)} %pad_maximum_fusion), channel_id=1, source_target_pairs={{0,8},{1,17},{2,10},{3,19},{4,12},{5,21},{6,14},{7,23},{8,0},{9,25... | collective-permute-start | bytes 393224 | tf_op jit(solution)/shard_map/ppermute | solution.py:204
  12.2 14.1 %copy-start.4 = (s32[4,15]{1,0:T(4,128)S(1)}, s32[4,15]{1,0:T(4,128)}, u32[]{:S(2)}) copy-start(s32[4,15]{1,0:T(4,128)} %edges_ref.1) | copy-start | bytes 724
  12.2 14.1 %copy-start.5 = (s32[2]{0:T(128)S(1)}, s32[2]{0:T(128)}, u32[]{:S(2)}) copy-start(s32[2]{0:T(128)} %live_ref.1) | copy-start | bytes 28
  12.2 14.1 %copy-start = (bf16[2,512,512]{2,1,0:T(8,128)(2,1)S(1)}, bf16[2,512,512]{2,1,0:T(8,128)(2,1)}, u32[]{:S(2)}) copy-start(bf16[2,512,512]{2,1,0:T(8,128)(2,1)} %constant.10.clone.coarse_ref) | copy-start | bytes 3145732
  12.2 14.1 %copy-start.1 = (f32[2,256,256]{2,1,0:T(8,128)S(1)}, f32[2,256,256]{2,1,0:T(8,128)}, u32[]{:S(2)}) copy-start(f32[2,256,256]{2,1,0:T(8,128)} %constant.11.clone.turn_ref) | copy-start | bytes 1572868
  12.3 14.1 %copy-start.2 = (bf16[512,512]{1,0:T(8,128)(2,1)S(1)}, bf16[512,512]{1,0:T(8,128)(2,1)}, u32[]{:S(2)}) copy-start(bf16[512,512]{1,0:T(8,128)(2,1)} %constant.8.clone.first_ref) | copy-start | bytes 1572868
  12.3 6.3 %collective-permute-start.3 = (bf16[8,2,32,256]{3,2,1,0:T(8,128)(2,1)S(1)}, bf16[8,2,32,256]{3,2,1,0:T(8,128)(2,1)}, u32[]{:S(2)}, u32[]{:S(2)}) collective-permute-start(bf16[8,2,32,256]{3,2,1,0:T(8,128)(2,1)S(1)} %constant_dynamic-update-slice_fusion.mine0), channel_id=1, source_target_pairs={{0,16},{1,9},{2,18},{3,11},{4,20},{5,13},{6,22},{7,15},{8,24},{9,1... | collective-permute-start | bytes 786440 | tf_op jit(solution)/shard_map/ppermute | solution.py:204
  13.5 12.7 %collective-permute-start.4 = (bf16[8,2,32,256]{3,2,1,0:T(8,128)(2,1)S(1)}, bf16[8,2,32,256]{3,2,1,0:T(8,128)(2,1)}, u32[]{:S(2)}, u32[]{:S(2)}) collective-permute-start(bf16[8,2,32,256]{3,2,1,0:T(8,128)(2,1)S(1)} %constant_dynamic-update-slice_fusion.mine0), channel_id=1, source_target_pairs={{0,1},{1,0},{2,3},{3,2},{4,5},{5,4},{6,7},{7,6},{8,9},{9,8},{10,11... | collective-permute-start | bytes 786440 | tf_op jit(solution)/shard_map/ppermute | solution.py:204
  18.5 7.8 %collective-permute-start.5 = (bf16[8,2,32,256]{3,2,1,0:T(8,128)(2,1)}, bf16[8,2,32,256]{3,2,1,0:T(8,128)(2,1)}, u32[]{:S(2)}, u32[]{:S(2)}) collective-permute-start(bf16[8,2,32,256]{3,2,1,0:T(8,128)(2,1)} %collective-permute-done.3.mine1), channel_id=1, source_target_pairs={{0,1},{1,0},{2,3},{3,2},{4,5},{5,4},{6,7},{7,6},{8,9},{9,8},{10,11... | collective-permute-start | bytes 786440 | tf_op jit(solution)/shard_map/ppermute | solution.py:204
  26.3 1.0 %copy-start.3 = (bf16[2,256,256]{2,1,0:T(8,128)(2,1)S(1)}, bf16[2,256,256]{2,1,0:T(8,128)(2,1)}, u32[]{:S(2)}) copy-start(bf16[2,256,256]{2,1,0:T(8,128)(2,1)} %constant.9.clone.second_ref) | copy-start | bytes 786436

commit v2 on v1

v2 whole, which is shorter than its diff:
```python
import functools
import math

import jax
import jax.numpy as jnp
import numpy as np
from jax import lax
from jax.experimental import pallas as pl
from jax.experimental.pallas import tpu as pltpu
from jax.sharding import PartitionSpec as P

FA = 256
FB = 256
HALF = 128
BINS = 16
STEP = 16
BF16 = jnp.bfloat16
F32 = jnp.float32


def waves(rows, cols, length):
    turns = np.outer(rows, cols) % length
    angle = turns * (2.0 * math.pi / length)
    return np.cos(angle), np.sin(angle)


def tables():
    bf = np.dtype(BF16)
    every = np.arange(FA)
    cosine, sine = waves(every, every, FA)
    first = np.block([[cosine, -sine], [sine, cosine]]).astype(bf)
    half = np.arange(HALF)
    even_c, even_s = waves(half, 2 * half, FA)
    odd_c, odd_s = waves(half, 2 * half + 1, FA)
    second = np.stack(
        [
            np.block([[even_c, even_s], [-even_s, even_c]]),
            np.block([[odd_c, odd_s], [-odd_s, odd_c]]),
        ]
    ).astype(bf)
    coarse = np.block([[cosine, sine], [-sine, cosine]]).astype(np.float32)
    upper = coarse.astype(bf)
    lower = (coarse - upper.astype(np.float32)).astype(bf)
    turn = np.stack(waves(every, every, FA * FB)).astype(np.float32)
    return first, second, np.stack([upper, lower]), turn


def dot(left, right):
    return jnp.dot(left, right, preferred_element_type=F32)


def split(value):
    upper = value.astype(BF16)
    return upper, (value - upper.astype(F32)).astype(BF16)


def flip_orders(nseg):
    flips = [1 << k for k in range(1, nseg.bit_length() - 1)]
    return flips[::-1], flips


def reach(order, place):
    seg = 0
    for k, flip in enumerate(order):
        if place >> k & 1:
            seg ^= flip
    return seg


def filter_body(
    nseg, held, flips, live_ref, edges_ref, halves, slots, first_ref, second_ref, turn_ref,
    sums, tops, powers, lefts, spectra, products, firsts, turneds, series,
):
    orders = flip_orders(nseg)
    my_bank = lax.axis_index("bank")
    my_seg = lax.axis_index("seg")
    core = my_seg & 1
    rows = FB // nseg
    low = nseg // 2
    tiles = powers.shape[0] // len(flips)
    blocks = lax.broadcasted_iota(jnp.int32, (BINS, FB), 1)
    bins = lax.broadcasted_iota(jnp.int32, (BINS, FB), 0)

    def stage(n):
        q, k = n // tiles, n % tiles
        left, spectrum = lefts[n % 2], spectra[n % 2]
        t = owner(my_bank, core, flips[q]) * tiles + k
        (mine, mine_at), (theirs, theirs_at) = halves[q]
        for z in range(low):
            even, odd = reach(orders[0], z), reach(orders[1], z)
            own = my_seg ^ jnp.where(core == 0, even, odd)
            other = my_seg ^ 1 ^ jnp.where(core == 0, odd, even)
            for ref, at, seg in ((mine, mine_at, own), (theirs, theirs_at, other)):
                start = pl.multiple_of(seg * rows, rows)
                spectrum[:, pl.ds(start, rows), :] = ref[(at + z) * tiles + k].astype(F32)
        label = jnp.zeros((BINS, FB), jnp.int32)
        for j in range(BINS - 1):
            label = label + (edges_ref[t, j] <= blocks).astype(jnp.int32)
        onehot = (label == bins).astype(F32).astype(BF16)
        nothing = jnp.zeros((BINS, FB), BF16)
        left[0 : 2 * FB] = first_ref[...]
        left[2 * FB : 2 * FB + BINS, 0:FB] = onehot
        left[2 * FB : 2 * FB + BINS, FB:] = nothing
        left[2 * FB + BINS :, 0:FB] = nothing
        left[2 * FB + BINS :, FB:] = onehot
        energy = spectrum[0] * spectrum[0] + spectrum[1] * spectrum[1]
        energy = energy[:, :HALF] + energy[:, HALF:]
        upper, lower = split(energy)
        powers[n] = dot(onehot, upper) + dot(onehot, lower)

    def multiply(u):
        n, s = u // held, u % held
        spectrum = spectra[n % 2]
        for r in range(0, FB, STEP):
            lines = slice(r, r + STEP)
            hre, him = spectrum[0, lines], spectrum[1, lines]
            for d in range(2):
                sre = slots[s][d, 0, lines].astype(F32)
                sim = slots[s][d, 1, lines].astype(F32)
                product = products[u % 2 * 2 + d]
                product[lines] = (sre * hre + sim * him).astype(BF16)
                product[FB + r : FB + r + STEP] = (sim * hre - sre * him).astype(BF16)

    def transform(u, d):
        at = u % 2 * 2 + d
        firsts[at][...] = dot(lefts[u // held % 2][...], products[at][...])

    def turn_round(u, d):
        first, turned = firsts[u % 2 * 2 + d], turneds[u % 2 * 2 + d]
        for r in range(0, FB, STEP):
            out = slice(r, r + STEP)
            are, aim = first[out], first[FB + r : FB + r + STEP]
            cos, sin = turn_ref[0, out], turn_ref[1, out]
            bre = are * cos - aim * sin
            bim = are * sin + aim * cos
            turned[0, out, 0:HALF] = (bre[:, :HALF] + bre[:, HALF:]).astype(BF16)
            turned[0, out, HALF:] = (bim[:, :HALF] + bim[:, HALF:]).astype(BF16)
            turned[1, out, 0:HALF] = (bre[:, :HALF] - bre[:, HALF:]).astype(BF16)
            turned[1, out, HALF:] = (bim[:, :HALF] - bim[:, HALF:]).astype(BF16)
        base = (u * 2 + d) * BINS
        sums[base : base + BINS, 0:FA] = first[2 * FB : 2 * FB + BINS]
        sums[base : base + BINS, FA:] = first[2 * FB + BINS :]

    def finish(u, d):
        at = u % 2 * 2 + d
        for parity in range(2):
            series[at][parity] = dot(turneds[at][parity], second_ref[parity])

    def highest(u):
        best = None
        ones, twos = series[u % 2 * 2], series[u % 2 * 2 + 1]
        for parity in range(2):
            for r in range(0, FB, STEP):
                one, two = ones[parity, r : r + STEP], twos[parity, r : r + STEP]
                both = one * one + two * two
                both = both[:, :HALF] + both[:, HALF:]
                best = both if best is None else jnp.maximum(best, both)
        tops[u] = best

    units = powers.shape[0] * held
    stage(0)
    multiply(0)
    transform(0, 0)
    transform(0, 1)
    for u in range(units):
        more = u + 1 < units
        if more:
            if (u + 1) % held == 0:
                stage((u + 1) // held)
            multiply(u + 1)
        turn_round(u, 0)
        if more:
            transform(u + 1, 0)
        finish(u, 0)
        turn_round(u, 1)
        if more:
            transform(u + 1, 1)
        if u > 0:
            highest(u - 1)
        finish(u, 1)
    highest(units - 1)


def owner(my_bank, core, flip):
    return my_bank ^ (flip[0] if flip[0] == flip[1] else jnp.where(core == 0, flip[0], flip[1]))


def statistics(
    held, flips, live_ref, coarse_ref, groups, peak_ref, snr_ref, chi_ref, gathered, parts
):
    my_bank = lax.axis_index("bank")
    core = lax.axis_index("seg") & 1
    tiles = peak_ref.shape[1] // len(flips)
    at = 0
    for sums, _, _ in groups:
        gathered[at : at + sums.shape[0]] = sums[...]
        at += sums.shape[0]
    upper, lower = split(gathered[...])
    parts[...] = dot(upper, coarse_ref[0]) + dot(lower, coarse_ref[0]) + dot(upper, coarse_ref[1])
    peaks = jnp.zeros(peak_ref.shape, F32)
    slot_at = lax.broadcasted_iota(jnp.int32, peak_ref.shape, 0)
    tile_at = lax.broadcasted_iota(jnp.int32, peak_ref.shape, 1)
    n = 0
    for _, tops, powers in groups:
        for k in range(powers.shape[0]):
            t = owner(my_bank, core, flips[n // tiles]) * tiles + n % tiles
            hpower = jnp.sum(powers[k], axis=1, keepdims=True)
            sigma = jnp.sum(hpower, axis=0, keepdims=True)
            share = hpower / sigma
            for s in range(held):
                live = live_ref[s] != 0
                base = (n * held + s) * 2 * BINS
                snr = jnp.zeros((1, FB), F32)
                chi = jnp.zeros((1, FB), F32)
                for d in range(2):
                    own = parts[base + d * BINS : base + (d + 1) * BINS]
                    whole = jnp.sum(own, axis=0, keepdims=True)
                    diff = own - share * whole
                    diff = jnp.sum(diff * diff, axis=0, keepdims=True)
                    whole = whole * whole
                    snr = snr + whole[:, :FB] + whole[:, FB:]
                    chi = chi + diff[:, :FB] + diff[:, FB:]
                snr_ref[t, s : s + 1] = jnp.where(live, snr / sigma, 0.0)
                chi = chi / sigma / (4.0 * (BINS - 1))
                chi_ref[t, s : s + 1] = jnp.where(live, chi, 0.0)
                top = jnp.max(tops[k * held + s], axis=0, keepdims=True)
                top = jnp.sqrt(jnp.max(top, axis=1, keepdims=True) / sigma)
                peaks = jnp.where((slot_at == s) & (tile_at == t) & live, top, peaks)
            n += 1
    peak_ref[...] = peaks


def on_device(nbank, nseg, strain, templates, bin_edges, live_flags):
    held = strain.shape[0]
    tiles = templates.shape[0]
    total = tiles * nbank
    rows = FB // nseg
    low = nseg // 2
    first, second, coarse, turn = (jnp.asarray(x) for x in tables())
    orders = flip_orders(nseg)
    smem = pl.BlockSpec(memory_space=pltpu.SMEM)
    vmem = pl.BlockSpec(memory_space=pltpu.VMEM)

    def swap(block, flips):
        route = []
        for b in range(nbank):
            for s in range(nseg):
                flip_bank, flip_seg = flips[s & 1]
                route.append((b * nseg + s, (b ^ flip_bank) * nseg + (s ^ flip_seg)))
        return lax.ppermute(block, ("bank", "seg"), route)

    twin = ((0, 1), (0, 1))

    def call(flips, arrays, halves, earlier=None):
        fresh = len(flips) * tiles
        made = [
            jax.ShapeDtypeStruct((fresh * held * 2 * BINS, 2 * FA), F32),
            jax.ShapeDtypeStruct((fresh * held, STEP, HALF), F32),
            jax.ShapeDtypeStruct((fresh, BINS, HALF), F32),
        ]
        scratch = [
            [pltpu.VMEM((2 * FB + 2 * BINS, 2 * FB), BF16) for _ in range(2)],
            [pltpu.VMEM((2, FB, FA), F32) for _ in range(2)],
            [pltpu.VMEM((2 * FB, FA), BF16) for _ in range(4)],
            [pltpu.VMEM((2 * FB + 2 * BINS, FA), F32) for _ in range(4)],
            [pltpu.VMEM((2, FB, FA), BF16) for _ in range(4)],
            [pltpu.VMEM((2, FB, FA), F32) for _ in range(4)],
        ]
        count = len(arrays)

        def run(live_ref, edges_ref, first_ref, second_ref, turn_ref, *rest):
            slots, rest = rest[:held], rest[held:]
            spectra, rest = rest[:count], rest[count:]
            pairs = [[(spectra[i], at) for i, at in half] for half in halves]
            if earlier is None:
                results, scratches = rest[:3], rest[3:]
            else:
                coarse_ref, rest = rest[0], rest[1:]
                groups = [rest[i : i + 3] for i in range(0, 3 * len(earlier[1]), 3)]
                rest = rest[3 * len(groups) :]
                outs, results, scratches = rest[:3], rest[3:6], rest[8:]
            filter_body(
                nseg, held, flips, live_ref, edges_ref, pairs, slots,
                first_ref, second_ref, turn_ref, *results, *scratches,
            )
            if earlier is not None:
                every = earlier[0] + flips
                groups = groups + [results]
                statistics(held, every, live_ref, coarse_ref, groups, *outs, *rest[6:8])

        inputs = [live_flags, bin_edges, first, second, turn, *slots, *arrays]
        if earlier is None:
            shapes = made
        else:
            inputs += [coarse] + [x for group in earlier[1] for x in group]
            shapes = [
                jax.ShapeDtypeStruct((held, total), F32),
                jax.ShapeDtypeStruct((total, held, FB), F32),
                jax.ShapeDtypeStruct((total, held, FB), F32),
            ]
            full = pltpu.VMEM((total * held * 2 * BINS, 2 * FA), F32)
            scratch = [pltpu.VMEM(x.shape, x.dtype) for x in made] + [full, full] + scratch
        return pl.pallas_call(
            run,
            in_specs=[smem, smem] + [vmem] * (len(inputs) - 2),
            out_specs=[vmem] * 3,
            out_shape=shapes,
            scratch_shapes=scratch,
            compiler_params=pltpu.CompilerParams(vmem_limit_bytes=24 << 20),
            cost_estimate=pl.CostEstimate(
                flops=1 * fresh * held * 2 * 12 * FA**3, bytes_accessed=1 << 20, transcendentals=0
            ),
        )(*inputs)

    block = templates.reshape(tiles, 2, rows, FA)
    slots = []
    for step in range(len(orders[0])):
        found = swap(block, [(0, orders[c][step]) for c in range(2)])
        if step < held:
            slot = strain[step].reshape(2, 2, FB, FA)
            found, slot = lax.optimization_barrier((found, slot))
            slots.append(slot)
        block = jnp.concatenate([block, found], axis=0)
    for s in range(len(slots), held):
        slots.append(strain[s].reshape(2, 2, FB, FA))
    other = swap(block, twin)
    corner = swap(block, ((3, 0), (3, 0)))
    side = swap(jnp.concatenate([block, other], axis=0), ((1, 0), (2, 0)))
    here = call([(0, 0)], [block, other], [((0, 0), (1, 0))])
    side, corner, here = lax.optimization_barrier((side, corner, here))
    far = swap(side, twin)
    other_corner = swap(corner, twin)
    beside = call([(1, 2)], [side], [((0, 0), (0, low))])
    far, other_corner, beside = lax.optimization_barrier((far, other_corner, beside))
    peak, snr, chi = call(
        [(2, 1), (3, 3)],
        [far, corner, other_corner],
        [((0, low), (0, 0)), ((1, 0), (2, 0))],
        ([(0, 0), (1, 2)], [here, beside]),
    )
    return peak.T, snr, chi


def solution(mesh):
    in_specs = (
        P(("bank", "seg"), None, None, None),
        P("bank", None, "seg"),
        P(),
        P(("bank", "seg")),
    )
    out_specs = (
        P(None, ("bank", "seg")),
        P(None, ("bank", "seg"), None),
        P(None, ("bank", "seg"), None),
    )
    body = functools.partial(on_device, mesh.shape["bank"], mesh.shape["seg"])
    return jax.shard_map(body, mesh=mesh, in_specs=in_specs, out_specs=out_specs, check_vma=False)
```

time: 40.5 us -> 32.1 us (0.79)
  the two profiles are of different devices: /device:TPU:21 before, /device:TPU:1 now
where the time goes in v2:
time: 32.1 us; the launch traced here: 31.5 us
  starting transfers between devices  12 us (37%)
  Pallas kernels  9.37 us (29%)
  waiting for transfers between devices  5.87 us (18%)
  local copies, waits for them, and re-layouts  3.48 us (11%)
  between operations  0.76 us (2%)
    ppermute x7, starting transfers between devices, swap(): return lax.ppermute(block, ('bank', 'seg'), route)  12 us
    pallas_call x3, Pallas kernels, call(): pl.pallas_call(run, in_specs=[smem, smem] + [vmem] * (len(inputs) - 2), o...  9.37 us
    ppermute x7, waiting for transfers between devices, swap(): return lax.ppermute(block, ('bank', 'seg'), route)  5.87 us
    slice x1, local copies, waits for them, and re-layouts, on_device(): slot = strain[step].reshape(2, 2, FB, FA)  1.92 us
    unnamed x14, local copies, waits for them, and re-layouts  0.8 us
    another operation x2, local copies, waits for them, and re-layouts, on_device(): slot = strain[step].reshape(2, 2, FB, FA)  0.76 us
  transfers between devices with their start and end apart: 7, of which 3 were waited for; matrix products, arithmetic and copies ran while one was open for 9% of the time, Pallas kernels for 14%

profile of v2, /device:TPU:1, one launch (start us, length us, event | category | flops | bytes accessed | tf_op | source)
XLA Modules:
  0.0 31.5 jit_solution(9818099398073811044)
XLA Ops:
  0.6 0.8 %constant_dynamic-update-slice_fusion.2 = (bf16[4,2,32,256]{3,2,1,0:T(8,128)(2,1)S(1)}, bf16[1,2,32,256]{3,2,1,0:T(8,128)(2,1)S(1)}) fusion(bf16[1,2,32,256]{3,1,2,0:T(2,128)(2,1)} %bitcast.8), kind=kLoop, calls=%fused_computation.5 | loop fusion | bytes 98304
  1.4 2.1 %collective-permute-start = (bf16[1,2,32,256]{3,2,1,0:T(8,128)(2,1)S(1)}, bf16[1,2,32,256]{3,2,1,0:T(8,128)(2,1)S(1)}, u32[]{:S(2)}, u32[]{:S(2)}) collective-permute-start(bf16[1,2,32,256]{3,2,1,0:T(8,128)(2,1)S(1)} %get-tuple-element.52), channel_id=1, source_target_pairs={{0,4},{1,3},{2,6},{3,1},{4,0},{5,7},{6,2},{7,5},{8,12},{9,11},{10,... | collective-permute-start | bytes 98312 | tf_op jit(solution)/shard_map/ppermute | solution.py:250
  3.5 1.9 %fusion = (bf16[1,2,2,65536]{3,2,1,0:T(2,128)(2,1)S(1)}, bf16[1,2,2,65536]{3,2,1,0:T(2,128)(2,1)S(1)}) fusion(bf16[2,2,2,65536]{3,2,1,0:T(2,128)(2,1)} %param.8), kind=kLoop, calls=%fused_computation.6 | loop fusion | bytes 2097152 | tf_op jit(solution)/shard_map/slice | solution.py:320
  5.4 0.4 %reshape_squeeze.6.rest_0_ = bf16[2,2,256,256]{3,2,1,0:T(8,128)(2,1)S(1)} reshape(bf16[1,2,2,65536]{3,2,1,0:T(2,128)(2,1)S(1)} %get-tuple-element.50) | data formatting | bytes 1048576 | tf_op jit(solution)/shard_map/reshape;squeeze | solution.py:320
  5.8 0.0 copy-start.4
  5.8 0.4 %reshape_squeeze.7.rest_1_ = bf16[2,2,256,256]{3,2,1,0:T(8,128)(2,1)S(1)} reshape(bf16[1,2,2,65536]{3,2,1,0:T(2,128)(2,1)S(1)} %get-tuple-element.49) | data formatting | bytes 1048576 | tf_op jit(solution)/shard_map/reshape;squeeze | solution.py:320
  6.2 0.0 copy-start.3
  6.2 0.0 collective-permute-done
  6.3 2.4 %collective-permute-start.1 = (bf16[2,2,32,256]{3,2,1,0:T(8,128)(2,1)S(1)}, bf16[2,2,32,256]{3,2,1,0:T(8,128)(2,1)S(1)}, u32[]{:S(2)}, u32[]{:S(2)}) collective-permute-start(bf16[2,2,32,256]{3,2,1,0:T(8,128)(2,1)S(1)} %pad_maximum_fusion.1), channel_id=1, source_target_pairs={{0,2},{1,5},{2,0},{3,7},{4,6},{5,1},{6,4},{7,3},{8,10},{9,13},{10,... | collective-permute-start | bytes 196616 | tf_op jit(solution)/shard_map/ppermute | solution.py:250
  8.6 2.2 %collective-permute-done.1 = bf16[2,2,32,256]{3,2,1,0:T(8,128)(2,1)S(1)} collective-permute-done((bf16[2,2,32,256]{3,2,1,0:T(8,128)(2,1)S(1)}, bf16[2,2,32,256]{3,2,1,0:T(8,128)(2,1)S(1)}, u32[]{:S(2)}, u32[]{:S(2)}) %collective-permute-start.1) | collective-permute-done | bytes 65568 | tf_op jit(solution)/shard_map/ppermute | solution.py:250
  10.9 0.0 copy-start
  10.9 0.0 copy-start.1
  10.9 0.0 copy-start.5
  10.9 1.7 %collective-permute-start.2 = (bf16[4,2,32,256]{3,2,1,0:T(8,128)(2,1)S(1)}, bf16[4,2,32,256]{3,2,1,0:T(8,128)(2,1)S(1)}, u32[]{:S(2)}, u32[]{:S(2)}) collective-permute-start(bf16[4,2,32,256]{3,2,1,0:T(8,128)(2,1)S(1)} %constant_dynamic-update-slice_fusion.rest_2_), channel_id=1, source_target_pairs={{0,1},{1,0},{2,3},{3,2},{4,5},{5,4},{6,7},{7,6},{8,9},{9,8},{10,11... | collective-permute-start | bytes 393224 | tf_op jit(solution)/shard_map/ppermute | solution.py:250
  12.7 1.0 %collective-permute-done.2.rest_3_ = bf16[4,2,32,256]{3,2,1,0:T(8,128)(2,1)S(1)} collective-permute-done((bf16[4,2,32,256]{3,2,1,0:T(8,128)(2,1)S(1)}, bf16[4,2,32,256]{3,2,1,0:T(8,128)(2,1)S(1)}, u32[]{:S(2)}, u32[]{:S(2)}) %collective-permute-start.2) | collective-permute-done | bytes 131104 | tf_op jit(solution)/shard_map/ppermute | solution.py:250
  13.7 1.3 %collective-permute-start.3 = (bf16[8,2,32,256]{3,2,1,0:T(8,128)(2,1)S(1)}, bf16[8,2,32,256]{3,2,1,0:T(8,128)(2,1)S(1)}, u32[]{:S(2)}, u32[]{:S(2)}) collective-permute-start(bf16[8,2,32,256]{3,2,1,0:T(8,128)(2,1)S(1)} %pad_maximum_fusion), channel_id=1, source_target_pairs={{0,8},{1,17},{2,10},{3,19},{4,12},{5,21},{6,14},{7,23},{8,0},{9,25... | collective-permute-start | bytes 786440 | tf_op jit(solution)/shard_map/ppermute | solution.py:250
  15.0 1.2 %collective-permute-start.4 = (bf16[4,2,32,256]{3,2,1,0:T(8,128)(2,1)S(1)}, bf16[4,2,32,256]{3,2,1,0:T(8,128)(2,1)S(1)}, u32[]{:S(2)}, u32[]{:S(2)}) collective-permute-start(bf16[4,2,32,256]{3,2,1,0:T(8,128)(2,1)S(1)} %constant_dynamic-update-slice_fusion.rest_2_), channel_id=1, source_target_pairs={{0,24},{1,25},{2,26},{3,27},{4,28},{5,29},{6,30},{7,31},{8,16},{9,... | collective-permute-start | bytes 393224 | tf_op jit(solution)/shard_map/ppermute | solution.py:250
  16.1 0.0 copy-done.4
  16.2 0.0 copy-done.3
  16.2 0.0 copy-done
  16.2 0.0 copy-done.1
  16.2 0.0 copy-done.5
  16.2 2.2 %shard_map.103 = (f32[64,512]{1,0:T(8,128)S(1)}, f32[2,16,128]{2,1,0:T(8,128)S(1)}, f32[1,16,128]{2,1,0:T(8,128)S(1)}) custom-call(s32[2]{0:T(128)S(1)} %copy-done.1, s32[4,15]{1,0:T(4,128)S(1)} %copy-done, bf16[512,512]{1,0:T(8,128)(2,1)S(1)} %copy-done.4, bf16[2,256,256]{2,1,0:T(8,128)(2,1)S(1)} %copy-done.5, f32[2,256,256]{2,1,0:T(8,128)S(1)} %copy-done.3, ...), custom_call_target="tpu_custom_call" | custom-call | flops 805306368 | bytes 1048576 | tf_op jit(solution)/shard_map/pallas_call | solution.py:303
  18.4 2.6 %collective-permute-done.4.rest_3_ = bf16[4,2,32,256]{3,2,1,0:T(8,128)(2,1)S(1)} collective-permute-done((bf16[4,2,32,256]{3,2,1,0:T(8,128)(2,1)S(1)}, bf16[4,2,32,256]{3,2,1,0:T(8,128)(2,1)S(1)}, u32[]{:S(2)}, u32[]{:S(2)}) %collective-permute-start.4) | collective-permute-done | bytes 131104 | tf_op jit(solution)/shard_map/ppermute | solution.py:250
  21.0 0.0 collective-permute-done.3.rest_2_
  21.0 3.2 %collective-permute-start.5 = (bf16[8,2,32,256]{3,2,1,0:T(8,128)(2,1)S(1)}, bf16[8,2,32,256]{3,2,1,0:T(8,128)(2,1)S(1)}, u32[]{:S(2)}, u32[]{:S(2)}) collective-permute-start(bf16[8,2,32,256]{3,2,1,0:T(8,128)(2,1)S(1)} %collective-permute-done.3.rest_2_), channel_id=1, source_target_pairs={{0,1},{1,0},{2,3},{3,2},{4,5},{5,4},{6,7},{7,6},{8,9},{9,8},{10,11... | collective-permute-start | bytes 786440 | tf_op jit(solution)/shard_map/ppermute | solution.py:250
  24.3 0.1 collective-permute-start.6
  24.3 2.2 %shard_map.104 = (f32[64,512]{1,0:T(8,128)S(1)}, f32[2,16,128]{2,1,0:T(8,128)S(1)}, f32[1,16,128]{2,1,0:T(8,128)S(1)}) custom-call(s32[2]{0:T(128)S(1)} %copy-done.1, s32[4,15]{1,0:T(4,128)S(1)} %copy-done, bf16[512,512]{1,0:T(8,128)(2,1)S(1)} %copy-done.4, bf16[2,256,256]{2,1,0:T(8,128)(2,1)S(1)} %copy-done.5, f32[2,256,256]{2,1,0:T(8,128)S(1)} %copy-done.3, ...), custom_call_target="tpu_custom_call" | custom-call | flops 805306368 | bytes 1048576 | tf_op jit(solution)/shard_map/pallas_call | solution.py:303
  26.5 0.0 collective-permute-done.6.rest_4_
  26.6 0.0 collective-permute-done.5.rest_2_
  26.6 0.0 copy-done.2
  26.6 4.9 %shard_map.105 = (f32[2,4]{1,0:T(2,128)}, f32[4,2,256]{2,1,0:T(2,128)}, f32[4,2,256]{2,1,0:T(2,128)}) custom-call(s32[2]{0:T(128)S(1)} %copy-done.1, s32[4,15]{1,0:T(4,128)S(1)} %copy-done, bf16[512,512]{1,0:T(8,128)(2,1)S(1)} %copy-done.4, bf16[2,256,256]{2,1,0:T(8,128)(2,1)S(1)} %copy-done.5, f32[2,256,256]{2,1,0:T(8,128)S(1)} %copy-done.3, ...), custom_call_target="tpu_custom_call" | custom-call | flops 1610612736 | bytes 1048576 | tf_op jit(solution)/shard_map/pallas_call | solution.py:303
  (5 shorter events, 0.0 us)
Async XLA Ops:
  1.4 4.8 %collective-permute-start = (bf16[1,2,32,256]{3,2,1,0:T(8,128)(2,1)S(1)}, bf16[1,2,32,256]{3,2,1,0:T(8,128)(2,1)S(1)}, u32[]{:S(2)}, u32[]{:S(2)}) collective-permute-start(bf16[1,2,32,256]{3,2,1,0:T(8,128)(2,1)S(1)} %get-tuple-element.52), channel_id=1, source_target_pairs={{0,4},{1,3},{2,6},{3,1},{4,0},{5,7},{6,2},{7,5},{8,12},{9,11},{10,... | collective-permute-start | bytes 98312 | tf_op jit(solution)/shard_map/ppermute | solution.py:250
  5.8 10.3 %copy-start.4 = (bf16[512,512]{1,0:T(8,128)(2,1)S(1)}, bf16[512,512]{1,0:T(8,128)(2,1)}, u32[]{:S(2)}) copy-start(bf16[512,512]{1,0:T(8,128)(2,1)} %constant.8.clone.first_ref) | copy-start | bytes 1572868
  6.2 9.9 %copy-start.3 = (f32[2,256,256]{2,1,0:T(8,128)S(1)}, f32[2,256,256]{2,1,0:T(8,128)}, u32[]{:S(2)}) copy-start(f32[2,256,256]{2,1,0:T(8,128)} %constant.11.clone.turn_ref) | copy-start | bytes 1572868
  6.3 4.6 %collective-permute-start.1 = (bf16[2,2,32,256]{3,2,1,0:T(8,128)(2,1)S(1)}, bf16[2,2,32,256]{3,2,1,0:T(8,128)(2,1)S(1)}, u32[]{:S(2)}, u32[]{:S(2)}) collective-permute-start(bf16[2,2,32,256]{3,2,1,0:T(8,128)(2,1)S(1)} %pad_maximum_fusion.1), channel_id=1, source_target_pairs={{0,2},{1,5},{2,0},{3,7},{4,6},{5,1},{6,4},{7,3},{8,10},{9,13},{10,... | collective-permute-start | bytes 196616 | tf_op jit(solution)/shard_map/ppermute | solution.py:250
  10.9 5.3 %copy-start = (s32[4,15]{1,0:T(4,128)S(1)}, s32[4,15]{1,0:T(4,128)}, u32[]{:S(2)}) copy-start(s32[4,15]{1,0:T(4,128)} %edges_ref.5) | copy-start | bytes 724
  10.9 5.3 %copy-start.1 = (s32[2]{0:T(128)S(1)}, s32[2]{0:T(128)}, u32[]{:S(2)}) copy-start(s32[2]{0:T(128)} %live_ref.5) | copy-start | bytes 28
  10.9 5.3 %copy-start.5 = (bf16[2,256,256]{2,1,0:T(8,128)(2,1)S(1)}, bf16[2,256,256]{2,1,0:T(8,128)(2,1)}, u32[]{:S(2)}) copy-start(bf16[2,256,256]{2,1,0:T(8,128)(2,1)} %constant.9.clone.second_ref) | copy-start | bytes 786436
  10.9 2.7 %collective-permute-start.2 = (bf16[4,2,32,256]{3,2,1,0:T(8,128)(2,1)S(1)}, bf16[4,2,32,256]{3,2,1,0:T(8,128)(2,1)S(1)}, u32[]{:S(2)}, u32[]{:S(2)}) collective-permute-start(bf16[4,2,32,256]{3,2,1,0:T(8,128)(2,1)S(1)} %constant_dynamic-update-slice_fusion.rest_2_), channel_id=1, source_target_pairs={{0,1},{1,0},{2,3},{3,2},{4,5},{5,4},{6,7},{7,6},{8,9},{9,8},{10,11... | collective-permute-start | bytes 393224 | tf_op jit(solution)/shard_map/ppermute | solution.py:250
  13.7 7.3 %collective-permute-start.3 = (bf16[8,2,32,256]{3,2,1,0:T(8,128)(2,1)S(1)}, bf16[8,2,32,256]{3,2,1,0:T(8,128)(2,1)S(1)}, u32[]{:S(2)}, u32[]{:S(2)}) collective-permute-start(bf16[8,2,32,256]{3,2,1,0:T(8,128)(2,1)S(1)} %pad_maximum_fusion), channel_id=1, source_target_pairs={{0,8},{1,17},{2,10},{3,19},{4,12},{5,21},{6,14},{7,23},{8,0},{9,25... | collective-permute-start | bytes 786440 | tf_op jit(solution)/shard_map/ppermute | solution.py:250
  15.0 6.0 %collective-permute-start.4 = (bf16[4,2,32,256]{3,2,1,0:T(8,128)(2,1)S(1)}, bf16[4,2,32,256]{3,2,1,0:T(8,128)(2,1)S(1)}, u32[]{:S(2)}, u32[]{:S(2)}) collective-permute-start(bf16[4,2,32,256]{3,2,1,0:T(8,128)(2,1)S(1)} %constant_dynamic-update-slice_fusion.rest_2_), channel_id=1, source_target_pairs={{0,24},{1,25},{2,26},{3,27},{4,28},{5,29},{6,30},{7,31},{8,16},{9,... | collective-permute-start | bytes 393224 | tf_op jit(solution)/shard_map/ppermute | solution.py:250
  21.0 5.5 %copy-start.2 = (bf16[2,512,512]{2,1,0:T(8,128)(2,1)S(1)}, bf16[2,512,512]{2,1,0:T(8,128)(2,1)}, u32[]{:S(2)}) copy-start(bf16[2,512,512]{2,1,0:T(8,128)(2,1)} %constant.10.clone.rest_5_) | copy-start | bytes 3145732
  21.0 5.5 %collective-permute-start.5 = (bf16[8,2,32,256]{3,2,1,0:T(8,128)(2,1)S(1)}, bf16[8,2,32,256]{3,2,1,0:T(8,128)(2,1)S(1)}, u32[]{:S(2)}, u32[]{:S(2)}) collective-permute-start(bf16[8,2,32,256]{3,2,1,0:T(8,128)(2,1)S(1)} %collective-permute-done.3.rest_2_), channel_id=1, source_target_pairs={{0,1},{1,0},{2,3},{3,2},{4,5},{5,4},{6,7},{7,6},{8,9},{9,8},{10,11... | collective-permute-start | bytes 786440 | tf_op jit(solution)/shard_map/ppermute | solution.py:250
  24.3 2.3 %collective-permute-start.6 = (bf16[4,2,32,256]{3,2,1,0:T(8,128)(2,1)S(1)}, bf16[4,2,32,256]{3,2,1,0:T(8,128)(2,1)S(1)}, u32[]{:S(2)}, u32[]{:S(2)}) collective-permute-start(bf16[4,2,32,256]{3,2,1,0:T(8,128)(2,1)S(1)} %collective-permute-done.4.rest_3_), channel_id=1, source_target_pairs={{0,1},{1,0},{2,3},{3,2},{4,5},{5,4},{6,7},{7,6},{8,9},{9,8},{10,11... | collective-permute-start | bytes 393224 | tf_op jit(solution)/shard_map/ppermute | solution.py:250

commit v3 on v2

--- a/solution.py
+++ b/solution.py
@@ -318,25 +318,27 @@
         found = swap(block, [(0, orders[c][step]) for c in range(2)])
         if step < held:
             slot = strain[step].reshape(2, 2, FB, FA)
-            found, slot = lax.optimization_barrier((found, slot))
+            found, slot, strain = lax.optimization_barrier((found, slot, strain))
             slots.append(slot)
         block = jnp.concatenate([block, found], axis=0)
     for s in range(len(slots), held):
         slots.append(strain[s].reshape(2, 2, FB, FA))
     other = swap(block, twin)
-    corner = swap(block, ((3, 0), (3, 0)))
     side = swap(jnp.concatenate([block, other], axis=0), ((1, 0), (2, 0)))
     here = call([(0, 0)], [block, other], [((0, 0), (1, 0))])
-    side, corner, here = lax.optimization_barrier((side, corner, here))
+    side, here = lax.optimization_barrier((side, here))
+    corner = swap(side[: low * tiles], ((2, 0), (1, 0)))
     far = swap(side, twin)
+    beside = call([(1, 2)], [side], [((0, 0), (0, low))])
+    corner, beside = lax.optimization_barrier((corner, beside))
     other_corner = swap(corner, twin)
-    beside = call([(1, 2)], [side], [((0, 0), (0, low))])
-    far, other_corner, beside = lax.optimization_barrier((far, other_corner, beside))
+    across = call([(2, 1)], [far], [((0, low), (0, 0))])
+    other_corner, across = lax.optimization_barrier((other_corner, across))
     peak, snr, chi = call(
-        [(2, 1), (3, 3)],
-        [far, corner, other_corner],
-        [((0, low), (0, 0)), ((1, 0), (2, 0))],
-        ([(0, 0), (1, 2)], [here, beside]),
+        [(3, 3)],
+        [corner, other_corner],
+        [((0, 0), (1, 0))],
+        ([(0, 0), (1, 2), (2, 1)], [here, beside, across]),
     )
     return peak.T, snr, chi
 

time: 32.1 us -> 30.4 us (0.947); the launches traced: 31.5 us -> 30.2 us
  local copies, waits for them, and re-layouts: 3.48 us -> 1.54 us
  starting transfers between devices: 12 us -> 12.6 us
    slice x1 -> x4, local copies, waits for them, and re-layouts: 1.92 us -> 0.01 us  [on_device(): slot = strain[step].reshape(2, 2, FB, FA)]
    ppermute x7, starting transfers between devices: 12 us -> 12.6 us  [swap(): return lax.ppermute(block, ('bank', 'seg'), route)]
    pallas_call x3 -> x4, Pallas kernels: 9.37 us -> 9.52 us  [call(): pl.pallas_call(run, in_specs=[smem, smem] + [vmem] * (len(inputs) - 2), o...]
  transfers between devices with their start and end apart: 7 -> 7, of which waited for: 3 -> 5; matrix products, arithmetic and copies ran while one was open for 9% -> 2% of each run, Pallas kernels for 14% -> 21%
where the time goes in v3:
time: 30.4 us; the launch traced here: 30.2 us
  starting transfers between devices  12.6 us (41%)
  Pallas kernels  9.52 us (31%)
  waiting for transfers between devices  5.7 us (19%)
  local copies, waits for them, and re-layouts  1.54 us (5%)
  between operations  0.75 us (2%)
    ppermute x7, starting transfers between devices, swap(): return lax.ppermute(block, ('bank', 'seg'), route)  12.6 us
    pallas_call x4, Pallas kernels, call(): pl.pallas_call(run, in_specs=[smem, smem] + [vmem] * (len(inputs) - 2), o...  9.52 us
    ppermute x7, waiting for transfers between devices, swap(): return lax.ppermute(block, ('bank', 'seg'), route)  5.7 us
    unnamed x14, local copies, waits for them, and re-layouts  0.8 us
    another operation x2, local copies, waits for them, and re-layouts, on_device(): slot = strain[step].reshape(2, 2, FB, FA)  0.71 us
  transfers between devices with their start and end apart: 7, of which 5 were waited for; matrix products, arithmetic and copies ran while one was open for 2% of the time, Pallas kernels for 21%

profile of v3, /device:TPU:1, one launch (start us, length us, event | category | flops | bytes accessed | tf_op | source)
XLA Modules:
  0.0 30.2 jit_solution(1934735076945673410)
XLA Ops:
  0.6 0.8 %constant_dynamic-update-slice_fusion.2 = (bf16[4,2,32,256]{3,2,1,0:T(8,128)(2,1)S(1)}, bf16[1,2,32,256]{3,2,1,0:T(8,128)(2,1)S(1)}) fusion(bf16[1,2,32,256]{3,1,2,0:T(2,128)(2,1)} %bitcast.8), kind=kLoop, calls=%fused_computation.5 | loop fusion | bytes 98304
  1.4 2.2 %collective-permute-start = (bf16[1,2,32,256]{3,2,1,0:T(8,128)(2,1)S(1)}, bf16[1,2,32,256]{3,2,1,0:T(8,128)(2,1)S(1)}, u32[]{:S(2)}, u32[]{:S(2)}) collective-permute-start(bf16[1,2,32,256]{3,2,1,0:T(8,128)(2,1)S(1)} %get-tuple-element.62), channel_id=1, source_target_pairs={{0,4},{1,3},{2,6},{3,1},{4,0},{5,7},{6,2},{7,5},{8,12},{9,11},{10,... | collective-permute-start | bytes 98312 | tf_op jit(solution)/shard_map/ppermute | solution.py:250
  3.6 0.0 slice-done
  3.6 0.4 %reshape_squeeze.6.rest_0_ = bf16[2,2,256,256]{3,2,1,0:T(8,128)(2,1)S(1)} reshape(bf16[1,2,2,65536]{3,2,1,0:T(2,128)(2,1)S(1)} %slice-done) | data formatting | bytes 1048576 | tf_op jit(solution)/shard_map/reshape;squeeze | solution.py:320
  4.0 0.9 %collective-permute-done = bf16[1,2,32,256]{3,2,1,0:T(8,128)(2,1)S(1)} collective-permute-done((bf16[1,2,32,256]{3,2,1,0:T(8,128)(2,1)S(1)}, bf16[1,2,32,256]{3,2,1,0:T(8,128)(2,1)S(1)}, u32[]{:S(2)}, u32[]{:S(2)}) %collective-permute-start) | collective-permute-done | bytes 32800 | tf_op jit(solution)/shard_map/ppermute | solution.py:250
  4.9 0.0 slice-start.1
  4.9 2.5 %collective-permute-start.1 = (bf16[2,2,32,256]{3,2,1,0:T(8,128)(2,1)S(1)}, bf16[2,2,32,256]{3,2,1,0:T(8,128)(2,1)S(1)}, u32[]{:S(2)}, u32[]{:S(2)}) collective-permute-start(bf16[2,2,32,256]{3,2,1,0:T(8,128)(2,1)S(1)} %pad_maximum_fusion.1), channel_id=1, source_target_pairs={{0,2},{1,5},{2,0},{3,7},{4,6},{5,1},{6,4},{7,3},{8,10},{9,13},{10,... | collective-permute-start | bytes 196616 | tf_op jit(solution)/shard_map/ppermute | solution.py:250
  7.5 0.0 slice-done.1
  7.5 0.4 %reshape_squeeze.7.rest_1_ = bf16[2,2,256,256]{3,2,1,0:T(8,128)(2,1)S(1)} reshape(bf16[1,2,2,65536]{3,2,1,0:T(2,128)(2,1)S(1)} %slice-done.1) | data formatting | bytes 1048576 | tf_op jit(solution)/shard_map/reshape;squeeze | solution.py:320
  7.8 0.0 copy-start.1
  7.9 1.3 %collective-permute-done.1 = bf16[2,2,32,256]{3,2,1,0:T(8,128)(2,1)S(1)} collective-permute-done((bf16[2,2,32,256]{3,2,1,0:T(8,128)(2,1)S(1)}, bf16[2,2,32,256]{3,2,1,0:T(8,128)(2,1)S(1)}, u32[]{:S(2)}, u32[]{:S(2)}) %collective-permute-start.1) | collective-permute-done | bytes 65568 | tf_op jit(solution)/shard_map/ppermute | solution.py:250
  9.1 0.0 copy-start.5
  9.1 2.8 %collective-permute-start.2 = (bf16[4,2,32,256]{3,2,1,0:T(8,128)(2,1)S(1)}, bf16[4,2,32,256]{3,2,1,0:T(8,128)(2,1)S(1)}, u32[]{:S(2)}, u32[]{:S(2)}) collective-permute-start(bf16[4,2,32,256]{3,2,1,0:T(8,128)(2,1)S(1)} %constant_dynamic-update-slice_fusion.rest_2_), channel_id=1, source_target_pairs={{0,1},{1,0},{2,3},{3,2},{4,5},{5,4},{6,7},{7,6},{8,9},{9,8},{10,11... | collective-permute-start | bytes 393224 | tf_op jit(solution)/shard_map/ppermute | solution.py:250
  11.9 1.0 %collective-permute-done.2.rest_3_ = bf16[4,2,32,256]{3,2,1,0:T(8,128)(2,1)S(1)} collective-permute-done((bf16[4,2,32,256]{3,2,1,0:T(8,128)(2,1)S(1)}, bf16[4,2,32,256]{3,2,1,0:T(8,128)(2,1)S(1)}, u32[]{:S(2)}, u32[]{:S(2)}) %collective-permute-start.2) | collective-permute-done | bytes 131104 | tf_op jit(solution)/shard_map/ppermute | solution.py:250
  12.9 1.6 %collective-permute-start.3 = (bf16[8,2,32,256]{3,2,1,0:T(8,128)(2,1)S(1)}, bf16[8,2,32,256]{3,2,1,0:T(8,128)(2,1)S(1)}, u32[]{:S(2)}, u32[]{:S(2)}) collective-permute-start(bf16[8,2,32,256]{3,2,1,0:T(8,128)(2,1)S(1)} %pad_maximum_fusion), channel_id=1, source_target_pairs={{0,8},{1,17},{2,10},{3,19},{4,12},{5,21},{6,14},{7,23},{8,0},{9,25... | collective-permute-start | bytes 786440 | tf_op jit(solution)/shard_map/ppermute | solution.py:250
  14.6 0.0 copy-done.2
  14.6 0.0 copy-done.3
  14.6 0.0 copy-done.1
  14.6 0.0 copy-done.4
  14.6 0.0 copy-done.5
  14.6 2.1 %shard_map.103 = (f32[64,512]{1,0:T(8,128)S(1)}, f32[2,16,128]{2,1,0:T(8,128)S(1)}, f32[1,16,128]{2,1,0:T(8,128)S(1)}) custom-call(s32[2]{0:T(128)S(1)} %copy-done.5, s32[4,15]{1,0:T(4,128)S(1)} %copy-done.4, bf16[512,512]{1,0:T(8,128)(2,1)S(1)} %copy-done.2, bf16[2,256,256]{2,1,0:T(8,128)(2,1)S(1)} %copy-done.3, f32[2,256,256]{2,1,0:T(8,128)S(1)} %copy-done.1, ...), custom_call_target="tpu_custom_call" | custom-call | flops 805306368 | bytes 1048576 | tf_op jit(solution)/shard_map/pallas_call | solution.py:303
  16.7 1.9 %collective-permute-done.3.rest_2_ = bf16[8,2,32,256]{3,2,1,0:T(8,128)(2,1)S(1)} collective-permute-done((bf16[8,2,32,256]{3,2,1,0:T(8,128)(2,1)S(1)}, bf16[8,2,32,256]{3,2,1,0:T(8,128)(2,1)S(1)}, u32[]{:S(2)}, u32[]{:S(2)}) %collective-permute-start.3) | collective-permute-done | bytes 262176 | tf_op jit(solution)/shard_map/ppermute | solution.py:250
  18.6 1.1 %collective-permute-start.6 = (bf16[8,2,32,256]{3,2,1,0:T(8,128)(2,1)S(1)}, bf16[8,2,32,256]{3,2,1,0:T(8,128)(2,1)S(1)}, u32[]{:S(2)}, u32[]{:S(2)}) collective-permute-start(bf16[8,2,32,256]{3,2,1,0:T(8,128)(2,1)S(1)} %collective-permute-done.3.rest_2_), channel_id=1, source_target_pairs={{0,1},{1,0},{2,3},{3,2},{4,5},{5,4},{6,7},{7,6},{8,9},{9,8},{10,11... | collective-permute-start | bytes 786440 | tf_op jit(solution)/shard_map/ppermute | solution.py:250
  19.7 1.6 %collective-permute-start.4 = (bf16[4,2,32,256]{3,2,1,0:T(8,128)(2,1)S(1)}, bf16[4,2,32,256]{3,2,1,0:T(8,128)(2,1)S(1)}, u32[]{:S(2)}, u32[]{:S(2)}) collective-permute-start(bf16[4,2,32,256]{3,2,1,0:T(8,128)(2,1)S(1)} %slice.11), channel_id=1, source_target_pairs={{0,16},{1,9},{2,18},{3,11},{4,20},{5,13},{6,22},{7,15},{8,24},{9,1... | collective-permute-start | bytes 393224 | tf_op jit(solution)/shard_map/ppermute | solution.py:250
  21.3 2.1 %shard_map.104 = (f32[64,512]{1,0:T(8,128)S(1)}, f32[2,16,128]{2,1,0:T(8,128)S(1)}, f32[1,16,128]{2,1,0:T(8,128)S(1)}) custom-call(s32[2]{0:T(128)S(1)} %copy-done.5, s32[4,15]{1,0:T(4,128)S(1)} %copy-done.4, bf16[512,512]{1,0:T(8,128)(2,1)S(1)} %copy-done.2, bf16[2,256,256]{2,1,0:T(8,128)(2,1)S(1)} %copy-done.3, f32[2,256,256]{2,1,0:T(8,128)S(1)} %copy-done.1, ...), custom_call_target="tpu_custom_call" | custom-call | flops 805306368 | bytes 1048576 | tf_op jit(solution)/shard_map/pallas_call | solution.py:303
  23.4 0.6 %collective-permute-done.4.rest_2_ = bf16[4,2,32,256]{3,2,1,0:T(8,128)(2,1)S(1)} collective-permute-done((bf16[4,2,32,256]{3,2,1,0:T(8,128)(2,1)S(1)}, bf16[4,2,32,256]{3,2,1,0:T(8,128)(2,1)S(1)}, u32[]{:S(2)}, u32[]{:S(2)}) %collective-permute-start.4) | collective-permute-done | bytes 131104 | tf_op jit(solution)/shard_map/ppermute | solution.py:250
  24.0 0.8 %collective-permute-start.5 = (bf16[4,2,32,256]{3,2,1,0:T(8,128)(2,1)S(1)}, bf16[4,2,32,256]{3,2,1,0:T(8,128)(2,1)S(1)}, u32[]{:S(2)}, u32[]{:S(2)}) collective-permute-start(bf16[4,2,32,256]{3,2,1,0:T(8,128)(2,1)S(1)} %collective-permute-done.4.rest_2_), channel_id=1, source_target_pairs={{0,1},{1,0},{2,3},{3,2},{4,5},{5,4},{6,7},{7,6},{8,9},{9,8},{10,11... | collective-permute-start | bytes 393224 | tf_op jit(solution)/shard_map/ppermute | solution.py:250
  24.8 0.0 collective-permute-done.6.rest_2_
  24.8 2.1 %shard_map.105 = (f32[64,512]{1,0:T(8,128)S(1)}, f32[2,16,128]{2,1,0:T(8,128)S(1)}, f32[1,16,128]{2,1,0:T(8,128)S(1)}) custom-call(s32[2]{0:T(128)S(1)} %copy-done.5, s32[4,15]{1,0:T(4,128)S(1)} %copy-done.4, bf16[512,512]{1,0:T(8,128)(2,1)S(1)} %copy-done.2, bf16[2,256,256]{2,1,0:T(8,128)(2,1)S(1)} %copy-done.3, f32[2,256,256]{2,1,0:T(8,128)S(1)} %copy-done.1, ...), custom_call_target="tpu_custom_call" | custom-call | flops 805306368 | bytes 1048576 | tf_op jit(solution)/shard_map/pallas_call | solution.py:303
  26.9 0.0 collective-permute-done.5.rest_3_
  26.9 0.0 copy-done
  26.9 3.3 %shard_map.106 = (f32[2,4]{1,0:T(2,128)}, f32[4,2,256]{2,1,0:T(2,128)}, f32[4,2,256]{2,1,0:T(2,128)}) custom-call(s32[2]{0:T(128)S(1)} %copy-done.5, s32[4,15]{1,0:T(4,128)S(1)} %copy-done.4, bf16[512,512]{1,0:T(8,128)(2,1)S(1)} %copy-done.2, bf16[2,256,256]{2,1,0:T(8,128)(2,1)S(1)} %copy-done.3, f32[2,256,256]{2,1,0:T(8,128)S(1)} %copy-done.1, ...), custom_call_target="tpu_custom_call" | custom-call | flops 805306368 | bytes 1048576 | tf_op jit(solution)/shard_map/pallas_call | solution.py:303
  (10 shorter events, 0.1 us)
Async XLA Ops:
  1.4 2.2 %slice-start = ((bf16[2,2,2,65536]{3,2,1,0:T(2,128)(2,1)}), bf16[1,2,2,65536]{3,2,1,0:T(2,128)(2,1)S(1)}, s32[]{:S(2)}) async-start(bf16[2,2,2,65536]{3,2,1,0:T(2,128)(2,1)} %param.8), calls=%async_computation | async-start | bytes 1048576 | tf_op jit(solution)/shard_map/slice | solution.py:320
  1.4 3.5 %collective-permute-start = (bf16[1,2,32,256]{3,2,1,0:T(8,128)(2,1)S(1)}, bf16[1,2,32,256]{3,2,1,0:T(8,128)(2,1)S(1)}, u32[]{:S(2)}, u32[]{:S(2)}) collective-permute-start(bf16[1,2,32,256]{3,2,1,0:T(8,128)(2,1)S(1)} %get-tuple-element.62), channel_id=1, source_target_pairs={{0,4},{1,3},{2,6},{3,1},{4,0},{5,7},{6,2},{7,5},{8,12},{9,11},{10,... | collective-permute-start | bytes 98312 | tf_op jit(solution)/shard_map/ppermute | solution.py:250
  4.9 2.6 %slice-start.1 = ((bf16[2,2,2,65536]{3,2,1,0:T(2,128)(2,1)}), bf16[1,2,2,65536]{3,2,1,0:T(2,128)(2,1)S(1)}, s32[]{:S(2)}) async-start(bf16[2,2,2,65536]{3,2,1,0:T(2,128)(2,1)} %param.8), calls=%async_computation.1 | async-start | bytes 1048576 | tf_op jit(solution)/shard_map/slice | solution.py:320
  4.9 4.2 %collective-permute-start.1 = (bf16[2,2,32,256]{3,2,1,0:T(8,128)(2,1)S(1)}, bf16[2,2,32,256]{3,2,1,0:T(8,128)(2,1)S(1)}, u32[]{:S(2)}, u32[]{:S(2)}) collective-permute-start(bf16[2,2,32,256]{3,2,1,0:T(8,128)(2,1)S(1)} %pad_maximum_fusion.1), channel_id=1, source_target_pairs={{0,2},{1,5},{2,0},{3,7},{4,6},{5,1},{6,4},{7,3},{8,10},{9,13},{10,... | collective-permute-start | bytes 196616 | tf_op jit(solution)/shard_map/ppermute | solution.py:250
  7.5 7.1 %copy-start.2 = (bf16[512,512]{1,0:T(8,128)(2,1)S(1)}, bf16[512,512]{1,0:T(8,128)(2,1)}, u32[]{:S(2)}) copy-start(bf16[512,512]{1,0:T(8,128)(2,1)} %constant.8.clone.first_ref) | copy-start | bytes 1572868
  7.5 7.1 %copy-start.3 = (bf16[2,256,256]{2,1,0:T(8,128)(2,1)S(1)}, bf16[2,256,256]{2,1,0:T(8,128)(2,1)}, u32[]{:S(2)}) copy-start(bf16[2,256,256]{2,1,0:T(8,128)(2,1)} %constant.9.clone.second_ref) | copy-start | bytes 786436
  7.8 6.7 %copy-start.1 = (f32[2,256,256]{2,1,0:T(8,128)S(1)}, f32[2,256,256]{2,1,0:T(8,128)}, u32[]{:S(2)}) copy-start(f32[2,256,256]{2,1,0:T(8,128)} %constant.11.clone.turn_ref) | copy-start | bytes 1572868
  9.1 5.4 %copy-start.4 = (s32[4,15]{1,0:T(4,128)S(1)}, s32[4,15]{1,0:T(4,128)}, u32[]{:S(2)}) copy-start(s32[4,15]{1,0:T(4,128)} %edges_ref.7) | copy-start | bytes 724
  9.1 5.4 %copy-start.5 = (s32[2]{0:T(128)S(1)}, s32[2]{0:T(128)}, u32[]{:S(2)}) copy-start(s32[2]{0:T(128)} %live_ref.7) | copy-start | bytes 28
  9.1 3.7 %collective-permute-start.2 = (bf16[4,2,32,256]{3,2,1,0:T(8,128)(2,1)S(1)}, bf16[4,2,32,256]{3,2,1,0:T(8,128)(2,1)S(1)}, u32[]{:S(2)}, u32[]{:S(2)}) collective-permute-start(bf16[4,2,32,256]{3,2,1,0:T(8,128)(2,1)S(1)} %constant_dynamic-update-slice_fusion.rest_2_), channel_id=1, source_target_pairs={{0,1},{1,0},{2,3},{3,2},{4,5},{5,4},{6,7},{7,6},{8,9},{9,8},{10,11... | collective-permute-start | bytes 393224 | tf_op jit(solution)/shard_map/ppermute | solution.py:250
  12.9 5.7 %collective-permute-start.3 = (bf16[8,2,32,256]{3,2,1,0:T(8,128)(2,1)S(1)}, bf16[8,2,32,256]{3,2,1,0:T(8,128)(2,1)S(1)}, u32[]{:S(2)}, u32[]{:S(2)}) collective-permute-start(bf16[8,2,32,256]{3,2,1,0:T(8,128)(2,1)S(1)} %pad_maximum_fusion), channel_id=1, source_target_pairs={{0,8},{1,17},{2,10},{3,19},{4,12},{5,21},{6,14},{7,23},{8,0},{9,25... | collective-permute-start | bytes 786440 | tf_op jit(solution)/shard_map/ppermute | solution.py:250
  18.6 6.2 %collective-permute-start.6 = (bf16[8,2,32,256]{3,2,1,0:T(8,128)(2,1)S(1)}, bf16[8,2,32,256]{3,2,1,0:T(8,128)(2,1)S(1)}, u32[]{:S(2)}, u32[]{:S(2)}) collective-permute-start(bf16[8,2,32,256]{3,2,1,0:T(8,128)(2,1)S(1)} %collective-permute-done.3.rest_2_), channel_id=1, source_target_pairs={{0,1},{1,0},{2,3},{3,2},{4,5},{5,4},{6,7},{7,6},{8,9},{9,8},{10,11... | collective-permute-start | bytes 786440 | tf_op jit(solution)/shard_map/ppermute | solution.py:250
  19.7 4.3 %collective-permute-start.4 = (bf16[4,2,32,256]{3,2,1,0:T(8,128)(2,1)S(1)}, bf16[4,2,32,256]{3,2,1,0:T(8,128)(2,1)S(1)}, u32[]{:S(2)}, u32[]{:S(2)}) collective-permute-start(bf16[4,2,32,256]{3,2,1,0:T(8,128)(2,1)S(1)} %slice.11), channel_id=1, source_target_pairs={{0,16},{1,9},{2,18},{3,11},{4,20},{5,13},{6,22},{7,15},{8,24},{9,1... | collective-permute-start | bytes 393224 | tf_op jit(solution)/shard_map/ppermute | solution.py:250
  24.0 2.9 %copy-start = (bf16[2,512,512]{2,1,0:T(8,128)(2,1)S(1)}, bf16[2,512,512]{2,1,0:T(8,128)(2,1)}, u32[]{:S(2)}) copy-start(bf16[2,512,512]{2,1,0:T(8,128)(2,1)} %constant.10.clone.rest_4_) | copy-start | bytes 3145732
  24.0 2.9 %collective-permute-start.5 = (bf16[4,2,32,256]{3,2,1,0:T(8,128)(2,1)S(1)}, bf16[4,2,32,256]{3,2,1,0:T(8,128)(2,1)S(1)}, u32[]{:S(2)}, u32[]{:S(2)}) collective-permute-start(bf16[4,2,32,256]{3,2,1,0:T(8,128)(2,1)S(1)} %collective-permute-done.4.rest_2_), channel_id=1, source_target_pairs={{0,1},{1,0},{2,3},{3,2},{4,5},{5,4},{6,7},{7,6},{8,9},{9,8},{10,11... | collective-permute-start | bytes 393224 | tf_op jit(solution)/shard_map/ppermute | solution.py:250

commit v4 on v3

--- a/solution.py
+++ b/solution.py
@@ -54,24 +54,28 @@
     return upper, (value - upper.astype(F32)).astype(BF16)
 
 
-def flip_orders(nseg):
+def doublings(nseg):
     flips = [1 << k for k in range(1, nseg.bit_length() - 1)]
     return flips[::-1], flips
 
 
-def reach(order, place):
-    seg = 0
-    for k, flip in enumerate(order):
-        if place >> k & 1:
-            seg ^= flip
-    return seg
+def holdings(nseg):
+    if nseg == 8:
+        return [0, 6, 2, 3], [0, 6, 4, 5]
+    held = []
+    for order in doublings(nseg):
+        flips = [0]
+        for flip in order:
+            flips = flips + [x ^ flip for x in flips]
+        held.append(flips)
+    return held
 
 
 def filter_body(
     nseg, held, flips, live_ref, edges_ref, halves, slots, first_ref, second_ref, turn_ref,
     sums, tops, powers, lefts, spectra, products, firsts, turneds, series,
 ):
-    orders = flip_orders(nseg)
+    evens, odds = holdings(nseg)
     my_bank = lax.axis_index("bank")
     my_seg = lax.axis_index("seg")
     core = my_seg & 1
@@ -87,7 +91,7 @@
         t = owner(my_bank, core, flips[q]) * tiles + k
         (mine, mine_at), (theirs, theirs_at) = halves[q]
         for z in range(low):
-            even, odd = reach(orders[0], z), reach(orders[1], z)
+            even, odd = evens[z], odds[z]
             own = my_seg ^ jnp.where(core == 0, even, odd)
             other = my_seg ^ 1 ^ jnp.where(core == 0, odd, even)
             for ref, at, seg in ((mine, mine_at, own), (theirs, theirs_at, other)):
@@ -237,7 +241,6 @@
     rows = FB // nseg
     low = nseg // 2
     first, second, coarse, turn = (jnp.asarray(x) for x in tables())
-    orders = flip_orders(nseg)
     smem = pl.BlockSpec(memory_space=pltpu.SMEM)
     vmem = pl.BlockSpec(memory_space=pltpu.VMEM)
 
@@ -314,25 +317,38 @@
 
     block = templates.reshape(tiles, 2, rows, FA)
     slots = []
-    for step in range(len(orders[0])):
-        found = swap(block, [(0, orders[c][step]) for c in range(2)])
-        if step < held:
-            slot = strain[step].reshape(2, 2, FB, FA)
-            found, slot, strain = lax.optimization_barrier((found, slot, strain))
-            slots.append(slot)
-        block = jnp.concatenate([block, found], axis=0)
-    for s in range(len(slots), held):
-        slots.append(strain[s].reshape(2, 2, FB, FA))
+
+    def slot_beside(found, strain):
+        slot = strain[len(slots)].reshape(2, 2, FB, FA)
+        found, slot, strain = lax.optimization_barrier((found, slot, strain))
+        slots.append(slot)
+        return found, strain
+
+    if nseg == 8:
+        pair = jnp.concatenate([block, swap(block, twin)], axis=0)
+        third = swap(block, ((0, 6), (0, 6)))
+        near = swap(pair, ((0, 2), (0, 4)))
+        near, strain = slot_beside(near, strain)
+        block = jnp.concatenate([block, third, near], axis=0)
+    else:
+        for even, odd in zip(*doublings(nseg)):
+            found = swap(block, ((0, even), (0, odd)))
+            if len(slots) < held:
+                found, strain = slot_beside(found, strain)
+            block = jnp.concatenate([block, found], axis=0)
     other = swap(block, twin)
-    side = swap(jnp.concatenate([block, other], axis=0), ((1, 0), (2, 0)))
+    one = swap(block, ((1, 0), (2, 0)))
+    two = swap(block, ((2, 0), (1, 0)))
+    while len(slots) < held:
+        slots.append(strain[len(slots)].reshape(2, 2, FB, FA))
     here = call([(0, 0)], [block, other], [((0, 0), (1, 0))])
-    side, here = lax.optimization_barrier((side, here))
-    corner = swap(side[: low * tiles], ((2, 0), (1, 0)))
-    far = swap(side, twin)
-    beside = call([(1, 2)], [side], [((0, 0), (0, low))])
+    one, two, here = lax.optimization_barrier((one, two, here))
+    others = swap(jnp.concatenate([one, two], axis=0), twin)
+    corner = swap(one, ((2, 0), (1, 0)))
+    beside = call([(1, 2)], [one, others], [((0, 0), (1, low))])
     corner, beside = lax.optimization_barrier((corner, beside))
     other_corner = swap(corner, twin)
-    across = call([(2, 1)], [far], [((0, low), (0, 0))])
+    across = call([(2, 1)], [two, others], [((0, 0), (1, 0))])
     other_corner, across = lax.optimization_barrier((other_corner, across))
     peak, snr, chi = call(
         [(3, 3)],

time: 30.4 us -> 29.5 us (0.970)
  starting transfers between devices: 12.6 us -> 10.7 us
  local copies, waits for them, and re-layouts: 1.54 us -> 2.42 us
    ppermute x7 -> x9, starting transfers between devices: 12.6 us -> 10.7 us  [swap(): return lax.ppermute(block, ('bank', 'seg'), route)]
    unnamed x14, local copies, waits for them, and re-layouts: 0.8 us -> 1.67 us
    ppermute x7 -> x9, waiting for transfers between devices: 5.7 us -> 5.84 us  [swap(): return lax.ppermute(block, ('bank', 'seg'), route)]
  transfers between devices with their start and end apart: 7 -> 9, of which waited for: 5 -> 5; matrix products, arithmetic and copies ran while one was open for 2% -> 3% of each run, Pallas kernels for 21% -> 21%
where the time goes in v4:
time: 29.5 us; the launch traced here: 29.2 us
  starting transfers between devices  10.7 us (36%)
  Pallas kernels  9.52 us (32%)
  waiting for transfers between devices  5.84 us (20%)
  local copies, waits for them, and re-layouts  2.42 us (8%)
  between operations  0.76 us (3%)
    ppermute x9, starting transfers between devices, swap(): return lax.ppermute(block, ('bank', 'seg'), route)  10.7 us
    pallas_call x4, Pallas kernels, call(): pl.pallas_call(run, in_specs=[smem, smem] + [vmem] * (len(inputs) - 2), o...  9.52 us
    ppermute x9, waiting for transfers between devices, swap(): return lax.ppermute(block, ('bank', 'seg'), route)  5.84 us
    unnamed x14, local copies, waits for them, and re-layouts  1.67 us
  transfers between devices with their start and end apart: 9, of which 5 were waited for; matrix products, arithmetic and copies ran while one was open for 3% of the time, Pallas kernels for 21%

profile of v4, /device:TPU:1, one launch (start us, length us, event | category | flops | bytes accessed | tf_op | source)
XLA Modules:
  0.0 29.2 jit_solution(4491173421682333446)
XLA Ops:
  0.6 0.8 %constant_dynamic-update-slice_fusion.2 = (bf16[4,2,32,256]{3,2,1,0:T(8,128)(2,1)S(1)}, bf16[1,2,32,256]{3,2,1,0:T(8,128)(2,1)S(1)}) fusion(bf16[1,2,32,256]{3,1,2,0:T(2,128)(2,1)} %bitcast.8), kind=kLoop, calls=%fused_computation.5 | loop fusion | bytes 98304
  1.4 0.1 collective-permute-start
  1.5 4.8 %collective-permute-start.2 = (bf16[1,2,32,256]{3,2,1,0:T(8,128)(2,1)S(1)}, bf16[1,2,32,256]{3,2,1,0:T(8,128)(2,1)S(1)}, u32[]{:S(2)}, u32[]{:S(2)}) collective-permute-start(bf16[1,2,32,256]{3,2,1,0:T(8,128)(2,1)S(1)} %get-tuple-element.60), channel_id=1, source_target_pairs={{0,6},{1,7},{2,4},{3,5},{4,2},{5,3},{6,0},{7,1},{8,14},{9,15},{10,... | collective-permute-start | bytes 98312 | tf_op jit(solution)/shard_map/ppermute | solution.py:253
  6.3 0.4 %reshape_squeeze.6.rest_0_ = bf16[2,2,256,256]{3,2,1,0:T(8,128)(2,1)S(1)} reshape(bf16[1,2,2,65536]{3,2,1,0:T(2,128)(2,1)S(1)} %slice-done) | data formatting | bytes 1048576 | tf_op jit(solution)/shard_map/reshape;squeeze | solution.py:322
  6.7 0.0 collective-permute-done
  6.7 0.1 collective-permute-start.1
  6.8 1.2 %collective-permute-done.2 = bf16[1,2,32,256]{3,2,1,0:T(8,128)(2,1)S(1)} collective-permute-done((bf16[1,2,32,256]{3,2,1,0:T(8,128)(2,1)S(1)}, bf16[1,2,32,256]{3,2,1,0:T(8,128)(2,1)S(1)}, u32[]{:S(2)}, u32[]{:S(2)}) %collective-permute-start.2) | collective-permute-done | bytes 32800 | tf_op jit(solution)/shard_map/ppermute | solution.py:253
  8.0 3.0 %collective-permute-done.1 = bf16[2,2,32,256]{3,2,1,0:T(8,128)(2,1)S(1)} collective-permute-done((bf16[2,2,32,256]{3,2,1,0:T(8,128)(2,1)S(1)}, bf16[2,2,32,256]{3,2,1,0:T(8,128)(2,1)S(1)}, u32[]{:S(2)}, u32[]{:S(2)}) %collective-permute-start.1) | collective-permute-done | bytes 65568 | tf_op jit(solution)/shard_map/ppermute | solution.py:253
  11.0 1.2 %collective-permute-start.5 = (bf16[4,2,32,256]{3,2,1,0:T(8,128)(2,1)S(1)}, bf16[4,2,32,256]{3,2,1,0:T(8,128)(2,1)S(1)}, u32[]{:S(2)}, u32[]{:S(2)}) collective-permute-start(bf16[4,2,32,256]{3,2,1,0:T(8,128)(2,1)S(1)} %constant_dynamic-update-slice_fusion.rest_2_), channel_id=1, source_target_pairs={{0,1},{1,0},{2,3},{3,2},{4,5},{5,4},{6,7},{7,6},{8,9},{9,8},{10,11... | collective-permute-start | bytes 393224 | tf_op jit(solution)/shard_map/ppermute | solution.py:253
  12.2 1.2 %collective-permute-start.3 = (bf16[4,2,32,256]{3,2,1,0:T(8,128)(2,1)S(1)}, bf16[4,2,32,256]{3,2,1,0:T(8,128)(2,1)S(1)}, u32[]{:S(2)}, u32[]{:S(2)}) collective-permute-start(bf16[4,2,32,256]{3,2,1,0:T(8,128)(2,1)S(1)} %constant_dynamic-update-slice_fusion.rest_2_), channel_id=1, source_target_pairs={{0,8},{1,17},{2,10},{3,19},{4,12},{5,21},{6,14},{7,23},{8,0},{9,25... | collective-permute-start | bytes 393224 | tf_op jit(solution)/shard_map/ppermute | solution.py:253
  13.4 1.2 %collective-permute-start.4 = (bf16[4,2,32,256]{3,2,1,0:T(8,128)(2,1)S(1)}, bf16[4,2,32,256]{3,2,1,0:T(8,128)(2,1)S(1)}, u32[]{:S(2)}, u32[]{:S(2)}) collective-permute-start(bf16[4,2,32,256]{3,2,1,0:T(8,128)(2,1)S(1)} %constant_dynamic-update-slice_fusion.rest_2_), channel_id=1, source_target_pairs={{0,16},{1,9},{2,18},{3,11},{4,20},{5,13},{6,22},{7,15},{8,24},{9,1... | collective-permute-start | bytes 393224 | tf_op jit(solution)/shard_map/ppermute | solution.py:253
  14.6 0.0 slice-done.1
  14.6 0.0 copy-start.1
  14.6 0.0 copy-start.2
  14.6 0.4 %reshape_squeeze.7.rest_1_ = bf16[2,2,256,256]{3,2,1,0:T(8,128)(2,1)S(1)} reshape(bf16[1,2,2,65536]{3,2,1,0:T(2,128)(2,1)S(1)} %slice-done.1) | data formatting | bytes 1048576 | tf_op jit(solution)/shard_map/reshape;squeeze | solution.py:343
  15.0 0.0 collective-permute-done.5.rest_3_
  15.0 0.5 %copy-done.3 = bf16[2,256,256]{2,1,0:T(8,128)(2,1)S(1)} copy-done((bf16[2,256,256]{2,1,0:T(8,128)(2,1)S(1)}, bf16[2,256,256]{2,1,0:T(8,128)(2,1)}, u32[]{:S(2)}) %copy-start.3) | copy-done | bytes 262168
  15.6 0.0 copy-done.5
  15.6 0.2 copy-done.1
  15.8 0.2 copy-done.2
  15.9 2.1 %shard_map.103 = (f32[64,512]{1,0:T(8,128)S(1)}, f32[2,16,128]{2,1,0:T(8,128)S(1)}, f32[1,16,128]{2,1,0:T(8,128)S(1)}) custom-call(s32[2]{0:T(128)S(1)} %copy-done.5, s32[4,15]{1,0:T(4,128)S(1)} %copy-done.4, bf16[512,512]{1,0:T(8,128)(2,1)S(1)} %copy-done.2, bf16[2,256,256]{2,1,0:T(8,128)(2,1)S(1)} %copy-done.3, f32[2,256,256]{2,1,0:T(8,128)S(1)} %copy-done.1, ...), custom_call_target="tpu_custom_call" | custom-call | flops 805306368 | bytes 1048576 | tf_op jit(solution)/shard_map/pallas_call | solution.py:306
  18.0 0.0 collective-permute-done.3.rest_2_
  18.0 0.2 collective-permute-done.4.rest_2_
  18.2 0.5 %collective-permute-start.7 = (bf16[8,2,32,256]{3,2,1,0:T(8,128)(2,1)S(1)}, bf16[8,2,32,256]{3,2,1,0:T(8,128)(2,1)S(1)}, u32[]{:S(2)}, u32[]{:S(2)}) collective-permute-start(bf16[8,2,32,256]{3,2,1,0:T(8,128)(2,1)S(1)} %pad_maximum_fusion), channel_id=1, source_target_pairs={{0,1},{1,0},{2,3},{3,2},{4,5},{5,4},{6,7},{7,6},{8,9},{9,8},{10,11... | collective-permute-start | bytes 786440 | tf_op jit(solution)/shard_map/ppermute | solution.py:253
  18.8 0.6 %collective-permute-start.6 = (bf16[4,2,32,256]{3,2,1,0:T(8,128)(2,1)S(1)}, bf16[4,2,32,256]{3,2,1,0:T(8,128)(2,1)S(1)}, u32[]{:S(2)}, u32[]{:S(2)}) collective-permute-start(bf16[4,2,32,256]{3,2,1,0:T(8,128)(2,1)S(1)} %collective-permute-done.3.rest_2_), channel_id=1, source_target_pairs={{0,16},{1,9},{2,18},{3,11},{4,20},{5,13},{6,22},{7,15},{8,24},{9,1... | collective-permute-start | bytes 393224 | tf_op jit(solution)/shard_map/ppermute | solution.py:253
  19.4 0.6 %collective-permute-done.7.rest_3_ = bf16[8,2,32,256]{3,2,1,0:T(8,128)(2,1)S(1)} collective-permute-done((bf16[8,2,32,256]{3,2,1,0:T(8,128)(2,1)S(1)}, bf16[8,2,32,256]{3,2,1,0:T(8,128)(2,1)S(1)}, u32[]{:S(2)}, u32[]{:S(2)}) %collective-permute-start.7) | collective-permute-done | bytes 262176 | tf_op jit(solution)/shard_map/ppermute | solution.py:253
  20.0 2.1 %shard_map.104 = (f32[64,512]{1,0:T(8,128)S(1)}, f32[2,16,128]{2,1,0:T(8,128)S(1)}, f32[1,16,128]{2,1,0:T(8,128)S(1)}) custom-call(s32[2]{0:T(128)S(1)} %copy-done.5, s32[4,15]{1,0:T(4,128)S(1)} %copy-done.4, bf16[512,512]{1,0:T(8,128)(2,1)S(1)} %copy-done.2, bf16[2,256,256]{2,1,0:T(8,128)(2,1)S(1)} %copy-done.3, f32[2,256,256]{2,1,0:T(8,128)S(1)} %copy-done.1, ...), custom_call_target="tpu_custom_call" | custom-call | flops 805306368 | bytes 1048576 | tf_op jit(solution)/shard_map/pallas_call | solution.py:306
  22.0 0.9 %collective-permute-done.6.rest_2_ = bf16[4,2,32,256]{3,2,1,0:T(8,128)(2,1)S(1)} collective-permute-done((bf16[4,2,32,256]{3,2,1,0:T(8,128)(2,1)S(1)}, bf16[4,2,32,256]{3,2,1,0:T(8,128)(2,1)S(1)}, u32[]{:S(2)}, u32[]{:S(2)}) %collective-permute-start.6) | collective-permute-done | bytes 131104 | tf_op jit(solution)/shard_map/ppermute | solution.py:253
  22.9 0.9 %collective-permute-start.8 = (bf16[4,2,32,256]{3,2,1,0:T(8,128)(2,1)S(1)}, bf16[4,2,32,256]{3,2,1,0:T(8,128)(2,1)S(1)}, u32[]{:S(2)}, u32[]{:S(2)}) collective-permute-start(bf16[4,2,32,256]{3,2,1,0:T(8,128)(2,1)S(1)} %collective-permute-done.6.rest_2_), channel_id=1, source_target_pairs={{0,1},{1,0},{2,3},{3,2},{4,5},{5,4},{6,7},{7,6},{8,9},{9,8},{10,11... | collective-permute-start | bytes 393224 | tf_op jit(solution)/shard_map/ppermute | solution.py:253
  23.8 2.1 %shard_map.105 = (f32[64,512]{1,0:T(8,128)S(1)}, f32[2,16,128]{2,1,0:T(8,128)S(1)}, f32[1,16,128]{2,1,0:T(8,128)S(1)}) custom-call(s32[2]{0:T(128)S(1)} %copy-done.5, s32[4,15]{1,0:T(4,128)S(1)} %copy-done.4, bf16[512,512]{1,0:T(8,128)(2,1)S(1)} %copy-done.2, bf16[2,256,256]{2,1,0:T(8,128)(2,1)S(1)} %copy-done.3, f32[2,256,256]{2,1,0:T(8,128)S(1)} %copy-done.1, ...), custom_call_target="tpu_custom_call" | custom-call | flops 805306368 | bytes 1048576 | tf_op jit(solution)/shard_map/pallas_call | solution.py:306
  25.9 0.0 collective-permute-done.8.rest_3_
  25.9 3.3 %shard_map.106 = (f32[2,4]{1,0:T(2,128)}, f32[4,2,256]{2,1,0:T(2,128)}, f32[4,2,256]{2,1,0:T(2,128)}) custom-call(s32[2]{0:T(128)S(1)} %copy-done.5, s32[4,15]{1,0:T(4,128)S(1)} %copy-done.4, bf16[512,512]{1,0:T(8,128)(2,1)S(1)} %copy-done.2, bf16[2,256,256]{2,1,0:T(8,128)(2,1)S(1)} %copy-done.3, f32[2,256,256]{2,1,0:T(8,128)S(1)} %copy-done.1, ...), custom_call_target="tpu_custom_call" | custom-call | flops 805306368 | bytes 1048576 | tf_op jit(solution)/shard_map/pallas_call | solution.py:306
  (13 shorter events, 0.1 us)
Async XLA Ops:
  1.4 4.9 %slice-start = ((bf16[2,2,2,65536]{3,2,1,0:T(2,128)(2,1)}), bf16[1,2,2,65536]{3,2,1,0:T(2,128)(2,1)S(1)}, s32[]{:S(2)}) async-start(bf16[2,2,2,65536]{3,2,1,0:T(2,128)(2,1)} %param.8), calls=%async_computation | async-start | bytes 1048576 | tf_op jit(solution)/shard_map/slice | solution.py:322
  1.4 5.3 %collective-permute-start = (bf16[1,2,32,256]{3,2,1,0:T(8,128)(2,1)S(1)}, bf16[1,2,32,256]{3,2,1,0:T(8,128)(2,1)S(1)}, u32[]{:S(2)}, u32[]{:S(2)}) collective-permute-start(bf16[1,2,32,256]{3,2,1,0:T(8,128)(2,1)S(1)} %get-tuple-element.60), channel_id=1, source_target_pairs={{0,1},{1,0},{2,3},{3,2},{4,5},{5,4},{6,7},{7,6},{8,9},{9,8},{10,11... | collective-permute-start | bytes 98312 | tf_op jit(solution)/shard_map/ppermute | solution.py:253
  1.5 6.5 %collective-permute-start.2 = (bf16[1,2,32,256]{3,2,1,0:T(8,128)(2,1)S(1)}, bf16[1,2,32,256]{3,2,1,0:T(8,128)(2,1)S(1)}, u32[]{:S(2)}, u32[]{:S(2)}) collective-permute-start(bf16[1,2,32,256]{3,2,1,0:T(8,128)(2,1)S(1)} %get-tuple-element.60), channel_id=1, source_target_pairs={{0,6},{1,7},{2,4},{3,5},{4,2},{5,3},{6,0},{7,1},{8,14},{9,15},{10,... | collective-permute-start | bytes 98312 | tf_op jit(solution)/shard_map/ppermute | solution.py:253
  6.7 4.3 %collective-permute-start.1 = (bf16[2,2,32,256]{3,2,1,0:T(8,128)(2,1)S(1)}, bf16[2,2,32,256]{3,2,1,0:T(8,128)(2,1)S(1)}, u32[]{:S(2)}, u32[]{:S(2)}) collective-permute-start(bf16[2,2,32,256]{3,2,1,0:T(8,128)(2,1)S(1)} %pad_maximum_fusion.1), channel_id=1, source_target_pairs={{0,2},{1,5},{2,0},{3,7},{4,6},{5,1},{6,4},{7,3},{8,10},{9,13},{10,... | collective-permute-start | bytes 196616 | tf_op jit(solution)/shard_map/ppermute | solution.py:253
  11.0 3.6 %slice-start.1 = ((bf16[2,2,2,65536]{3,2,1,0:T(2,128)(2,1)}), bf16[1,2,2,65536]{3,2,1,0:T(2,128)(2,1)S(1)}, s32[]{:S(2)}) async-start(bf16[2,2,2,65536]{3,2,1,0:T(2,128)(2,1)} %param.8), calls=%async_computation.1 | async-start | bytes 1048576 | tf_op jit(solution)/shard_map/slice | solution.py:343
  11.0 4.0 %collective-permute-start.5 = (bf16[4,2,32,256]{3,2,1,0:T(8,128)(2,1)S(1)}, bf16[4,2,32,256]{3,2,1,0:T(8,128)(2,1)S(1)}, u32[]{:S(2)}, u32[]{:S(2)}) collective-permute-start(bf16[4,2,32,256]{3,2,1,0:T(8,128)(2,1)S(1)} %constant_dynamic-update-slice_fusion.rest_2_), channel_id=1, source_target_pairs={{0,1},{1,0},{2,3},{3,2},{4,5},{5,4},{6,7},{7,6},{8,9},{9,8},{10,11... | collective-permute-start | bytes 393224 | tf_op jit(solution)/shard_map/ppermute | solution.py:253
  12.2 5.9 %collective-permute-start.3 = (bf16[4,2,32,256]{3,2,1,0:T(8,128)(2,1)S(1)}, bf16[4,2,32,256]{3,2,1,0:T(8,128)(2,1)S(1)}, u32[]{:S(2)}, u32[]{:S(2)}) collective-permute-start(bf16[4,2,32,256]{3,2,1,0:T(8,128)(2,1)S(1)} %constant_dynamic-update-slice_fusion.rest_2_), channel_id=1, source_target_pairs={{0,8},{1,17},{2,10},{3,19},{4,12},{5,21},{6,14},{7,23},{8,0},{9,25... | collective-permute-start | bytes 393224 | tf_op jit(solution)/shard_map/ppermute | solution.py:253
  13.4 4.8 %collective-permute-start.4 = (bf16[4,2,32,256]{3,2,1,0:T(8,128)(2,1)S(1)}, bf16[4,2,32,256]{3,2,1,0:T(8,128)(2,1)S(1)}, u32[]{:S(2)}, u32[]{:S(2)}) collective-permute-start(bf16[4,2,32,256]{3,2,1,0:T(8,128)(2,1)S(1)} %constant_dynamic-update-slice_fusion.rest_2_), channel_id=1, source_target_pairs={{0,16},{1,9},{2,18},{3,11},{4,20},{5,13},{6,22},{7,15},{8,24},{9,1... | collective-permute-start | bytes 393224 | tf_op jit(solution)/shard_map/ppermute | solution.py:253
  14.6 0.9 %copy-start.3 = (bf16[2,256,256]{2,1,0:T(8,128)(2,1)S(1)}, bf16[2,256,256]{2,1,0:T(8,128)(2,1)}, u32[]{:S(2)}) copy-start(bf16[2,256,256]{2,1,0:T(8,128)(2,1)} %constant.9.clone.second_ref) | copy-start | bytes 786436
  14.6 1.0 %copy-start.4 = (s32[4,15]{1,0:T(4,128)S(1)}, s32[4,15]{1,0:T(4,128)}, u32[]{:S(2)}) copy-start(s32[4,15]{1,0:T(4,128)} %edges_ref.7) | copy-start | bytes 724
  14.6 1.0 %copy-start.5 = (s32[2]{0:T(128)S(1)}, s32[2]{0:T(128)}, u32[]{:S(2)}) copy-start(s32[2]{0:T(128)} %live_ref.7) | copy-start | bytes 28
  14.6 1.1 %copy-start.1 = (f32[2,256,256]{2,1,0:T(8,128)S(1)}, f32[2,256,256]{2,1,0:T(8,128)}, u32[]{:S(2)}) copy-start(f32[2,256,256]{2,1,0:T(8,128)} %constant.11.clone.turn_ref) | copy-start | bytes 1572868
  14.6 1.3 %copy-start.2 = (bf16[512,512]{1,0:T(8,128)(2,1)S(1)}, bf16[512,512]{1,0:T(8,128)(2,1)}, u32[]{:S(2)}) copy-start(bf16[512,512]{1,0:T(8,128)(2,1)} %constant.8.clone.first_ref) | copy-start | bytes 1572868
  18.2 1.7 %collective-permute-start.7 = (bf16[8,2,32,256]{3,2,1,0:T(8,128)(2,1)S(1)}, bf16[8,2,32,256]{3,2,1,0:T(8,128)(2,1)S(1)}, u32[]{:S(2)}, u32[]{:S(2)}) collective-permute-start(bf16[8,2,32,256]{3,2,1,0:T(8,128)(2,1)S(1)} %pad_maximum_fusion), channel_id=1, source_target_pairs={{0,1},{1,0},{2,3},{3,2},{4,5},{5,4},{6,7},{7,6},{8,9},{9,8},{10,11... | collective-permute-start | bytes 786440 | tf_op jit(solution)/shard_map/ppermute | solution.py:253
  18.8 4.1 %collective-permute-start.6 = (bf16[4,2,32,256]{3,2,1,0:T(8,128)(2,1)S(1)}, bf16[4,2,32,256]{3,2,1,0:T(8,128)(2,1)S(1)}, u32[]{:S(2)}, u32[]{:S(2)}) collective-permute-start(bf16[4,2,32,256]{3,2,1,0:T(8,128)(2,1)S(1)} %collective-permute-done.3.rest_2_), channel_id=1, source_target_pairs={{0,16},{1,9},{2,18},{3,11},{4,20},{5,13},{6,22},{7,15},{8,24},{9,1... | collective-permute-start | bytes 393224 | tf_op jit(solution)/shard_map/ppermute | solution.py:253
  22.9 3.0 %copy-start = (bf16[2,512,512]{2,1,0:T(8,128)(2,1)S(1)}, bf16[2,512,512]{2,1,0:T(8,128)(2,1)}, u32[]{:S(2)}) copy-start(bf16[2,512,512]{2,1,0:T(8,128)(2,1)} %constant.10.clone.rest_4_) | copy-start | bytes 3145732
  22.9 3.0 %collective-permute-start.8 = (bf16[4,2,32,256]{3,2,1,0:T(8,128)(2,1)S(1)}, bf16[4,2,32,256]{3,2,1,0:T(8,128)(2,1)S(1)}, u32[]{:S(2)}, u32[]{:S(2)}) collective-permute-start(bf16[4,2,32,256]{3,2,1,0:T(8,128)(2,1)S(1)} %collective-permute-done.6.rest_2_), channel_id=1, source_target_pairs={{0,1},{1,0},{2,3},{3,2},{4,5},{5,4},{6,7},{7,6},{8,9},{9,8},{10,11... | collective-permute-start | bytes 393224 | tf_op jit(solution)/shard_map/ppermute | solution.py:253

commit v5 on v4

--- a/solution.py
+++ b/solution.py
@@ -61,7 +61,7 @@
 
 def holdings(nseg):
     if nseg == 8:
-        return [0, 6, 2, 3], [0, 6, 4, 5]
+        return [0, 6, 4, 2], [0, 6, 4, 2]
     held = []
     for order in doublings(nseg):
         flips = [0]
@@ -190,11 +190,11 @@
 
 
 def statistics(
-    held, flips, live_ref, coarse_ref, groups, peak_ref, snr_ref, chi_ref, gathered, parts
+    held, flips, live_ref, coarse_ref, groups, before, peak_ref, snr_ref, chi_ref, gathered, parts
 ):
     my_bank = lax.axis_index("bank")
     core = lax.axis_index("seg") & 1
-    tiles = peak_ref.shape[1] // len(flips)
+    tiles = groups[0][2].shape[0]
     at = 0
     for sums, _, _ in groups:
         gathered[at : at + sums.shape[0]] = sums[...]
@@ -202,6 +202,10 @@
     upper, lower = split(gathered[...])
     parts[...] = dot(upper, coarse_ref[0]) + dot(lower, coarse_ref[0]) + dot(upper, coarse_ref[1])
     peaks = jnp.zeros(peak_ref.shape, F32)
+    if before:
+        peaks = before[0][...]
+        snr_ref[...] = before[1][...]
+        chi_ref[...] = before[2][...]
     slot_at = lax.broadcasted_iota(jnp.int32, peak_ref.shape, 0)
     tile_at = lax.broadcasted_iota(jnp.int32, peak_ref.shape, 1)
     n = 0
@@ -254,7 +258,7 @@
 
     twin = ((0, 1), (0, 1))
 
-    def call(flips, arrays, halves, earlier=None):
+    def call(flips, arrays, halves, earlier=None, before=()):
         fresh = len(flips) * tiles
         made = [
             jax.ShapeDtypeStruct((fresh * held * 2 * BINS, 2 * FA), F32),
@@ -281,6 +285,7 @@
                 coarse_ref, rest = rest[0], rest[1:]
                 groups = [rest[i : i + 3] for i in range(0, 3 * len(earlier[1]), 3)]
                 rest = rest[3 * len(groups) :]
+                older, rest = rest[: len(before)], rest[len(before) :]
                 outs, results, scratches = rest[:3], rest[3:6], rest[8:]
             filter_body(
                 nseg, held, flips, live_ref, edges_ref, pairs, slots,
@@ -289,19 +294,20 @@
             if earlier is not None:
                 every = earlier[0] + flips
                 groups = groups + [results]
-                statistics(held, every, live_ref, coarse_ref, groups, *outs, *rest[6:8])
+                statistics(held, every, live_ref, coarse_ref, groups, older, *outs, *rest[6:8])
 
         inputs = [live_flags, bin_edges, first, second, turn, *slots, *arrays]
         if earlier is None:
             shapes = made
         else:
-            inputs += [coarse] + [x for group in earlier[1] for x in group]
+            inputs += [coarse] + [x for group in earlier[1] for x in group] + list(before)
             shapes = [
                 jax.ShapeDtypeStruct((held, total), F32),
                 jax.ShapeDtypeStruct((total, held, FB), F32),
                 jax.ShapeDtypeStruct((total, held, FB), F32),
             ]
-            full = pltpu.VMEM((total * held * 2 * BINS, 2 * FA), F32)
+            every = (len(earlier[1]) + 1) * fresh
+            full = pltpu.VMEM((every * held * 2 * BINS, 2 * FA), F32)
             scratch = [pltpu.VMEM(x.shape, x.dtype) for x in made] + [full, full] + scratch
         return pl.pallas_call(
             run,
@@ -315,7 +321,7 @@
             ),
         )(*inputs)
 
-    block = templates.reshape(tiles, 2, rows, FA)
+    block = templates if nseg == 8 else templates.reshape(tiles, 2, rows, FA)
     slots = []
 
     def slot_beside(found, strain):
@@ -325,11 +331,10 @@
         return found, strain
 
     if nseg == 8:
-        pair = jnp.concatenate([block, swap(block, twin)], axis=0)
-        third = swap(block, ((0, 6), (0, 6)))
-        near = swap(pair, ((0, 2), (0, 4)))
+        third, second_, near = (swap(block, ((0, x), (0, x))) for x in (6, 4, 2))
+        third, strain = slot_beside(third, strain)
         near, strain = slot_beside(near, strain)
-        block = jnp.concatenate([block, third, near], axis=0)
+        block = jnp.concatenate([block, third, second_, near], axis=0).reshape(low * tiles, 2, rows, FA)
     else:
         for even, odd in zip(*doublings(nseg)):
             found = swap(block, ((0, even), (0, odd)))
@@ -345,7 +350,9 @@
     one, two, here = lax.optimization_barrier((one, two, here))
     others = swap(jnp.concatenate([one, two], axis=0), twin)
     corner = swap(one, ((2, 0), (1, 0)))
-    beside = call([(1, 2)], [one, others], [((0, 0), (1, low))])
+    beside = call(
+        [(1, 2)], [one, others], [((0, 0), (1, low))], ([(0, 0)], [here])
+    )
     corner, beside = lax.optimization_barrier((corner, beside))
     other_corner = swap(corner, twin)
     across = call([(2, 1)], [two, others], [((0, 0), (1, 0))])
@@ -354,7 +361,8 @@
         [(3, 3)],
         [corner, other_corner],
         [((0, 0), (1, 0))],
-        ([(0, 0), (1, 2), (2, 1)], [here, beside, across]),
+        ([(2, 1)], [across]),
+        beside,
     )
     return peak.T, snr, chi
 

time: 29.5 us -> 28.3 us (0.959)
  local copies, waits for them, and re-layouts: 2.42 us -> 1.1 us
  waiting for transfers between devices: 5.84 us -> 5.13 us
  starting transfers between devices: 10.7 us -> 11.4 us
    unnamed x14, local copies, waits for them, and re-layouts: 1.67 us -> 0.04 us
    ppermute x9, starting transfers between devices: 10.7 us -> 11.4 us  [swap(): return lax.ppermute(block, ('bank', 'seg'), route)]
    ppermute x9, waiting for transfers between devices: 5.84 us -> 5.13 us  [swap(): return lax.ppermute(block, ('bank', 'seg'), route)]
    another operation x1 -> x0, local copies, waits for them, and re-layouts: 0.38 us -> none  [on_device(): slots.append(strain[len(slots)].reshape(2, 2, FB, FA))]
    another operation x1 -> x2, local copies, waits for them, and re-layouts: 0.36 us -> 0.71 us  [slot_beside(): slot = strain[len(slots)].reshape(2, 2, FB, FA)]
  transfers between devices with their start and end apart: 9 -> 9, of which waited for: 5 -> 6; matrix products, arithmetic and copies ran while one was open for 3% -> 3% of each run, Pallas kernels for 21% -> 23%
where the time goes in v5:
time: 28.3 us; the launch traced here: 28.1 us
  starting transfers between devices  11.4 us (40%)
  Pallas kernels  9.49 us (34%)
  waiting for transfers between devices  5.13 us (18%)
  local copies, waits for them, and re-layouts  1.1 us (4%)
  between operations  0.78 us (3%)
    ppermute x9, starting transfers between devices, swap(): return lax.ppermute(block, ('bank', 'seg'), route)  11.4 us
    pallas_call x4, Pallas kernels, call(): pl.pallas_call(run, in_specs=[smem, smem] + [vmem] * (len(inputs) - 2), o...  9.49 us
    ppermute x9, waiting for transfers between devices, swap(): return lax.ppermute(block, ('bank', 'seg'), route)  5.13 us
    another operation x2, local copies, waits for them, and re-layouts, slot_beside(): slot = strain[len(slots)].reshape(2, 2, FB, FA)  0.71 us
  transfers between devices with their start and end apart: 9, of which 6 were waited for; matrix products, arithmetic and copies ran while one was open for 3% of the time, Pallas kernels for 23%

profile of v5, /device:TPU:1, one launch (start us, length us, event | category | flops | bytes accessed | tf_op | source)
XLA Modules:
  0.0 28.1 jit_solution(6708507278307842540)
XLA Ops:
  0.6 0.0 slice-start
  0.6 4.2 %collective-permute-start = (bf16[1,2,8192]{2,1,0:T(2,128)(2,1)}, bf16[1,2,8192]{2,1,0:T(2,128)(2,1)S(1)}, u32[]{:S(2)}, u32[]{:S(2)}) collective-permute-start(bf16[1,2,8192]{2,1,0:T(2,128)(2,1)} %param.9), channel_id=1, source_target_pairs={{0,6},{1,7},{2,4},{3,5},{4,2},{5,3},{6,0},{7,1},{8,14},{9,15},{10,... | collective-permute-start | bytes 98312 | tf_op jit(solution)/shard_map/ppermute | solution.py:257
  4.9 0.0 collective-permute-start.1
  4.9 0.4 %collective-permute-start.2 = (bf16[1,2,8192]{2,1,0:T(2,128)(2,1)}, bf16[1,2,8192]{2,1,0:T(2,128)(2,1)S(1)}, u32[]{:S(2)}, u32[]{:S(2)}) collective-permute-start(bf16[1,2,8192]{2,1,0:T(2,128)(2,1)} %param.9), channel_id=1, source_target_pairs={{0,4},{1,5},{2,6},{3,7},{4,0},{5,1},{6,2},{7,3},{8,12},{9,13},{10,... | collective-permute-start | bytes 98312 | tf_op jit(solution)/shard_map/ppermute | solution.py:257
  5.2 0.4 %reshape_squeeze.6.rest_0_ = bf16[2,2,256,256]{3,2,1,0:T(8,128)(2,1)S(1)} reshape(bf16[1,2,2,65536]{3,2,1,0:T(2,128)(2,1)S(1)} %slice-done) | data formatting | bytes 1048576 | tf_op jit(solution)/shard_map/reshape;squeeze | solution.py:328
  5.6 0.0 slice-start.1
  5.6 0.8 %collective-permute-done = bf16[1,2,8192]{2,1,0:T(2,128)(2,1)S(1)} collective-permute-done((bf16[1,2,8192]{2,1,0:T(2,128)(2,1)}, bf16[1,2,8192]{2,1,0:T(2,128)(2,1)S(1)}, u32[]{:S(2)}, u32[]{:S(2)}) %collective-permute-start) | collective-permute-done | bytes 32800 | tf_op jit(solution)/shard_map/ppermute | solution.py:257
  6.4 0.3 slice-done.1
  6.6 0.4 %reshape_squeeze.7.rest_1_ = bf16[2,2,256,256]{3,2,1,0:T(8,128)(2,1)S(1)} reshape(bf16[1,2,2,65536]{3,2,1,0:T(2,128)(2,1)S(1)} %slice-done.1) | data formatting | bytes 1048576 | tf_op jit(solution)/shard_map/reshape;squeeze | solution.py:328
  7.0 0.0 copy-start.3
  7.0 0.8 %collective-permute-done.1 = bf16[1,2,8192]{2,1,0:T(2,128)(2,1)S(1)} collective-permute-done((bf16[1,2,8192]{2,1,0:T(2,128)(2,1)}, bf16[1,2,8192]{2,1,0:T(2,128)(2,1)S(1)}, u32[]{:S(2)}, u32[]{:S(2)}) %collective-permute-start.1) | collective-permute-done | bytes 32800 | tf_op jit(solution)/shard_map/ppermute | solution.py:257
  7.8 0.9 %collective-permute-done.2 = bf16[1,2,8192]{2,1,0:T(2,128)(2,1)S(1)} collective-permute-done((bf16[1,2,8192]{2,1,0:T(2,128)(2,1)}, bf16[1,2,8192]{2,1,0:T(2,128)(2,1)S(1)}, u32[]{:S(2)}, u32[]{:S(2)}) %collective-permute-start.2) | collective-permute-done | bytes 32800 | tf_op jit(solution)/shard_map/ppermute | solution.py:257
  8.7 0.2 pad_maximum_fusion.1
  9.0 0.0 copy-start.4
  9.0 0.0 copy-start.5
  9.0 0.1 reshape.9.rest_2_
  9.1 0.0 copy-start
  9.1 2.3 %collective-permute-start.5 = (bf16[4,2,32,256]{3,2,1,0:T(8,128)(2,1)S(1)}, bf16[4,2,32,256]{3,2,1,0:T(8,128)(2,1)S(1)}, u32[]{:S(2)}, u32[]{:S(2)}) collective-permute-start(bf16[4,2,32,256]{3,2,1,0:T(8,128)(2,1)S(1)} %reshape.9.rest_2_), channel_id=1, source_target_pairs={{0,1},{1,0},{2,3},{3,2},{4,5},{5,4},{6,7},{7,6},{8,9},{9,8},{10,11... | collective-permute-start | bytes 393224 | tf_op jit(solution)/shard_map/ppermute | solution.py:257
  11.4 1.2 %collective-permute-start.3 = (bf16[4,2,32,256]{3,2,1,0:T(8,128)(2,1)S(1)}, bf16[4,2,32,256]{3,2,1,0:T(8,128)(2,1)S(1)}, u32[]{:S(2)}, u32[]{:S(2)}) collective-permute-start(bf16[4,2,32,256]{3,2,1,0:T(8,128)(2,1)S(1)} %reshape.9.rest_2_), channel_id=1, source_target_pairs={{0,8},{1,17},{2,10},{3,19},{4,12},{5,21},{6,14},{7,23},{8,0},{9,25... | collective-permute-start | bytes 393224 | tf_op jit(solution)/shard_map/ppermute | solution.py:257
  12.6 1.2 %collective-permute-start.4 = (bf16[4,2,32,256]{3,2,1,0:T(8,128)(2,1)S(1)}, bf16[4,2,32,256]{3,2,1,0:T(8,128)(2,1)S(1)}, u32[]{:S(2)}, u32[]{:S(2)}) collective-permute-start(bf16[4,2,32,256]{3,2,1,0:T(8,128)(2,1)S(1)} %reshape.9.rest_2_), channel_id=1, source_target_pairs={{0,16},{1,9},{2,18},{3,11},{4,20},{5,13},{6,22},{7,15},{8,24},{9,1... | collective-permute-start | bytes 393224 | tf_op jit(solution)/shard_map/ppermute | solution.py:257
  13.8 0.0 collective-permute-done.5.rest_3_
  13.9 2.1 %shard_map.103 = (f32[64,512]{1,0:T(8,128)S(1)}, f32[2,16,128]{2,1,0:T(8,128)S(1)}, f32[1,16,128]{2,1,0:T(8,128)S(1)}) custom-call(s32[2]{0:T(128)S(1)} %copy-done.5, s32[4,15]{1,0:T(4,128)S(1)} %copy-done.4, bf16[512,512]{1,0:T(8,128)(2,1)S(1)} %copy-done.2, bf16[2,256,256]{2,1,0:T(8,128)(2,1)S(1)} %copy-done.3, f32[2,256,256]{2,1,0:T(8,128)S(1)} %copy-done.1, ...), custom_call_target="tpu_custom_call" | custom-call | flops 805306368 | bytes 1048576 | tf_op jit(solution)/shard_map/pallas_call | solution.py:312
  16.0 1.5 %collective-permute-done.4.rest_2_ = bf16[4,2,32,256]{3,2,1,0:T(8,128)(2,1)S(1)} collective-permute-done((bf16[4,2,32,256]{3,2,1,0:T(8,128)(2,1)S(1)}, bf16[4,2,32,256]{3,2,1,0:T(8,128)(2,1)S(1)}, u32[]{:S(2)}, u32[]{:S(2)}) %collective-permute-start.4) | collective-permute-done | bytes 131104 | tf_op jit(solution)/shard_map/ppermute | solution.py:257
  17.5 0.5 %collective-permute-start.7 = (bf16[8,2,32,256]{3,2,1,0:T(8,128)(2,1)S(1)}, bf16[8,2,32,256]{3,2,1,0:T(8,128)(2,1)S(1)}, u32[]{:S(2)}, u32[]{:S(2)}) collective-permute-start(bf16[8,2,32,256]{3,2,1,0:T(8,128)(2,1)S(1)} %pad_maximum_fusion), channel_id=1, source_target_pairs={{0,1},{1,0},{2,3},{3,2},{4,5},{5,4},{6,7},{7,6},{8,9},{9,8},{10,11... | collective-permute-start | bytes 786440 | tf_op jit(solution)/shard_map/ppermute | solution.py:257
  18.0 0.6 %collective-permute-start.6 = (bf16[4,2,32,256]{3,2,1,0:T(8,128)(2,1)S(1)}, bf16[4,2,32,256]{3,2,1,0:T(8,128)(2,1)S(1)}, u32[]{:S(2)}, u32[]{:S(2)}) collective-permute-start(bf16[4,2,32,256]{3,2,1,0:T(8,128)(2,1)S(1)} %collective-permute-done.3.rest_2_), channel_id=1, source_target_pairs={{0,16},{1,9},{2,18},{3,11},{4,20},{5,13},{6,22},{7,15},{8,24},{9,1... | collective-permute-start | bytes 393224 | tf_op jit(solution)/shard_map/ppermute | solution.py:257
  18.6 0.6 %collective-permute-done.7.rest_3_ = bf16[8,2,32,256]{3,2,1,0:T(8,128)(2,1)S(1)} collective-permute-done((bf16[8,2,32,256]{3,2,1,0:T(8,128)(2,1)S(1)}, bf16[8,2,32,256]{3,2,1,0:T(8,128)(2,1)S(1)}, u32[]{:S(2)}, u32[]{:S(2)}) %collective-permute-start.7) | collective-permute-done | bytes 262176 | tf_op jit(solution)/shard_map/ppermute | solution.py:257
  19.2 2.4 %shard_map.104 = (f32[2,4]{1,0:T(2,128)S(1)}, f32[4,2,256]{2,1,0:T(2,128)S(1)}, f32[4,2,256]{2,1,0:T(2,128)S(1)}) custom-call(s32[2]{0:T(128)S(1)} %copy-done.5, s32[4,15]{1,0:T(4,128)S(1)} %copy-done.4, bf16[512,512]{1,0:T(8,128)(2,1)S(1)} %copy-done.2, bf16[2,256,256]{2,1,0:T(8,128)(2,1)S(1)} %copy-done.3, f32[2,256,256]{2,1,0:T(8,128)S(1)} %copy-done.1, ...), custom_call_target="tpu_custom_call" | custom-call | flops 805306368 | bytes 1048576 | tf_op jit(solution)/shard_map/pallas_call | solution.py:312
  21.6 0.6 %collective-permute-done.6.rest_2_ = bf16[4,2,32,256]{3,2,1,0:T(8,128)(2,1)S(1)} collective-permute-done((bf16[4,2,32,256]{3,2,1,0:T(8,128)(2,1)S(1)}, bf16[4,2,32,256]{3,2,1,0:T(8,128)(2,1)S(1)}, u32[]{:S(2)}, u32[]{:S(2)}) %collective-permute-start.6) | collective-permute-done | bytes 131104 | tf_op jit(solution)/shard_map/ppermute | solution.py:257
  22.1 0.9 %collective-permute-start.8 = (bf16[4,2,32,256]{3,2,1,0:T(8,128)(2,1)S(1)}, bf16[4,2,32,256]{3,2,1,0:T(8,128)(2,1)S(1)}, u32[]{:S(2)}, u32[]{:S(2)}) collective-permute-start(bf16[4,2,32,256]{3,2,1,0:T(8,128)(2,1)S(1)} %collective-permute-done.6.rest_2_), channel_id=1, source_target_pairs={{0,1},{1,0},{2,3},{3,2},{4,5},{5,4},{6,7},{7,6},{8,9},{9,8},{10,11... | collective-permute-start | bytes 393224 | tf_op jit(solution)/shard_map/ppermute | solution.py:257
  23.1 2.1 %shard_map.105 = (f32[64,512]{1,0:T(8,128)S(1)}, f32[2,16,128]{2,1,0:T(8,128)S(1)}, f32[1,16,128]{2,1,0:T(8,128)S(1)}) custom-call(s32[2]{0:T(128)S(1)} %copy-done.5, s32[4,15]{1,0:T(4,128)S(1)} %copy-done.4, bf16[512,512]{1,0:T(8,128)(2,1)S(1)} %copy-done.2, bf16[2,256,256]{2,1,0:T(8,128)(2,1)S(1)} %copy-done.3, f32[2,256,256]{2,1,0:T(8,128)S(1)} %copy-done.1, ...), custom_call_target="tpu_custom_call" | custom-call | flops 805306368 | bytes 1048576 | tf_op jit(solution)/shard_map/pallas_call | solution.py:312
  25.1 0.0 collective-permute-done.8.rest_3_
  25.2 3.0 %shard_map.106 = (f32[2,4]{1,0:T(2,128)}, f32[4,2,256]{2,1,0:T(2,128)}, f32[4,2,256]{2,1,0:T(2,128)}) custom-call(s32[2]{0:T(128)S(1)} %copy-done.5, s32[4,15]{1,0:T(4,128)S(1)} %copy-done.4, bf16[512,512]{1,0:T(8,128)(2,1)S(1)} %copy-done.2, bf16[2,256,256]{2,1,0:T(8,128)(2,1)S(1)} %copy-done.3, f32[2,256,256]{2,1,0:T(8,128)S(1)} %copy-done.1, ...), custom_call_target="tpu_custom_call" | custom-call | flops 805306368 | bytes 1048576 | tf_op jit(solution)/shard_map/pallas_call | solution.py:312
  (13 shorter events, 0.0 us)
Async XLA Ops:
  0.6 4.6 %slice-start = ((bf16[2,2,2,65536]{3,2,1,0:T(2,128)(2,1)}), bf16[1,2,2,65536]{3,2,1,0:T(2,128)(2,1)S(1)}, s32[]{:S(2)}) async-start(bf16[2,2,2,65536]{3,2,1,0:T(2,128)(2,1)} %param.8), calls=%async_computation | async-start | bytes 1048576 | tf_op jit(solution)/shard_map/slice | solution.py:328
  0.6 5.7 %collective-permute-start = (bf16[1,2,8192]{2,1,0:T(2,128)(2,1)}, bf16[1,2,8192]{2,1,0:T(2,128)(2,1)S(1)}, u32[]{:S(2)}, u32[]{:S(2)}) collective-permute-start(bf16[1,2,8192]{2,1,0:T(2,128)(2,1)} %param.9), channel_id=1, source_target_pairs={{0,6},{1,7},{2,4},{3,5},{4,2},{5,3},{6,0},{7,1},{8,14},{9,15},{10,... | collective-permute-start | bytes 98312 | tf_op jit(solution)/shard_map/ppermute | solution.py:257
  4.9 3.0 %collective-permute-start.1 = (bf16[1,2,8192]{2,1,0:T(2,128)(2,1)}, bf16[1,2,8192]{2,1,0:T(2,128)(2,1)S(1)}, u32[]{:S(2)}, u32[]{:S(2)}) collective-permute-start(bf16[1,2,8192]{2,1,0:T(2,128)(2,1)} %param.9), channel_id=1, source_target_pairs={{0,2},{1,3},{2,0},{3,1},{4,6},{5,7},{6,4},{7,5},{8,10},{9,11},{10,... | collective-permute-start | bytes 98312 | tf_op jit(solution)/shard_map/ppermute | solution.py:257
  4.9 3.9 %collective-permute-start.2 = (bf16[1,2,8192]{2,1,0:T(2,128)(2,1)}, bf16[1,2,8192]{2,1,0:T(2,128)(2,1)S(1)}, u32[]{:S(2)}, u32[]{:S(2)}) collective-permute-start(bf16[1,2,8192]{2,1,0:T(2,128)(2,1)} %param.9), channel_id=1, source_target_pairs={{0,4},{1,5},{2,6},{3,7},{4,0},{5,1},{6,2},{7,3},{8,12},{9,13},{10,... | collective-permute-start | bytes 98312 | tf_op jit(solution)/shard_map/ppermute | solution.py:257
  5.6 1.0 %slice-start.1 = ((bf16[2,2,2,65536]{3,2,1,0:T(2,128)(2,1)}), bf16[1,2,2,65536]{3,2,1,0:T(2,128)(2,1)S(1)}, s32[]{:S(2)}) async-start(bf16[2,2,2,65536]{3,2,1,0:T(2,128)(2,1)} %param.8), calls=%async_computation.1 | async-start | bytes 1048576 | tf_op jit(solution)/shard_map/slice | solution.py:328
  6.4 2.4 %copy-start.6 = (bf16[1,2,8192]{2,1,0:T(2,128)(2,1)S(1)}, bf16[1,2,8192]{2,1,0:T(2,128)(2,1)}, u32[]{:S(2)}) copy-start(bf16[1,2,8192]{2,1,0:T(2,128)(2,1)} %param.9) | copy-start | bytes 98308
  6.6 7.2 %copy-start.1 = (f32[2,256,256]{2,1,0:T(8,128)S(1)}, f32[2,256,256]{2,1,0:T(8,128)}, u32[]{:S(2)}) copy-start(f32[2,256,256]{2,1,0:T(8,128)} %constant.11.clone.turn_ref) | copy-start | bytes 1572868
  6.6 7.2 %copy-start.2 = (bf16[512,512]{1,0:T(8,128)(2,1)S(1)}, bf16[512,512]{1,0:T(8,128)(2,1)}, u32[]{:S(2)}) copy-start(bf16[512,512]{1,0:T(8,128)(2,1)} %constant.8.clone.first_ref) | copy-start | bytes 1572868
  7.0 6.9 %copy-start.3 = (bf16[2,256,256]{2,1,0:T(8,128)(2,1)S(1)}, bf16[2,256,256]{2,1,0:T(8,128)(2,1)}, u32[]{:S(2)}) copy-start(bf16[2,256,256]{2,1,0:T(8,128)(2,1)} %constant.9.clone.second_ref) | copy-start | bytes 786436
  9.0 4.9 %copy-start.4 = (s32[4,15]{1,0:T(4,128)S(1)}, s32[4,15]{1,0:T(4,128)}, u32[]{:S(2)}) copy-start(s32[4,15]{1,0:T(4,128)} %edges_ref.7) | copy-start | bytes 724
  9.0 4.9 %copy-start.5 = (s32[2]{0:T(128)S(1)}, s32[2]{0:T(128)}, u32[]{:S(2)}) copy-start(s32[2]{0:T(128)} %live_ref.7) | copy-start | bytes 28
  9.1 10.1 %copy-start = (bf16[2,512,512]{2,1,0:T(8,128)(2,1)S(1)}, bf16[2,512,512]{2,1,0:T(8,128)(2,1)}, u32[]{:S(2)}) copy-start(bf16[2,512,512]{2,1,0:T(8,128)(2,1)} %constant.10.clone.rest_4_) | copy-start | bytes 3145732
  9.1 4.7 %collective-permute-start.5 = (bf16[4,2,32,256]{3,2,1,0:T(8,128)(2,1)S(1)}, bf16[4,2,32,256]{3,2,1,0:T(8,128)(2,1)S(1)}, u32[]{:S(2)}, u32[]{:S(2)}) collective-permute-start(bf16[4,2,32,256]{3,2,1,0:T(8,128)(2,1)S(1)} %reshape.9.rest_2_), channel_id=1, source_target_pairs={{0,1},{1,0},{2,3},{3,2},{4,5},{5,4},{6,7},{7,6},{8,9},{9,8},{10,11... | collective-permute-start | bytes 393224 | tf_op jit(solution)/shard_map/ppermute | solution.py:257
  11.4 4.6 %collective-permute-start.3 = (bf16[4,2,32,256]{3,2,1,0:T(8,128)(2,1)S(1)}, bf16[4,2,32,256]{3,2,1,0:T(8,128)(2,1)S(1)}, u32[]{:S(2)}, u32[]{:S(2)}) collective-permute-start(bf16[4,2,32,256]{3,2,1,0:T(8,128)(2,1)S(1)} %reshape.9.rest_2_), channel_id=1, source_target_pairs={{0,8},{1,17},{2,10},{3,19},{4,12},{5,21},{6,14},{7,23},{8,0},{9,25... | collective-permute-start | bytes 393224 | tf_op jit(solution)/shard_map/ppermute | solution.py:257
  12.6 4.8 %collective-permute-start.4 = (bf16[4,2,32,256]{3,2,1,0:T(8,128)(2,1)S(1)}, bf16[4,2,32,256]{3,2,1,0:T(8,128)(2,1)S(1)}, u32[]{:S(2)}, u32[]{:S(2)}) collective-permute-start(bf16[4,2,32,256]{3,2,1,0:T(8,128)(2,1)S(1)} %reshape.9.rest_2_), channel_id=1, source_target_pairs={{0,16},{1,9},{2,18},{3,11},{4,20},{5,13},{6,22},{7,15},{8,24},{9,1... | collective-permute-start | bytes 393224 | tf_op jit(solution)/shard_map/ppermute | solution.py:257
  17.5 1.7 %collective-permute-start.7 = (bf16[8,2,32,256]{3,2,1,0:T(8,128)(2,1)S(1)}, bf16[8,2,32,256]{3,2,1,0:T(8,128)(2,1)S(1)}, u32[]{:S(2)}, u32[]{:S(2)}) collective-permute-start(bf16[8,2,32,256]{3,2,1,0:T(8,128)(2,1)S(1)} %pad_maximum_fusion), channel_id=1, source_target_pairs={{0,1},{1,0},{2,3},{3,2},{4,5},{5,4},{6,7},{7,6},{8,9},{9,8},{10,11... | collective-permute-start | bytes 786440 | tf_op jit(solution)/shard_map/ppermute | solution.py:257
  18.0 4.1 %collective-permute-start.6 = (bf16[4,2,32,256]{3,2,1,0:T(8,128)(2,1)S(1)}, bf16[4,2,32,256]{3,2,1,0:T(8,128)(2,1)S(1)}, u32[]{:S(2)}, u32[]{:S(2)}) collective-permute-start(bf16[4,2,32,256]{3,2,1,0:T(8,128)(2,1)S(1)} %collective-permute-done.3.rest_2_), channel_id=1, source_target_pairs={{0,16},{1,9},{2,18},{3,11},{4,20},{5,13},{6,22},{7,15},{8,24},{9,1... | collective-permute-start | bytes 393224 | tf_op jit(solution)/shard_map/ppermute | solution.py:257
  22.1 3.0 %collective-permute-start.8 = (bf16[4,2,32,256]{3,2,1,0:T(8,128)(2,1)S(1)}, bf16[4,2,32,256]{3,2,1,0:T(8,128)(2,1)S(1)}, u32[]{:S(2)}, u32[]{:S(2)}) collective-permute-start(bf16[4,2,32,256]{3,2,1,0:T(8,128)(2,1)S(1)} %collective-permute-done.6.rest_2_), channel_id=1, source_target_pairs={{0,1},{1,0},{2,3},{3,2},{4,5},{5,4},{6,7},{7,6},{8,9},{9,8},{10,11... | collective-permute-start | bytes 393224 | tf_op jit(solution)/shard_map/ppermute | solution.py:257

commit v6 on v5

--- a/solution.py
+++ b/solution.py
@@ -28,7 +28,6 @@
     bf = np.dtype(BF16)
     every = np.arange(FA)
     cosine, sine = waves(every, every, FA)
-    first = np.block([[cosine, -sine], [sine, cosine]]).astype(bf)
     half = np.arange(HALF)
     even_c, even_s = waves(half, 2 * half, FA)
     odd_c, odd_s = waves(half, 2 * half + 1, FA)
@@ -41,7 +40,9 @@
     coarse = np.block([[cosine, sine], [-sine, cosine]]).astype(np.float32)
     upper = coarse.astype(bf)
     lower = (coarse - upper.astype(np.float32)).astype(bf)
-    turn = np.stack(waves(every, every, FA * FB)).astype(np.float32)
+    samples = np.concatenate([2 * half, 2 * half + 1])
+    turn = np.stack(waves(samples, every, FA * FB)).astype(np.float32)
+    first = np.transpose(second, (0, 2, 1))
     return first, second, np.stack([upper, lower]), turn
 
 
@@ -52,6 +53,14 @@
 def split(value):
     upper = value.astype(BF16)
     return upper, (value - upper.astype(F32)).astype(BF16)
+
+
+def bin_table(edges):
+    ends = jnp.full((edges.shape[0], 1), FB, edges.dtype)
+    low = jnp.concatenate([ends - FB, edges], axis=1)[:, :, None]
+    high = jnp.concatenate([edges, ends], axis=1)[:, :, None]
+    blocks = jnp.arange(FB, dtype=edges.dtype)[None, None, :]
+    return ((low <= blocks) & (blocks < high)).astype(BF16)
 
 
 def doublings(nseg):
@@ -72,7 +81,7 @@
 
 
 def filter_body(
-    nseg, held, flips, live_ref, edges_ref, halves, slots, first_ref, second_ref, turn_ref,
+    nseg, held, flips, bins_ref, halves, slots, first_ref, second_ref, turn_ref,
     sums, tops, powers, lefts, spectra, products, firsts, turneds, series,
 ):
     evens, odds = holdings(nseg)
@@ -82,8 +91,6 @@
     rows = FB // nseg
     low = nseg // 2
     tiles = powers.shape[0] // len(flips)
-    blocks = lax.broadcasted_iota(jnp.int32, (BINS, FB), 1)
-    bins = lax.broadcasted_iota(jnp.int32, (BINS, FB), 0)
 
     def stage(n):
         q, k = n // tiles, n % tiles
@@ -97,16 +104,17 @@
             for ref, at, seg in ((mine, mine_at, own), (theirs, theirs_at, other)):
                 start = pl.multiple_of(seg * rows, rows)
                 spectrum[:, pl.ds(start, rows), :] = ref[(at + z) * tiles + k].astype(F32)
-        label = jnp.zeros((BINS, FB), jnp.int32)
-        for j in range(BINS - 1):
-            label = label + (edges_ref[t, j] <= blocks).astype(jnp.int32)
-        onehot = (label == bins).astype(F32).astype(BF16)
-        nothing = jnp.zeros((BINS, FB), BF16)
-        left[0 : 2 * FB] = first_ref[...]
-        left[2 * FB : 2 * FB + BINS, 0:FB] = onehot
-        left[2 * FB : 2 * FB + BINS, FB:] = nothing
-        left[2 * FB + BINS :, 0:FB] = nothing
-        left[2 * FB + BINS :, FB:] = onehot
+        onehot = bins_ref[t]
+        nothing = jnp.zeros((BINS, HALF), BF16)
+        lead = onehot.astype(F32)
+        lead, trail = 0.5 * lead[:, :HALF], 0.5 * lead[:, HALF:]
+        for parity, mean in enumerate((lead + trail, lead - trail)):
+            mean = mean.astype(BF16)
+            left[parity, 0:FB] = first_ref[parity]
+            left[parity, FB : FB + BINS, 0:HALF] = mean
+            left[parity, FB : FB + BINS, HALF:] = nothing
+            left[parity, FB + BINS :, 0:HALF] = nothing
+            left[parity, FB + BINS :, HALF:] = mean
         energy = spectrum[0] * spectrum[0] + spectrum[1] * spectrum[1]
         energy = energy[:, :HALF] + energy[:, HALF:]
         upper, lower = split(energy)
@@ -115,25 +123,35 @@
     def multiply(u):
         n, s = u // held, u % held
         spectrum = spectra[n % 2]
-        for r in range(0, FB, STEP):
-            lines = slice(r, r + STEP)
-            hre, him = spectrum[0, lines], spectrum[1, lines]
+        for r in range(0, HALF, STEP):
+            out = slice(r, r + STEP)
             for d in range(2):
-                sre = slots[s][d, 0, lines].astype(F32)
-                sim = slots[s][d, 1, lines].astype(F32)
-                product = products[u % 2 * 2 + d]
-                product[lines] = (sre * hre + sim * him).astype(BF16)
-                product[FB + r : FB + r + STEP] = (sim * hre - sre * him).astype(BF16)
+                product, pair = products[u % 2 * 2 + d], []
+                for at in (r, r + HALF):
+                    lines = slice(at, at + STEP)
+                    hre, him = spectrum[0, lines], spectrum[1, lines]
+                    sre = slots[s][d, 0, lines].astype(F32)
+                    sim = slots[s][d, 1, lines].astype(F32)
+                    pair.append((sre * hre + sim * him, sim * hre - sre * him))
+                (are, aim), (bre, bim) = pair
+                product[0, out] = (are + bre).astype(BF16)
+                product[0, HALF + r : HALF + r + STEP] = (aim + bim).astype(BF16)
+                product[1, out] = (are - bre).astype(BF16)
+                product[1, HALF + r : HALF + r + STEP] = (aim - bim).astype(BF16)
+
+    results = {}
 
     def transform(u, d):
         at = u % 2 * 2 + d
-        firsts[at][...] = dot(lefts[u // held % 2][...], products[at][...])
+        for parity in range(2):
+            results[u, d, parity] = dot(lefts[u // held % 2][parity], products[at][parity])
 
     def turn_round(u, d):
-        first, turned = firsts[u % 2 * 2 + d], turneds[u % 2 * 2 + d]
+        turned = turneds[u % 2 * 2 + d]
         for r in range(0, FB, STEP):
-            out = slice(r, r + STEP)
-            are, aim = first[out], first[FB + r : FB + r + STEP]
+            out, parity, at = slice(r, r + STEP), r // HALF, r % HALF
+            first = results[u, d, parity]
+            are, aim = first[at : at + STEP], first[HALF + at : HALF + at + STEP]
             cos, sin = turn_ref[0, out], turn_ref[1, out]
             bre = are * cos - aim * sin
             bim = are * sin + aim * cos
@@ -142,24 +160,27 @@
             turned[1, out, 0:HALF] = (bre[:, :HALF] - bre[:, HALF:]).astype(BF16)
             turned[1, out, HALF:] = (bim[:, :HALF] - bim[:, HALF:]).astype(BF16)
         base = (u * 2 + d) * BINS
-        sums[base : base + BINS, 0:FA] = first[2 * FB : 2 * FB + BINS]
-        sums[base : base + BINS, FA:] = first[2 * FB + BINS :]
+        inner = slice(FB, FB + BINS)
+        outer = slice(FB + BINS, FB + 2 * BINS)
+        sums[base : base + BINS, 0:FA] = results[u, d, 0][inner] + results[u, d, 1][inner]
+        sums[base : base + BINS, FA:] = results[u, d, 0][outer] + results[u, d, 1][outer]
 
     def finish(u, d):
         at = u % 2 * 2 + d
+        best = None
         for parity in range(2):
-            series[at][parity] = dot(turneds[at][parity], second_ref[parity])
-
-    def highest(u):
-        best = None
-        ones, twos = series[u % 2 * 2], series[u % 2 * 2 + 1]
-        for parity in range(2):
+            result = dot(turneds[at][parity], second_ref[parity])
             for r in range(0, FB, STEP):
-                one, two = ones[parity, r : r + STEP], twos[parity, r : r + STEP]
-                both = one * one + two * two
-                both = both[:, :HALF] + both[:, HALF:]
-                best = both if best is None else jnp.maximum(best, both)
-        tops[u] = best
+                one = result[r : r + STEP]
+                one = one * one
+                one = one[:, :HALF] + one[:, HALF:]
+                if d == 0:
+                    series[u % 2][parity, r : r + STEP] = one
+                else:
+                    one = one + series[u % 2][parity, r : r + STEP]
+                    best = one if best is None else jnp.maximum(best, one)
+        if d == 1:
+            tops[u] = best
 
     units = powers.shape[0] * held
     stage(0)
@@ -179,10 +200,7 @@
         turn_round(u, 1)
         if more:
             transform(u + 1, 1)
-        if u > 0:
-            highest(u - 1)
         finish(u, 1)
-    highest(units - 1)
 
 
 def owner(my_bank, core, flip):
@@ -216,7 +234,8 @@
             sigma = jnp.sum(hpower, axis=0, keepdims=True)
             share = hpower / sigma
             for s in range(held):
-                live = live_ref[s] != 0
+                live = live_ref[0:1, s : s + 1].astype(F32)
+                lives = jnp.broadcast_to(live, (1, FB)) > 0
                 base = (n * held + s) * 2 * BINS
                 snr = jnp.zeros((1, FB), F32)
                 chi = jnp.zeros((1, FB), F32)
@@ -228,12 +247,13 @@
                     whole = whole * whole
                     snr = snr + whole[:, :FB] + whole[:, FB:]
                     chi = chi + diff[:, :FB] + diff[:, FB:]
-                snr_ref[t, s : s + 1] = jnp.where(live, snr / sigma, 0.0)
+                snr_ref[t, s : s + 1] = jnp.where(lives, snr / sigma, 0.0)
                 chi = chi / sigma / (4.0 * (BINS - 1))
-                chi_ref[t, s : s + 1] = jnp.where(live, chi, 0.0)
+                chi_ref[t, s : s + 1] = jnp.where(lives, chi, 0.0)
                 top = jnp.max(tops[k * held + s], axis=0, keepdims=True)
                 top = jnp.sqrt(jnp.max(top, axis=1, keepdims=True) / sigma)
-                peaks = jnp.where((slot_at == s) & (tile_at == t) & live, top, peaks)
+                top = jnp.where(live > 0, top, 0.0)
+                peaks = jnp.where((slot_at == s) & (tile_at == t), top, peaks)
             n += 1
     peak_ref[...] = peaks
 
@@ -245,7 +265,6 @@
     rows = FB // nseg
     low = nseg // 2
     first, second, coarse, turn = (jnp.asarray(x) for x in tables())
-    smem = pl.BlockSpec(memory_space=pltpu.SMEM)
     vmem = pl.BlockSpec(memory_space=pltpu.VMEM)
 
     def swap(block, flips):
@@ -266,16 +285,16 @@
             jax.ShapeDtypeStruct((fresh, BINS, HALF), F32),
         ]
         scratch = [
-            [pltpu.VMEM((2 * FB + 2 * BINS, 2 * FB), BF16) for _ in range(2)],
+            [pltpu.VMEM((2, FB + 2 * BINS, FB), BF16) for _ in range(2)],
             [pltpu.VMEM((2, FB, FA), F32) for _ in range(2)],
-            [pltpu.VMEM((2 * FB, FA), BF16) for _ in range(4)],
-            [pltpu.VMEM((2 * FB + 2 * BINS, FA), F32) for _ in range(4)],
             [pltpu.VMEM((2, FB, FA), BF16) for _ in range(4)],
-            [pltpu.VMEM((2, FB, FA), F32) for _ in range(4)],
+            [pltpu.VMEM((2, FB + 2 * BINS, FA), F32) for _ in range(4)],
+            [pltpu.VMEM((2, FB, FA), BF16) for _ in range(4)],
+            [pltpu.VMEM((2, FB, HALF), F32) for _ in range(2)],
         ]
         count = len(arrays)
 
-        def run(live_ref, edges_ref, first_ref, second_ref, turn_ref, *rest):
+        def run(live_ref, bins_ref, first_ref, second_ref, turn_ref, *rest):
             slots, rest = rest[:held], rest[held:]
             spectra, rest = rest[:count], rest[count:]
             pairs = [[(spectra[i], at) for i, at in half] for half in halves]
@@ -288,7 +307,7 @@
                 older, rest = rest[: len(before)], rest[len(before) :]
                 outs, results, scratches = rest[:3], rest[3:6], rest[8:]
             filter_body(
-                nseg, held, flips, live_ref, edges_ref, pairs, slots,
+                nseg, held, flips, bins_ref, pairs, slots,
                 first_ref, second_ref, turn_ref, *results, *scratches,
             )
             if earlier is not None:
@@ -296,7 +315,7 @@
                 groups = groups + [results]
                 statistics(held, every, live_ref, coarse_ref, groups, older, *outs, *rest[6:8])
 
-        inputs = [live_flags, bin_edges, first, second, turn, *slots, *arrays]
+        inputs = [live_flags.reshape(1, held), onehot, first, second, turn, *slots, *arrays]
         if earlier is None:
             shapes = made
         else:
@@ -311,7 +330,7 @@
             scratch = [pltpu.VMEM(x.shape, x.dtype) for x in made] + [full, full] + scratch
         return pl.pallas_call(
             run,
-            in_specs=[smem, smem] + [vmem] * (len(inputs) - 2),
+            in_specs=[vmem] * len(inputs),
             out_specs=[vmem] * 3,
             out_shape=shapes,
             scratch_shapes=scratch,
@@ -333,9 +352,13 @@
     if nseg == 8:
         third, second_, near = (swap(block, ((0, x), (0, x))) for x in (6, 4, 2))
         third, strain = slot_beside(third, strain)
+        third, bin_edges = lax.optimization_barrier((third, bin_edges))
+        onehot = bin_table(bin_edges)
+        near, onehot = lax.optimization_barrier((near, onehot))
         near, strain = slot_beside(near, strain)
         block = jnp.concatenate([block, third, second_, near], axis=0).reshape(low * tiles, 2, rows, FA)
     else:
+        onehot = bin_table(bin_edges)
         for even, odd in zip(*doublings(nseg)):
             found = swap(block, ((0, even), (0, odd)))
             if len(slots) < held:

time: 28.3 us -> 27 us (0.954)
  Pallas kernels: 9.49 us -> 6.88 us
  waiting for transfers between devices: 5.13 us -> 6.51 us
    pallas_call x4, Pallas kernels: 9.49 us -> 6.88 us  [call(): pl.pallas_call(run, in_specs=[vmem] * len(inputs), out_specs=[vmem] * 3,...]
    ppermute x9, waiting for transfers between devices: 5.13 us -> 6.51 us  [swap(): return lax.ppermute(block, ('bank', 'seg'), route)]
  transfers between devices with their start and end apart: 9 -> 9, of which waited for: 6 -> 7; matrix products, arithmetic and copies ran while one was open for 3% -> 3% of each run, Pallas kernels for 23% -> 17%
where the time goes in v6:
time: 27 us; the launch traced here: 26.8 us
  starting transfers between devices  11.4 us (42%)
  Pallas kernels  6.88 us (25%)
  waiting for transfers between devices  6.51 us (24%)
  local copies, waits for them, and re-layouts  0.94 us (3%)
  between operations  0.77 us (3%)
  other arithmetic  0.35 us (1%)
    ppermute x9, starting transfers between devices, swap(): return lax.ppermute(block, ('bank', 'seg'), route)  11.4 us
    pallas_call x4, Pallas kernels, call(): pl.pallas_call(run, in_specs=[vmem] * len(inputs), out_specs=[vmem] * 3,...  6.88 us
    ppermute x9, waiting for transfers between devices, swap(): return lax.ppermute(block, ('bank', 'seg'), route)  6.51 us
    another operation x2, local copies, waits for them, and re-layouts, slot_beside(): slot = strain[len(slots)].reshape(2, 2, FB, FA)  0.73 us
  transfers between devices with their start and end apart: 9, of which 7 were waited for; matrix products, arithmetic and copies ran while one was open for 3% of the time, Pallas kernels for 17%

profile of v6, /device:TPU:1, one launch (start us, length us, event | category | flops | bytes accessed | tf_op | source)
XLA Modules:
  0.0 26.8 jit_solution(3179292743641325595)
XLA Ops:
  0.6 0.0 slice-start
  0.6 4.2 %collective-permute-start.1 = (bf16[1,2,8192]{2,1,0:T(2,128)(2,1)}, bf16[1,2,8192]{2,1,0:T(2,128)(2,1)S(1)}, u32[]{:S(2)}, u32[]{:S(2)}) collective-permute-start(bf16[1,2,8192]{2,1,0:T(2,128)(2,1)} %param.9), channel_id=1, source_target_pairs={{0,6},{1,7},{2,4},{3,5},{4,2},{5,3},{6,0},{7,1},{8,14},{9,15},{10,... | collective-permute-start | bytes 98312 | tf_op jit(solution)/shard_map/ppermute | solution.py:276
  4.9 0.0 collective-permute-start
  4.9 0.4 %collective-permute-start.2 = (bf16[1,2,8192]{2,1,0:T(2,128)(2,1)}, bf16[1,2,8192]{2,1,0:T(2,128)(2,1)S(1)}, u32[]{:S(2)}, u32[]{:S(2)}) collective-permute-start(bf16[1,2,8192]{2,1,0:T(2,128)(2,1)} %param.9), channel_id=1, source_target_pairs={{0,4},{1,5},{2,6},{3,7},{4,0},{5,1},{6,2},{7,3},{8,12},{9,13},{10,... | collective-permute-start | bytes 98312 | tf_op jit(solution)/shard_map/ppermute | solution.py:276
  5.2 0.4 %reshape_squeeze.6.rest_0_ = bf16[2,2,256,256]{3,2,1,0:T(8,128)(2,1)S(1)} reshape(bf16[1,2,2,65536]{3,2,1,0:T(2,128)(2,1)S(1)} %slice-done) | data formatting | bytes 1048576 | tf_op jit(solution)/shard_map/reshape;squeeze | solution.py:347
  5.6 0.8 %collective-permute-done.1 = bf16[1,2,8192]{2,1,0:T(2,128)(2,1)S(1)} collective-permute-done((bf16[1,2,8192]{2,1,0:T(2,128)(2,1)}, bf16[1,2,8192]{2,1,0:T(2,128)(2,1)S(1)}, u32[]{:S(2)}, u32[]{:S(2)}) %collective-permute-start.1) | collective-permute-done | bytes 32800 | tf_op jit(solution)/shard_map/ppermute | solution.py:276
  6.4 0.1 fusion.2
  6.5 0.1 fusion.1.bins_ref
  6.6 0.0 slice-start.1
  6.6 1.3 %collective-permute-done = bf16[1,2,8192]{2,1,0:T(2,128)(2,1)S(1)} collective-permute-done((bf16[1,2,8192]{2,1,0:T(2,128)(2,1)}, bf16[1,2,8192]{2,1,0:T(2,128)(2,1)S(1)}, u32[]{:S(2)}, u32[]{:S(2)}) %collective-permute-start) | collective-permute-done | bytes 32800 | tf_op jit(solution)/shard_map/ppermute | solution.py:276
  7.9 0.4 %reshape_squeeze.7.rest_1_ = bf16[2,2,256,256]{3,2,1,0:T(8,128)(2,1)S(1)} reshape(bf16[1,2,2,65536]{3,2,1,0:T(2,128)(2,1)S(1)} %slice-done.1) | data formatting | bytes 1048576 | tf_op jit(solution)/shard_map/reshape;squeeze | solution.py:347
  8.2 0.0 copy-start.1
  8.2 0.5 %collective-permute-done.2 = bf16[1,2,8192]{2,1,0:T(2,128)(2,1)S(1)} collective-permute-done((bf16[1,2,8192]{2,1,0:T(2,128)(2,1)}, bf16[1,2,8192]{2,1,0:T(2,128)(2,1)S(1)}, u32[]{:S(2)}, u32[]{:S(2)}) %collective-permute-start.2) | collective-permute-done | bytes 32800 | tf_op jit(solution)/shard_map/ppermute | solution.py:276
  8.7 0.2 pad_maximum_fusion.1
  9.0 0.1 reshape.18.rest_2_
  9.1 0.0 copy-start.4
  9.1 2.3 %collective-permute-start.5 = (bf16[4,2,32,256]{3,2,1,0:T(8,128)(2,1)S(1)}, bf16[4,2,32,256]{3,2,1,0:T(8,128)(2,1)S(1)}, u32[]{:S(2)}, u32[]{:S(2)}) collective-permute-start(bf16[4,2,32,256]{3,2,1,0:T(8,128)(2,1)S(1)} %reshape.18.rest_2_), channel_id=1, source_target_pairs={{0,1},{1,0},{2,3},{3,2},{4,5},{5,4},{6,7},{7,6},{8,9},{9,8},{10,11... | collective-permute-start | bytes 393224 | tf_op jit(solution)/shard_map/ppermute | solution.py:276
  11.4 1.2 %collective-permute-start.3 = (bf16[4,2,32,256]{3,2,1,0:T(8,128)(2,1)S(1)}, bf16[4,2,32,256]{3,2,1,0:T(8,128)(2,1)S(1)}, u32[]{:S(2)}, u32[]{:S(2)}) collective-permute-start(bf16[4,2,32,256]{3,2,1,0:T(8,128)(2,1)S(1)} %reshape.18.rest_2_), channel_id=1, source_target_pairs={{0,8},{1,17},{2,10},{3,19},{4,12},{5,21},{6,14},{7,23},{8,0},{9,25... | collective-permute-start | bytes 393224 | tf_op jit(solution)/shard_map/ppermute | solution.py:276
  12.6 1.2 %collective-permute-start.4 = (bf16[4,2,32,256]{3,2,1,0:T(8,128)(2,1)S(1)}, bf16[4,2,32,256]{3,2,1,0:T(8,128)(2,1)S(1)}, u32[]{:S(2)}, u32[]{:S(2)}) collective-permute-start(bf16[4,2,32,256]{3,2,1,0:T(8,128)(2,1)S(1)} %reshape.18.rest_2_), channel_id=1, source_target_pairs={{0,16},{1,9},{2,18},{3,11},{4,20},{5,13},{6,22},{7,15},{8,24},{9,1... | collective-permute-start | bytes 393224 | tf_op jit(solution)/shard_map/ppermute | solution.py:276
  13.8 0.0 collective-permute-done.5.rest_3_
  13.9 0.0 copy-start
  13.9 1.4 %shard_map.103 = (f32[64,512]{1,0:T(8,128)S(1)}, f32[2,16,128]{2,1,0:T(8,128)S(1)}, f32[1,16,128]{2,1,0:T(8,128)S(1)}) custom-call(s32[1,2]{1,0:T(1,128)S(1)} %bitcast.2, bf16[4,16,256]{2,1,0:T(8,128)(2,1)S(1)} %fusion.1.bins_ref, bf16[2,256,256]{2,1,0:T(8,128)(2,1)S(1)} %copy-done.2, bf16[2,256,256]{2,1,0:T(8,128)(2,1)S(1)} %copy-done.3, ...), custom_call_target="tpu_custom_call" | custom-call | flops 805306368 | bytes 1048576 | tf_op jit(solution)/shard_map/pallas_call | solution.py:331
  15.3 0.2 collective-permute-done.3.rest_2_
  15.5 1.9 %collective-permute-done.4.rest_2_ = bf16[4,2,32,256]{3,2,1,0:T(8,128)(2,1)S(1)} collective-permute-done((bf16[4,2,32,256]{3,2,1,0:T(8,128)(2,1)S(1)}, bf16[4,2,32,256]{3,2,1,0:T(8,128)(2,1)S(1)}, u32[]{:S(2)}, u32[]{:S(2)}) %collective-permute-start.4) | collective-permute-done | bytes 131104 | tf_op jit(solution)/shard_map/ppermute | solution.py:276
  17.5 0.5 %collective-permute-start.7 = (bf16[8,2,32,256]{3,2,1,0:T(8,128)(2,1)S(1)}, bf16[8,2,32,256]{3,2,1,0:T(8,128)(2,1)S(1)}, u32[]{:S(2)}, u32[]{:S(2)}) collective-permute-start(bf16[8,2,32,256]{3,2,1,0:T(8,128)(2,1)S(1)} %pad_maximum_fusion), channel_id=1, source_target_pairs={{0,1},{1,0},{2,3},{3,2},{4,5},{5,4},{6,7},{7,6},{8,9},{9,8},{10,11... | collective-permute-start | bytes 786440 | tf_op jit(solution)/shard_map/ppermute | solution.py:276
  18.0 0.6 %collective-permute-start.6 = (bf16[4,2,32,256]{3,2,1,0:T(8,128)(2,1)S(1)}, bf16[4,2,32,256]{3,2,1,0:T(8,128)(2,1)S(1)}, u32[]{:S(2)}, u32[]{:S(2)}) collective-permute-start(bf16[4,2,32,256]{3,2,1,0:T(8,128)(2,1)S(1)} %collective-permute-done.3.rest_2_), channel_id=1, source_target_pairs={{0,16},{1,9},{2,18},{3,11},{4,20},{5,13},{6,22},{7,15},{8,24},{9,1... | collective-permute-start | bytes 393224 | tf_op jit(solution)/shard_map/ppermute | solution.py:276
  18.6 0.6 %collective-permute-done.7.rest_3_ = bf16[8,2,32,256]{3,2,1,0:T(8,128)(2,1)S(1)} collective-permute-done((bf16[8,2,32,256]{3,2,1,0:T(8,128)(2,1)S(1)}, bf16[8,2,32,256]{3,2,1,0:T(8,128)(2,1)S(1)}, u32[]{:S(2)}, u32[]{:S(2)}) %collective-permute-start.7) | collective-permute-done | bytes 262176 | tf_op jit(solution)/shard_map/ppermute | solution.py:276
  19.2 1.7 %shard_map.104 = (f32[2,4]{1,0:T(2,128)S(1)}, f32[4,2,256]{2,1,0:T(2,128)S(1)}, f32[4,2,256]{2,1,0:T(2,128)S(1)}) custom-call(s32[1,2]{1,0:T(1,128)S(1)} %bitcast.3, bf16[4,16,256]{2,1,0:T(8,128)(2,1)S(1)} %fusion.1.bins_ref, bf16[2,256,256]{2,1,0:T(8,128)(2,1)S(1)} %copy-done.2, bf16[2,256,256]{2,1,0:T(8,128)(2,1)S(1)} %copy-done.3, ...), custom_call_target="tpu_custom_call" | custom-call | flops 805306368 | bytes 1048576 | tf_op jit(solution)/shard_map/pallas_call | solution.py:331
  20.9 1.2 %collective-permute-done.6.rest_2_ = bf16[4,2,32,256]{3,2,1,0:T(8,128)(2,1)S(1)} collective-permute-done((bf16[4,2,32,256]{3,2,1,0:T(8,128)(2,1)S(1)}, bf16[4,2,32,256]{3,2,1,0:T(8,128)(2,1)S(1)}, u32[]{:S(2)}, u32[]{:S(2)}) %collective-permute-start.6) | collective-permute-done | bytes 131104 | tf_op jit(solution)/shard_map/ppermute | solution.py:276
  22.1 0.9 %collective-permute-start.8 = (bf16[4,2,32,256]{3,2,1,0:T(8,128)(2,1)S(1)}, bf16[4,2,32,256]{3,2,1,0:T(8,128)(2,1)S(1)}, u32[]{:S(2)}, u32[]{:S(2)}) collective-permute-start(bf16[4,2,32,256]{3,2,1,0:T(8,128)(2,1)S(1)} %collective-permute-done.6.rest_2_), channel_id=1, source_target_pairs={{0,1},{1,0},{2,3},{3,2},{4,5},{5,4},{6,7},{7,6},{8,9},{9,8},{10,11... | collective-permute-start | bytes 393224 | tf_op jit(solution)/shard_map/ppermute | solution.py:276
  23.1 1.4 %shard_map.105 = (f32[64,512]{1,0:T(8,128)S(1)}, f32[2,16,128]{2,1,0:T(8,128)S(1)}, f32[1,16,128]{2,1,0:T(8,128)S(1)}) custom-call(s32[1,2]{1,0:T(1,128)S(1)} %bitcast.4, bf16[4,16,256]{2,1,0:T(8,128)(2,1)S(1)} %fusion.1.bins_ref, bf16[2,256,256]{2,1,0:T(8,128)(2,1)S(1)} %copy-done.2, bf16[2,256,256]{2,1,0:T(8,128)(2,1)S(1)} %copy-done.3, ...), custom_call_target="tpu_custom_call" | custom-call | flops 805306368 | bytes 1048576 | tf_op jit(solution)/shard_map/pallas_call | solution.py:331
  24.5 2.4 %shard_map.106 = (f32[2,4]{1,0:T(2,128)}, f32[4,2,256]{2,1,0:T(2,128)}, f32[4,2,256]{2,1,0:T(2,128)}) custom-call(s32[1,2]{1,0:T(1,128)S(1)} %bitcast.5, bf16[4,16,256]{2,1,0:T(8,128)(2,1)S(1)} %fusion.1.bins_ref, bf16[2,256,256]{2,1,0:T(8,128)(2,1)S(1)} %copy-done.2, bf16[2,256,256]{2,1,0:T(8,128)(2,1)S(1)} %copy-done.3, f32[2,256,256]{2,1,0:T(8,128)S(1)} %copy-done.1, ...), custom_call_target="tpu_custom_call" | custom-call | flops 805306368 | bytes 1048576 | tf_op jit(solution)/shard_map/pallas_call | solution.py:331
  (15 shorter events, 0.1 us)
Async XLA Ops:
  0.6 4.6 %slice-start = ((bf16[2,2,2,65536]{3,2,1,0:T(2,128)(2,1)}), bf16[1,2,2,65536]{3,2,1,0:T(2,128)(2,1)S(1)}, s32[]{:S(2)}) async-start(bf16[2,2,2,65536]{3,2,1,0:T(2,128)(2,1)} %param.8), calls=%async_computation | async-start | bytes 1048576 | tf_op jit(solution)/shard_map/slice | solution.py:347
  0.6 5.7 %collective-permute-start.1 = (bf16[1,2,8192]{2,1,0:T(2,128)(2,1)}, bf16[1,2,8192]{2,1,0:T(2,128)(2,1)S(1)}, u32[]{:S(2)}, u32[]{:S(2)}) collective-permute-start(bf16[1,2,8192]{2,1,0:T(2,128)(2,1)} %param.9), channel_id=1, source_target_pairs={{0,6},{1,7},{2,4},{3,5},{4,2},{5,3},{6,0},{7,1},{8,14},{9,15},{10,... | collective-permute-start | bytes 98312 | tf_op jit(solution)/shard_map/ppermute | solution.py:276
  4.9 3.0 %collective-permute-start = (bf16[1,2,8192]{2,1,0:T(2,128)(2,1)}, bf16[1,2,8192]{2,1,0:T(2,128)(2,1)S(1)}, u32[]{:S(2)}, u32[]{:S(2)}) collective-permute-start(bf16[1,2,8192]{2,1,0:T(2,128)(2,1)} %param.9), channel_id=1, source_target_pairs={{0,2},{1,3},{2,0},{3,1},{4,6},{5,7},{6,4},{7,5},{8,10},{9,11},{10,... | collective-permute-start | bytes 98312 | tf_op jit(solution)/shard_map/ppermute | solution.py:276
  4.9 3.9 %collective-permute-start.2 = (bf16[1,2,8192]{2,1,0:T(2,128)(2,1)}, bf16[1,2,8192]{2,1,0:T(2,128)(2,1)S(1)}, u32[]{:S(2)}, u32[]{:S(2)}) collective-permute-start(bf16[1,2,8192]{2,1,0:T(2,128)(2,1)} %param.9), channel_id=1, source_target_pairs={{0,4},{1,5},{2,6},{3,7},{4,0},{5,1},{6,2},{7,3},{8,12},{9,13},{10,... | collective-permute-start | bytes 98312 | tf_op jit(solution)/shard_map/ppermute | solution.py:276
  5.2 1.2 %copy-start.6 = (s32[4,15]{1,0:T(4,128)S(1)}, s32[4,15]{1,0:T(4,128)}, u32[]{:S(2)}) copy-start(s32[4,15]{1,0:T(4,128)} %param.10) | copy-start | bytes 724
  6.6 1.3 %slice-start.1 = ((bf16[2,2,2,65536]{3,2,1,0:T(2,128)(2,1)}), bf16[1,2,2,65536]{3,2,1,0:T(2,128)(2,1)S(1)}, s32[]{:S(2)}) async-start(bf16[2,2,2,65536]{3,2,1,0:T(2,128)(2,1)} %param.8), calls=%async_computation.1 | async-start | bytes 1048576 | tf_op jit(solution)/shard_map/slice | solution.py:347
  7.8 0.9 %copy-start.5 = (bf16[1,2,8192]{2,1,0:T(2,128)(2,1)S(1)}, bf16[1,2,8192]{2,1,0:T(2,128)(2,1)}, u32[]{:S(2)}) copy-start(bf16[1,2,8192]{2,1,0:T(2,128)(2,1)} %param.9) | copy-start | bytes 98308
  7.8 6.0 %copy-start.2 = (bf16[2,256,256]{2,1,0:T(8,128)(2,1)S(1)}, bf16[2,256,256]{2,1,0:T(8,128)(2,1)}, u32[]{:S(2)}) copy-start(bf16[2,256,256]{2,1,0:T(8,128)(2,1)} %constant.12.clone.first_ref) | copy-start | bytes 786436
  7.8 6.0 %copy-start.3 = (bf16[2,256,256]{2,1,0:T(8,128)(2,1)S(1)}, bf16[2,256,256]{2,1,0:T(8,128)(2,1)}, u32[]{:S(2)}) copy-start(bf16[2,256,256]{2,1,0:T(8,128)(2,1)} %constant.13.clone.second_ref) | copy-start | bytes 786436
  8.2 5.6 %copy-start.1 = (f32[2,256,256]{2,1,0:T(8,128)S(1)}, f32[2,256,256]{2,1,0:T(8,128)}, u32[]{:S(2)}) copy-start(f32[2,256,256]{2,1,0:T(8,128)} %constant.15.clone.turn_ref) | copy-start | bytes 1572868
  9.1 4.8 %copy-start.4 = (s32[2]{0:T(128)S(1)}, s32[2]{0:T(128)}, u32[]{:S(2)}) copy-start(s32[2]{0:T(128)} %param.11) | copy-start | bytes 28
  9.1 4.7 %collective-permute-start.5 = (bf16[4,2,32,256]{3,2,1,0:T(8,128)(2,1)S(1)}, bf16[4,2,32,256]{3,2,1,0:T(8,128)(2,1)S(1)}, u32[]{:S(2)}, u32[]{:S(2)}) collective-permute-start(bf16[4,2,32,256]{3,2,1,0:T(8,128)(2,1)S(1)} %reshape.18.rest_2_), channel_id=1, source_target_pairs={{0,1},{1,0},{2,3},{3,2},{4,5},{5,4},{6,7},{7,6},{8,9},{9,8},{10,11... | collective-permute-start | bytes 393224 | tf_op jit(solution)/shard_map/ppermute | solution.py:276
  11.4 4.1 %collective-permute-start.3 = (bf16[4,2,32,256]{3,2,1,0:T(8,128)(2,1)S(1)}, bf16[4,2,32,256]{3,2,1,0:T(8,128)(2,1)S(1)}, u32[]{:S(2)}, u32[]{:S(2)}) collective-permute-start(bf16[4,2,32,256]{3,2,1,0:T(8,128)(2,1)S(1)} %reshape.18.rest_2_), channel_id=1, source_target_pairs={{0,8},{1,17},{2,10},{3,19},{4,12},{5,21},{6,14},{7,23},{8,0},{9,25... | collective-permute-start | bytes 393224 | tf_op jit(solution)/shard_map/ppermute | solution.py:276
  12.6 4.8 %collective-permute-start.4 = (bf16[4,2,32,256]{3,2,1,0:T(8,128)(2,1)S(1)}, bf16[4,2,32,256]{3,2,1,0:T(8,128)(2,1)S(1)}, u32[]{:S(2)}, u32[]{:S(2)}) collective-permute-start(bf16[4,2,32,256]{3,2,1,0:T(8,128)(2,1)S(1)} %reshape.18.rest_2_), channel_id=1, source_target_pairs={{0,16},{1,9},{2,18},{3,11},{4,20},{5,13},{6,22},{7,15},{8,24},{9,1... | collective-permute-start | bytes 393224 | tf_op jit(solution)/shard_map/ppermute | solution.py:276
  13.9 5.3 %copy-start = (bf16[2,512,512]{2,1,0:T(8,128)(2,1)S(1)}, bf16[2,512,512]{2,1,0:T(8,128)(2,1)}, u32[]{:S(2)}) copy-start(bf16[2,512,512]{2,1,0:T(8,128)(2,1)} %constant.14.clone.rest_4_) | copy-start | bytes 3145732
  17.5 1.7 %collective-permute-start.7 = (bf16[8,2,32,256]{3,2,1,0:T(8,128)(2,1)S(1)}, bf16[8,2,32,256]{3,2,1,0:T(8,128)(2,1)S(1)}, u32[]{:S(2)}, u32[]{:S(2)}) collective-permute-start(bf16[8,2,32,256]{3,2,1,0:T(8,128)(2,1)S(1)} %pad_maximum_fusion), channel_id=1, source_target_pairs={{0,1},{1,0},{2,3},{3,2},{4,5},{5,4},{6,7},{7,6},{8,9},{9,8},{10,11... | collective-permute-start | bytes 786440 | tf_op jit(solution)/shard_map/ppermute | solution.py:276
  18.0 4.1 %collective-permute-start.6 = (bf16[4,2,32,256]{3,2,1,0:T(8,128)(2,1)S(1)}, bf16[4,2,32,256]{3,2,1,0:T(8,128)(2,1)S(1)}, u32[]{:S(2)}, u32[]{:S(2)}) collective-permute-start(bf16[4,2,32,256]{3,2,1,0:T(8,128)(2,1)S(1)} %collective-permute-done.3.rest_2_), channel_id=1, source_target_pairs={{0,16},{1,9},{2,18},{3,11},{4,20},{5,13},{6,22},{7,15},{8,24},{9,1... | collective-permute-start | bytes 393224 | tf_op jit(solution)/shard_map/ppermute | solution.py:276
  22.1 2.3 %collective-permute-start.8 = (bf16[4,2,32,256]{3,2,1,0:T(8,128)(2,1)S(1)}, bf16[4,2,32,256]{3,2,1,0:T(8,128)(2,1)S(1)}, u32[]{:S(2)}, u32[]{:S(2)}) collective-permute-start(bf16[4,2,32,256]{3,2,1,0:T(8,128)(2,1)S(1)} %collective-permute-done.6.rest_2_), channel_id=1, source_target_pairs={{0,1},{1,0},{2,3},{3,2},{4,5},{5,4},{6,7},{7,6},{8,9},{9,8},{10,11... | collective-permute-start | bytes 393224 | tf_op jit(solution)/shard_map/ppermute | solution.py:276

commit v7 on v6

--- a/solution.py
+++ b/solution.py
@@ -28,6 +28,7 @@
     bf = np.dtype(BF16)
     every = np.arange(FA)
     cosine, sine = waves(every, every, FA)
+    first = np.block([[cosine, -sine], [sine, cosine]]).astype(bf)
     half = np.arange(HALF)
     even_c, even_s = waves(half, 2 * half, FA)
     odd_c, odd_s = waves(half, 2 * half + 1, FA)
@@ -40,9 +41,7 @@
     coarse = np.block([[cosine, sine], [-sine, cosine]]).astype(np.float32)
     upper = coarse.astype(bf)
     lower = (coarse - upper.astype(np.float32)).astype(bf)
-    samples = np.concatenate([2 * half, 2 * half + 1])
-    turn = np.stack(waves(samples, every, FA * FB)).astype(np.float32)
-    first = np.transpose(second, (0, 2, 1))
+    turn = np.stack(waves(every, every, FA * FB)).astype(np.float32)
     return first, second, np.stack([upper, lower]), turn
 
 
@@ -82,7 +81,7 @@
 
 def filter_body(
     nseg, held, flips, bins_ref, halves, slots, first_ref, second_ref, turn_ref,
-    sums, tops, powers, lefts, spectra, products, firsts, turneds, series,
+    sums, tops, powers, lefts, spectra, products, turneds, series,
 ):
     evens, odds = holdings(nseg)
     my_bank = lax.axis_index("bank")
@@ -105,16 +104,12 @@
                 start = pl.multiple_of(seg * rows, rows)
                 spectrum[:, pl.ds(start, rows), :] = ref[(at + z) * tiles + k].astype(F32)
         onehot = bins_ref[t]
-        nothing = jnp.zeros((BINS, HALF), BF16)
-        lead = onehot.astype(F32)
-        lead, trail = 0.5 * lead[:, :HALF], 0.5 * lead[:, HALF:]
-        for parity, mean in enumerate((lead + trail, lead - trail)):
-            mean = mean.astype(BF16)
-            left[parity, 0:FB] = first_ref[parity]
-            left[parity, FB : FB + BINS, 0:HALF] = mean
-            left[parity, FB : FB + BINS, HALF:] = nothing
-            left[parity, FB + BINS :, 0:HALF] = nothing
-            left[parity, FB + BINS :, HALF:] = mean
+        nothing = jnp.zeros((BINS, FB), BF16)
+        left[0 : 2 * FB] = first_ref[...]
+        left[2 * FB : 2 * FB + BINS, 0:FB] = onehot
+        left[2 * FB : 2 * FB + BINS, FB:] = nothing
+        left[2 * FB + BINS :, 0:FB] = nothing
+        left[2 * FB + BINS :, FB:] = onehot
         energy = spectrum[0] * spectrum[0] + spectrum[1] * spectrum[1]
         energy = energy[:, :HALF] + energy[:, HALF:]
         upper, lower = split(energy)
@@ -123,35 +118,26 @@
     def multiply(u):
         n, s = u // held, u % held
         spectrum = spectra[n % 2]
-        for r in range(0, HALF, STEP):
+        for r in range(0, FB, STEP):
+            lines = slice(r, r + STEP)
+            hre, him = spectrum[0, lines], spectrum[1, lines]
+            for d in range(2):
+                sre = slots[s][d, 0, lines].astype(F32)
+                sim = slots[s][d, 1, lines].astype(F32)
+                product = products[u % 2 * 2 + d]
+                product[lines] = (sre * hre + sim * him).astype(BF16)
+                product[FB + r : FB + r + STEP] = (sim * hre - sre * him).astype(BF16)
+
+    results = {}
+
+    def transform(u, d):
+        results[u, d] = dot(lefts[u // held % 2][...], products[u % 2 * 2 + d][...])
+
+    def turn_round(u, d):
+        first, turned = results[u, d], turneds[u % 2 * 2 + d]
+        for r in range(0, FB, STEP):
             out = slice(r, r + STEP)
-            for d in range(2):
-                product, pair = products[u % 2 * 2 + d], []
-                for at in (r, r + HALF):
-                    lines = slice(at, at + STEP)
-                    hre, him = spectrum[0, lines], spectrum[1, lines]
-                    sre = slots[s][d, 0, lines].astype(F32)
-                    sim = slots[s][d, 1, lines].astype(F32)
-                    pair.append((sre * hre + sim * him, sim * hre - sre * him))
-                (are, aim), (bre, bim) = pair
-                product[0, out] = (are + bre).astype(BF16)
-                product[0, HALF + r : HALF + r + STEP] = (aim + bim).astype(BF16)
-                product[1, out] = (are - bre).astype(BF16)
-                product[1, HALF + r : HALF + r + STEP] = (aim - bim).astype(BF16)
-
-    results = {}
-
-    def transform(u, d):
-        at = u % 2 * 2 + d
-        for parity in range(2):
-            results[u, d, parity] = dot(lefts[u // held % 2][parity], products[at][parity])
-
-    def turn_round(u, d):
-        turned = turneds[u % 2 * 2 + d]
-        for r in range(0, FB, STEP):
-            out, parity, at = slice(r, r + STEP), r // HALF, r % HALF
-            first = results[u, d, parity]
-            are, aim = first[at : at + STEP], first[HALF + at : HALF + at + STEP]
+            are, aim = first[out], first[FB + r : FB + r + STEP]
             cos, sin = turn_ref[0, out], turn_ref[1, out]
             bre = are * cos - aim * sin
             bim = are * sin + aim * cos
@@ -160,10 +146,8 @@
             turned[1, out, 0:HALF] = (bre[:, :HALF] - bre[:, HALF:]).astype(BF16)
             turned[1, out, HALF:] = (bim[:, :HALF] - bim[:, HALF:]).astype(BF16)
         base = (u * 2 + d) * BINS
-        inner = slice(FB, FB + BINS)
-        outer = slice(FB + BINS, FB + 2 * BINS)
-        sums[base : base + BINS, 0:FA] = results[u, d, 0][inner] + results[u, d, 1][inner]
-        sums[base : base + BINS, FA:] = results[u, d, 0][outer] + results[u, d, 1][outer]
+        sums[base : base + BINS, 0:FA] = first[2 * FB : 2 * FB + BINS]
+        sums[base : base + BINS, FA:] = first[2 * FB + BINS :]
 
     def finish(u, d):
         at = u % 2 * 2 + d
@@ -285,10 +269,9 @@
             jax.ShapeDtypeStruct((fresh, BINS, HALF), F32),
         ]
         scratch = [
-            [pltpu.VMEM((2, FB + 2 * BINS, FB), BF16) for _ in range(2)],
+            [pltpu.VMEM((2 * FB + 2 * BINS, 2 * FB), BF16) for _ in range(2)],
             [pltpu.VMEM((2, FB, FA), F32) for _ in range(2)],
-            [pltpu.VMEM((2, FB, FA), BF16) for _ in range(4)],
-            [pltpu.VMEM((2, FB + 2 * BINS, FA), F32) for _ in range(4)],
+            [pltpu.VMEM((2 * FB, FA), BF16) for _ in range(4)],
             [pltpu.VMEM((2, FB, FA), BF16) for _ in range(4)],
             [pltpu.VMEM((2, FB, HALF), F32) for _ in range(2)],
         ]

time: 27 us -> 27.1 us (level)
  Pallas kernels: 6.88 us -> 7.22 us
    pallas_call x4, Pallas kernels: 6.88 us -> 7.22 us  [call(): pl.pallas_call(run, in_specs=[vmem] * len(inputs), out_specs=[vmem] * 3,...]
  transfers between devices with their start and end apart: 9 -> 9, of which waited for: 7 -> 7; matrix products, arithmetic and copies ran while one was open for 3% -> 3% of each run, Pallas kernels for 17% -> 18%
where the time goes in v7:
time: 27.1 us; the launch traced here: 27 us
  starting transfers between devices  11.4 us (42%)
  Pallas kernels  7.22 us (27%)
  waiting for transfers between devices  6.33 us (23%)
  local copies, waits for them, and re-layouts  0.94 us (3%)
  between operations  0.77 us (3%)
  other arithmetic  0.35 us (1%)
    ppermute x9, starting transfers between devices, swap(): return lax.ppermute(block, ('bank', 'seg'), route)  11.4 us
    pallas_call x4, Pallas kernels, call(): pl.pallas_call(run, in_specs=[vmem] * len(inputs), out_specs=[vmem] * 3,...  7.22 us
    ppermute x9, waiting for transfers between devices, swap(): return lax.ppermute(block, ('bank', 'seg'), route)  6.33 us
    another operation x2, local copies, waits for them, and re-layouts, slot_beside(): slot = strain[len(slots)].reshape(2, 2, FB, FA)  0.73 us
  transfers between devices with their start and end apart: 9, of which 7 were waited for; matrix products, arithmetic and copies ran while one was open for 3% of the time, Pallas kernels for 18%

profile of v7, /device:TPU:1, one launch (start us, length us, event | category | flops | bytes accessed | tf_op | source)
XLA Modules:
  0.0 27.0 jit_solution(14005813267065108467)
XLA Ops:
  0.6 0.0 slice-start
  0.6 4.2 %collective-permute-start.1 = (bf16[1,2,8192]{2,1,0:T(2,128)(2,1)}, bf16[1,2,8192]{2,1,0:T(2,128)(2,1)S(1)}, u32[]{:S(2)}, u32[]{:S(2)}) collective-permute-start(bf16[1,2,8192]{2,1,0:T(2,128)(2,1)} %param.9), channel_id=1, source_target_pairs={{0,6},{1,7},{2,4},{3,5},{4,2},{5,3},{6,0},{7,1},{8,14},{9,15},{10,... | collective-permute-start | bytes 98312 | tf_op jit(solution)/shard_map/ppermute | solution.py:260
  4.9 0.0 collective-permute-start
  4.9 0.4 %collective-permute-start.2 = (bf16[1,2,8192]{2,1,0:T(2,128)(2,1)}, bf16[1,2,8192]{2,1,0:T(2,128)(2,1)S(1)}, u32[]{:S(2)}, u32[]{:S(2)}) collective-permute-start(bf16[1,2,8192]{2,1,0:T(2,128)(2,1)} %param.9), channel_id=1, source_target_pairs={{0,4},{1,5},{2,6},{3,7},{4,0},{5,1},{6,2},{7,3},{8,12},{9,13},{10,... | collective-permute-start | bytes 98312 | tf_op jit(solution)/shard_map/ppermute | solution.py:260
  5.2 0.4 %reshape_squeeze.6.rest_0_ = bf16[2,2,256,256]{3,2,1,0:T(8,128)(2,1)S(1)} reshape(bf16[1,2,2,65536]{3,2,1,0:T(2,128)(2,1)S(1)} %slice-done) | data formatting | bytes 1048576 | tf_op jit(solution)/shard_map/reshape;squeeze | solution.py:330
  5.6 0.8 %collective-permute-done.1 = bf16[1,2,8192]{2,1,0:T(2,128)(2,1)S(1)} collective-permute-done((bf16[1,2,8192]{2,1,0:T(2,128)(2,1)}, bf16[1,2,8192]{2,1,0:T(2,128)(2,1)S(1)}, u32[]{:S(2)}, u32[]{:S(2)}) %collective-permute-start.1) | collective-permute-done | bytes 32800 | tf_op jit(solution)/shard_map/ppermute | solution.py:260
  6.4 0.1 fusion.2
  6.5 0.1 fusion.1.bins_ref
  6.6 0.0 slice-start.1
  6.6 1.3 %collective-permute-done = bf16[1,2,8192]{2,1,0:T(2,128)(2,1)S(1)} collective-permute-done((bf16[1,2,8192]{2,1,0:T(2,128)(2,1)}, bf16[1,2,8192]{2,1,0:T(2,128)(2,1)S(1)}, u32[]{:S(2)}, u32[]{:S(2)}) %collective-permute-start) | collective-permute-done | bytes 32800 | tf_op jit(solution)/shard_map/ppermute | solution.py:260
  7.9 0.4 %reshape_squeeze.7.rest_1_ = bf16[2,2,256,256]{3,2,1,0:T(8,128)(2,1)S(1)} reshape(bf16[1,2,2,65536]{3,2,1,0:T(2,128)(2,1)S(1)} %slice-done.1) | data formatting | bytes 1048576 | tf_op jit(solution)/shard_map/reshape;squeeze | solution.py:330
  8.2 0.0 copy-start.1
  8.2 0.5 %collective-permute-done.2 = bf16[1,2,8192]{2,1,0:T(2,128)(2,1)S(1)} collective-permute-done((bf16[1,2,8192]{2,1,0:T(2,128)(2,1)}, bf16[1,2,8192]{2,1,0:T(2,128)(2,1)S(1)}, u32[]{:S(2)}, u32[]{:S(2)}) %collective-permute-start.2) | collective-permute-done | bytes 32800 | tf_op jit(solution)/shard_map/ppermute | solution.py:260
  8.7 0.2 pad_maximum_fusion.1
  9.0 0.1 reshape.18.rest_2_
  9.1 0.0 copy-start.4
  9.1 2.3 %collective-permute-start.5 = (bf16[4,2,32,256]{3,2,1,0:T(8,128)(2,1)S(1)}, bf16[4,2,32,256]{3,2,1,0:T(8,128)(2,1)S(1)}, u32[]{:S(2)}, u32[]{:S(2)}) collective-permute-start(bf16[4,2,32,256]{3,2,1,0:T(8,128)(2,1)S(1)} %reshape.18.rest_2_), channel_id=1, source_target_pairs={{0,1},{1,0},{2,3},{3,2},{4,5},{5,4},{6,7},{7,6},{8,9},{9,8},{10,11... | collective-permute-start | bytes 393224 | tf_op jit(solution)/shard_map/ppermute | solution.py:260
  11.4 1.2 %collective-permute-start.3 = (bf16[4,2,32,256]{3,2,1,0:T(8,128)(2,1)S(1)}, bf16[4,2,32,256]{3,2,1,0:T(8,128)(2,1)S(1)}, u32[]{:S(2)}, u32[]{:S(2)}) collective-permute-start(bf16[4,2,32,256]{3,2,1,0:T(8,128)(2,1)S(1)} %reshape.18.rest_2_), channel_id=1, source_target_pairs={{0,8},{1,17},{2,10},{3,19},{4,12},{5,21},{6,14},{7,23},{8,0},{9,25... | collective-permute-start | bytes 393224 | tf_op jit(solution)/shard_map/ppermute | solution.py:260
  12.6 1.2 %collective-permute-start.4 = (bf16[4,2,32,256]{3,2,1,0:T(8,128)(2,1)S(1)}, bf16[4,2,32,256]{3,2,1,0:T(8,128)(2,1)S(1)}, u32[]{:S(2)}, u32[]{:S(2)}) collective-permute-start(bf16[4,2,32,256]{3,2,1,0:T(8,128)(2,1)S(1)} %reshape.18.rest_2_), channel_id=1, source_target_pairs={{0,16},{1,9},{2,18},{3,11},{4,20},{5,13},{6,22},{7,15},{8,24},{9,1... | collective-permute-start | bytes 393224 | tf_op jit(solution)/shard_map/ppermute | solution.py:260
  13.8 0.0 collective-permute-done.5.rest_3_
  13.9 0.0 copy-start
  13.9 1.5 %shard_map.103 = (f32[64,512]{1,0:T(8,128)S(1)}, f32[2,16,128]{2,1,0:T(8,128)S(1)}, f32[1,16,128]{2,1,0:T(8,128)S(1)}) custom-call(s32[1,2]{1,0:T(1,128)S(1)} %bitcast.2, bf16[4,16,256]{2,1,0:T(8,128)(2,1)S(1)} %fusion.1.bins_ref, bf16[512,512]{1,0:T(8,128)(2,1)S(1)} %copy-done.1, bf16[2,256,256]{2,1,0:T(8,128)(2,1)S(1)} %copy-done.3, ...), custom_call_target="tpu_custom_call" | custom-call | flops 805306368 | bytes 1048576 | tf_op jit(solution)/shard_map/pallas_call | solution.py:314
  15.4 0.1 collective-permute-done.3.rest_2_
  15.5 1.9 %collective-permute-done.4.rest_2_ = bf16[4,2,32,256]{3,2,1,0:T(8,128)(2,1)S(1)} collective-permute-done((bf16[4,2,32,256]{3,2,1,0:T(8,128)(2,1)S(1)}, bf16[4,2,32,256]{3,2,1,0:T(8,128)(2,1)S(1)}, u32[]{:S(2)}, u32[]{:S(2)}) %collective-permute-start.4) | collective-permute-done | bytes 131104 | tf_op jit(solution)/shard_map/ppermute | solution.py:260
  17.5 0.5 %collective-permute-start.7 = (bf16[8,2,32,256]{3,2,1,0:T(8,128)(2,1)S(1)}, bf16[8,2,32,256]{3,2,1,0:T(8,128)(2,1)S(1)}, u32[]{:S(2)}, u32[]{:S(2)}) collective-permute-start(bf16[8,2,32,256]{3,2,1,0:T(8,128)(2,1)S(1)} %pad_maximum_fusion), channel_id=1, source_target_pairs={{0,1},{1,0},{2,3},{3,2},{4,5},{5,4},{6,7},{7,6},{8,9},{9,8},{10,11... | collective-permute-start | bytes 786440 | tf_op jit(solution)/shard_map/ppermute | solution.py:260
  18.0 0.6 %collective-permute-start.6 = (bf16[4,2,32,256]{3,2,1,0:T(8,128)(2,1)S(1)}, bf16[4,2,32,256]{3,2,1,0:T(8,128)(2,1)S(1)}, u32[]{:S(2)}, u32[]{:S(2)}) collective-permute-start(bf16[4,2,32,256]{3,2,1,0:T(8,128)(2,1)S(1)} %collective-permute-done.3.rest_2_), channel_id=1, source_target_pairs={{0,16},{1,9},{2,18},{3,11},{4,20},{5,13},{6,22},{7,15},{8,24},{9,1... | collective-permute-start | bytes 393224 | tf_op jit(solution)/shard_map/ppermute | solution.py:260
  18.6 0.6 %collective-permute-done.7.rest_3_ = bf16[8,2,32,256]{3,2,1,0:T(8,128)(2,1)S(1)} collective-permute-done((bf16[8,2,32,256]{3,2,1,0:T(8,128)(2,1)S(1)}, bf16[8,2,32,256]{3,2,1,0:T(8,128)(2,1)S(1)}, u32[]{:S(2)}, u32[]{:S(2)}) %collective-permute-start.7) | collective-permute-done | bytes 262176 | tf_op jit(solution)/shard_map/ppermute | solution.py:260
  19.2 1.8 %shard_map.104 = (f32[2,4]{1,0:T(2,128)S(1)}, f32[4,2,256]{2,1,0:T(2,128)S(1)}, f32[4,2,256]{2,1,0:T(2,128)S(1)}) custom-call(s32[1,2]{1,0:T(1,128)S(1)} %bitcast.3, bf16[4,16,256]{2,1,0:T(8,128)(2,1)S(1)} %fusion.1.bins_ref, bf16[512,512]{1,0:T(8,128)(2,1)S(1)} %copy-done.1, bf16[2,256,256]{2,1,0:T(8,128)(2,1)S(1)} %copy-done.3, ...), custom_call_target="tpu_custom_call" | custom-call | flops 805306368 | bytes 1048576 | tf_op jit(solution)/shard_map/pallas_call | solution.py:314
  21.0 1.1 %collective-permute-done.6.rest_2_ = bf16[4,2,32,256]{3,2,1,0:T(8,128)(2,1)S(1)} collective-permute-done((bf16[4,2,32,256]{3,2,1,0:T(8,128)(2,1)S(1)}, bf16[4,2,32,256]{3,2,1,0:T(8,128)(2,1)S(1)}, u32[]{:S(2)}, u32[]{:S(2)}) %collective-permute-start.6) | collective-permute-done | bytes 131104 | tf_op jit(solution)/shard_map/ppermute | solution.py:260
  22.1 0.9 %collective-permute-start.8 = (bf16[4,2,32,256]{3,2,1,0:T(8,128)(2,1)S(1)}, bf16[4,2,32,256]{3,2,1,0:T(8,128)(2,1)S(1)}, u32[]{:S(2)}, u32[]{:S(2)}) collective-permute-start(bf16[4,2,32,256]{3,2,1,0:T(8,128)(2,1)S(1)} %collective-permute-done.6.rest_2_), channel_id=1, source_target_pairs={{0,1},{1,0},{2,3},{3,2},{4,5},{5,4},{6,7},{7,6},{8,9},{9,8},{10,11... | collective-permute-start | bytes 393224 | tf_op jit(solution)/shard_map/ppermute | solution.py:260
  23.1 1.5 %shard_map.105 = (f32[64,512]{1,0:T(8,128)S(1)}, f32[2,16,128]{2,1,0:T(8,128)S(1)}, f32[1,16,128]{2,1,0:T(8,128)S(1)}) custom-call(s32[1,2]{1,0:T(1,128)S(1)} %bitcast.4, bf16[4,16,256]{2,1,0:T(8,128)(2,1)S(1)} %fusion.1.bins_ref, bf16[512,512]{1,0:T(8,128)(2,1)S(1)} %copy-done.1, bf16[2,256,256]{2,1,0:T(8,128)(2,1)S(1)} %copy-done.3, ...), custom_call_target="tpu_custom_call" | custom-call | flops 805306368 | bytes 1048576 | tf_op jit(solution)/shard_map/pallas_call | solution.py:314
  24.6 2.4 %shard_map.106 = (f32[2,4]{1,0:T(2,128)}, f32[4,2,256]{2,1,0:T(2,128)}, f32[4,2,256]{2,1,0:T(2,128)}) custom-call(s32[1,2]{1,0:T(1,128)S(1)} %bitcast.5, bf16[4,16,256]{2,1,0:T(8,128)(2,1)S(1)} %fusion.1.bins_ref, bf16[512,512]{1,0:T(8,128)(2,1)S(1)} %copy-done.1, bf16[2,256,256]{2,1,0:T(8,128)(2,1)S(1)} %copy-done.3, f32[2,256,256]{2,1,0:T(8,128)S(1)} %copy-done.2, ...), custom_call_target="tpu_custom_call" | custom-call | flops 805306368 | bytes 1048576 | tf_op jit(solution)/shard_map/pallas_call | solution.py:314
  (15 shorter events, 0.1 us)
Async XLA Ops:
  0.6 4.6 %slice-start = ((bf16[2,2,2,65536]{3,2,1,0:T(2,128)(2,1)}), bf16[1,2,2,65536]{3,2,1,0:T(2,128)(2,1)S(1)}, s32[]{:S(2)}) async-start(bf16[2,2,2,65536]{3,2,1,0:T(2,128)(2,1)} %param.8), calls=%async_computation | async-start | bytes 1048576 | tf_op jit(solution)/shard_map/slice | solution.py:330
  0.6 5.7 %collective-permute-start.1 = (bf16[1,2,8192]{2,1,0:T(2,128)(2,1)}, bf16[1,2,8192]{2,1,0:T(2,128)(2,1)S(1)}, u32[]{:S(2)}, u32[]{:S(2)}) collective-permute-start(bf16[1,2,8192]{2,1,0:T(2,128)(2,1)} %param.9), channel_id=1, source_target_pairs={{0,6},{1,7},{2,4},{3,5},{4,2},{5,3},{6,0},{7,1},{8,14},{9,15},{10,... | collective-permute-start | bytes 98312 | tf_op jit(solution)/shard_map/ppermute | solution.py:260
  4.9 3.0 %collective-permute-start = (bf16[1,2,8192]{2,1,0:T(2,128)(2,1)}, bf16[1,2,8192]{2,1,0:T(2,128)(2,1)S(1)}, u32[]{:S(2)}, u32[]{:S(2)}) collective-permute-start(bf16[1,2,8192]{2,1,0:T(2,128)(2,1)} %param.9), channel_id=1, source_target_pairs={{0,2},{1,3},{2,0},{3,1},{4,6},{5,7},{6,4},{7,5},{8,10},{9,11},{10,... | collective-permute-start | bytes 98312 | tf_op jit(solution)/shard_map/ppermute | solution.py:260
  4.9 3.9 %collective-permute-start.2 = (bf16[1,2,8192]{2,1,0:T(2,128)(2,1)}, bf16[1,2,8192]{2,1,0:T(2,128)(2,1)S(1)}, u32[]{:S(2)}, u32[]{:S(2)}) collective-permute-start(bf16[1,2,8192]{2,1,0:T(2,128)(2,1)} %param.9), channel_id=1, source_target_pairs={{0,4},{1,5},{2,6},{3,7},{4,0},{5,1},{6,2},{7,3},{8,12},{9,13},{10,... | collective-permute-start | bytes 98312 | tf_op jit(solution)/shard_map/ppermute | solution.py:260
  5.2 1.2 %copy-start.6 = (s32[4,15]{1,0:T(4,128)S(1)}, s32[4,15]{1,0:T(4,128)}, u32[]{:S(2)}) copy-start(s32[4,15]{1,0:T(4,128)} %param.10) | copy-start | bytes 724
  6.6 1.3 %slice-start.1 = ((bf16[2,2,2,65536]{3,2,1,0:T(2,128)(2,1)}), bf16[1,2,2,65536]{3,2,1,0:T(2,128)(2,1)S(1)}, s32[]{:S(2)}) async-start(bf16[2,2,2,65536]{3,2,1,0:T(2,128)(2,1)} %param.8), calls=%async_computation.1 | async-start | bytes 1048576 | tf_op jit(solution)/shard_map/slice | solution.py:330
  7.8 0.9 %copy-start.5 = (bf16[1,2,8192]{2,1,0:T(2,128)(2,1)S(1)}, bf16[1,2,8192]{2,1,0:T(2,128)(2,1)}, u32[]{:S(2)}) copy-start(bf16[1,2,8192]{2,1,0:T(2,128)(2,1)} %param.9) | copy-start | bytes 98308
  7.8 6.0 %copy-start.2 = (f32[2,256,256]{2,1,0:T(8,128)S(1)}, f32[2,256,256]{2,1,0:T(8,128)}, u32[]{:S(2)}) copy-start(f32[2,256,256]{2,1,0:T(8,128)} %constant.15.clone.turn_ref) | copy-start | bytes 1572868
  7.8 6.0 %copy-start.3 = (bf16[2,256,256]{2,1,0:T(8,128)(2,1)S(1)}, bf16[2,256,256]{2,1,0:T(8,128)(2,1)}, u32[]{:S(2)}) copy-start(bf16[2,256,256]{2,1,0:T(8,128)(2,1)} %constant.13.clone.second_ref) | copy-start | bytes 786436
  8.2 5.6 %copy-start.1 = (bf16[512,512]{1,0:T(8,128)(2,1)S(1)}, bf16[512,512]{1,0:T(8,128)(2,1)}, u32[]{:S(2)}) copy-start(bf16[512,512]{1,0:T(8,128)(2,1)} %constant.12.clone.first_ref) | copy-start | bytes 1572868
  9.1 4.8 %copy-start.4 = (s32[2]{0:T(128)S(1)}, s32[2]{0:T(128)}, u32[]{:S(2)}) copy-start(s32[2]{0:T(128)} %param.11) | copy-start | bytes 28
  9.1 4.7 %collective-permute-start.5 = (bf16[4,2,32,256]{3,2,1,0:T(8,128)(2,1)S(1)}, bf16[4,2,32,256]{3,2,1,0:T(8,128)(2,1)S(1)}, u32[]{:S(2)}, u32[]{:S(2)}) collective-permute-start(bf16[4,2,32,256]{3,2,1,0:T(8,128)(2,1)S(1)} %reshape.18.rest_2_), channel_id=1, source_target_pairs={{0,1},{1,0},{2,3},{3,2},{4,5},{5,4},{6,7},{7,6},{8,9},{9,8},{10,11... | collective-permute-start | bytes 393224 | tf_op jit(solution)/shard_map/ppermute | solution.py:260
  11.4 4.1 %collective-permute-start.3 = (bf16[4,2,32,256]{3,2,1,0:T(8,128)(2,1)S(1)}, bf16[4,2,32,256]{3,2,1,0:T(8,128)(2,1)S(1)}, u32[]{:S(2)}, u32[]{:S(2)}) collective-permute-start(bf16[4,2,32,256]{3,2,1,0:T(8,128)(2,1)S(1)} %reshape.18.rest_2_), channel_id=1, source_target_pairs={{0,8},{1,17},{2,10},{3,19},{4,12},{5,21},{6,14},{7,23},{8,0},{9,25... | collective-permute-start | bytes 393224 | tf_op jit(solution)/shard_map/ppermute | solution.py:260
  12.6 4.8 %collective-permute-start.4 = (bf16[4,2,32,256]{3,2,1,0:T(8,128)(2,1)S(1)}, bf16[4,2,32,256]{3,2,1,0:T(8,128)(2,1)S(1)}, u32[]{:S(2)}, u32[]{:S(2)}) collective-permute-start(bf16[4,2,32,256]{3,2,1,0:T(8,128)(2,1)S(1)} %reshape.18.rest_2_), channel_id=1, source_target_pairs={{0,16},{1,9},{2,18},{3,11},{4,20},{5,13},{6,22},{7,15},{8,24},{9,1... | collective-permute-start | bytes 393224 | tf_op jit(solution)/shard_map/ppermute | solution.py:260
  13.9 5.3 %copy-start = (bf16[2,512,512]{2,1,0:T(8,128)(2,1)S(1)}, bf16[2,512,512]{2,1,0:T(8,128)(2,1)}, u32[]{:S(2)}) copy-start(bf16[2,512,512]{2,1,0:T(8,128)(2,1)} %constant.14.clone.rest_4_) | copy-start | bytes 3145732
  17.5 1.7 %collective-permute-start.7 = (bf16[8,2,32,256]{3,2,1,0:T(8,128)(2,1)S(1)}, bf16[8,2,32,256]{3,2,1,0:T(8,128)(2,1)S(1)}, u32[]{:S(2)}, u32[]{:S(2)}) collective-permute-start(bf16[8,2,32,256]{3,2,1,0:T(8,128)(2,1)S(1)} %pad_maximum_fusion), channel_id=1, source_target_pairs={{0,1},{1,0},{2,3},{3,2},{4,5},{5,4},{6,7},{7,6},{8,9},{9,8},{10,11... | collective-permute-start | bytes 786440 | tf_op jit(solution)/shard_map/ppermute | solution.py:260
  18.0 4.1 %collective-permute-start.6 = (bf16[4,2,32,256]{3,2,1,0:T(8,128)(2,1)S(1)}, bf16[4,2,32,256]{3,2,1,0:T(8,128)(2,1)S(1)}, u32[]{:S(2)}, u32[]{:S(2)}) collective-permute-start(bf16[4,2,32,256]{3,2,1,0:T(8,128)(2,1)S(1)} %collective-permute-done.3.rest_2_), channel_id=1, source_target_pairs={{0,16},{1,9},{2,18},{3,11},{4,20},{5,13},{6,22},{7,15},{8,24},{9,1... | collective-permute-start | bytes 393224 | tf_op jit(solution)/shard_map/ppermute | solution.py:260
  22.1 2.4 %collective-permute-start.8 = (bf16[4,2,32,256]{3,2,1,0:T(8,128)(2,1)S(1)}, bf16[4,2,32,256]{3,2,1,0:T(8,128)(2,1)S(1)}, u32[]{:S(2)}, u32[]{:S(2)}) collective-permute-start(bf16[4,2,32,256]{3,2,1,0:T(8,128)(2,1)S(1)} %collective-permute-done.6.rest_2_), channel_id=1, source_target_pairs={{0,1},{1,0},{2,3},{3,2},{4,5},{5,4},{6,7},{7,6},{8,9},{9,8},{10,11... | collective-permute-start | bytes 393224 | tf_op jit(solution)/shard_map/ppermute | solution.py:260
